TPU v7x, 512 devices: a whole 4x8x8 slice. The times are simulated.
512 devices in a mesh: tm: 16 (over x, z_hi), space: 32 (over z_lo, y, core).
Axes of the slice: x: 4, y: 8, z: 8 (z_hi: 4, z_lo: 2; z = z_hi * 2 + z_lo), core: 2. Of those that a mesh axis runs over, the one named last changes fastest.
Arguments:
- guesses: float32 [16, 256, 32, 128], P('tm', 'space'), may hold values from -6 to 6
- forcing: float32 [16, 256, 32, 128], P('tm', 'space'), may hold values from -6 to 6
- initial: float32 [256, 32, 128], P('space'), may hold values from -12 to 12
- kappa: float32 [256, 32, 128], P('space'), may hold values from 0.02 to 0.1
- velocity: float32 [3, 256, 32, 128], P(None, 'space'), may hold values from -0.2 to 0.2
Outputs:
- fine_states: float32 [64, 256, 32, 128], P('tm', 'space')
All inputs are finite; a program needn't handle non-finite values.
Results may differ from a plain program's by a relative error of at most 0.00002.
Values sent between devices are 32-bit elements; how exact they have to be, the bound alone decides.
No kernel may reach another device: no remote copies, remote signals or barrier semaphores. Data moves between devices by JAX's collectives and lax.ppermute only.
A program may use at most 64 MiB of HBM per device.

v0:
```python
import jax
import jax.numpy as jnp
from jax import lax
from jax.sharding import PartitionSpec as P

M = 4


step_size = 0.3


def padded_2(x, sides, width):
    for axis, dim in sides:
        count, length = (lax.axis_size(axis), x.shape[dim])
        up = [(i, (i + 1) % count) for i in range(count - 1)]
        down = [(j, i) for i, j in up]
        last = lax.slice_in_dim(x, length - width, length, axis=dim)
        initial = lax.slice_in_dim(x, 0, width, axis=dim)
        before = lax.ppermute(last, axis, up)
        after = lax.ppermute(initial, axis, down)
        x = jnp.concatenate([before, x, after], axis=dim)
    return x


def from_behind(value, axis, steps):
    count = lax.axis_size(axis)
    initial, last = (max(0, -steps), min(count, count - steps))
    return lax.ppermute(value, axis, [(source, source + steps) for source in range(initial, last)])


def advance(padded, diffuse, drift, source, delta):
    center = padded[..., 1:-1, :, :]
    margins = [(0, 0)] * (center.ndim - 2) + [(1, 1), (1, 1)]
    padded_xy = jnp.pad(center, margins)
    above_z = padded[..., 2:, :, :]
    below_z = padded[..., :-2, :, :]
    above_y = padded_xy[..., 2:, 1:-1]
    below_y = padded_xy[..., :-2, 1:-1]
    above_x = padded_xy[..., 1:-1, 2:]
    below_x = padded_xy[..., 1:-1, :-2]
    laplace = above_z + below_z + above_y + below_y + above_x + below_x - 6.0 * center
    transport = jnp.zeros_like(center)
    for speed, above, below in (
        (drift[0], above_z, below_z),
        (drift[1], above_y, below_y),
        (drift[2], above_x, below_x),
    ):
        transport = (
            transport
            + jnp.maximum(speed, 0.0) * (center - below)
            + jnp.minimum(speed, 0.0) * (above - center)
        )
    return center + delta * (diffuse * laplace - transport + source)


def coarse_step(correction, kappa, velocity):
    padded = padded_2(correction, (("space", 0),), 1)
    return advance(padded, kappa, velocity, 0.0, 2.0 * step_size)


def coarse_pair(correction, kappa, velocity):
    return coarse_step(coarse_step(correction, kappa, velocity), kappa, velocity)


def body(guesses, forcing, initial, kappa, velocity):
    intervals = guesses.shape[0]
    layers = guesses.shape[1]
    slab_index = lax.axis_index("tm")

    def relax(states, steps_wanted):
        stored = []
        for section in range(steps_wanted):
            padded = padded_2(states, (("space", 1),), 1)
            states = advance(padded, kappa, velocity, forcing, step_size)
            stored.append(states)
        return stored

    def chain_group(correction, jumps):
        correction = coarse_pair(correction, kappa, velocity) + jumps[0]
        produced = [correction]
        return jnp.stack(produced)

    shifted = from_behind(guesses[intervals - 1], "tm", 1)
    opening = jnp.where(slab_index == 0, initial, shifted)
    starts = jnp.concatenate([opening[None], guesses[:-1]], axis=0)
    relaxed = relax(starts, M)[M - 1]
    residual = relaxed - guesses

    def relay_turn(turn, errors):
        correction = from_behind(errors[intervals - 1], "tm", 1)
        return chain_group(correction, residual)

    errors = lax.fori_loop(0, lax.axis_size("tm"), relay_turn, jnp.zeros_like(guesses))
    corrected = guesses + errors
    shifted_back = from_behind(corrected[intervals - 1], "tm", 1)
    opening = jnp.where(slab_index == 0, initial, shifted_back)
    starts = jnp.concatenate([opening[None], corrected[:-1]], axis=0)
    stored = relax(starts, M - 1)
    stored.append(corrected)
    return jnp.stack(stored, axis=1).reshape(
        intervals * M, layers, guesses.shape[2], guesses.shape[3]
    )


def solution(mesh):
    placed = (
        P("tm", "space", None, None),
        P("tm", "space", None, None),
        P("space", None, None),
        P("space", None, None),
        P(None, "space", None, None),
    )
    return jax.shard_map(
        body, mesh=mesh, in_specs=placed, out_specs=P("tm", "space", None, None), check_vma=False
    )
```

profile of v0, /device:TPU:66, one launch (start us, length us, event | category | flops | bytes accessed | tf_op | source)
XLA Modules:
  0.0 554.7 jit_solution(19979639438320625)
XLA Ops:
  0.0 6.2 %collective-permute-start.5 = (f32[8,32,128]{2,1,0:T(8,128)}, f32[8,32,128]{2,1,0:T(8,128)S(1)}, u32[]{:S(2)}, u32[]{:S(2)}) collective-permute-start(f32[8,32,128]{2,1,0:T(8,128)} %bitcast.98), channel_id=1, source_target_pairs={{0,32},{32,64},{64,96},{96,128},{128,160},{160,192},{192,224},{224... | collective-permute-start | bytes 393224 | tf_op jit(solution)/shard_map/ppermute | solution.py:28
  6.2 10.4 %collective-permute-done.5 = f32[8,32,128]{2,1,0:T(8,128)S(1)} collective-permute-done((f32[8,32,128]{2,1,0:T(8,128)}, f32[8,32,128]{2,1,0:T(8,128)S(1)}, u32[]{:S(2)}, u32[]{:S(2)}) %collective-permute-start.5) | collective-permute-done | bytes 131104 | tf_op jit(solution)/shard_map/ppermute | solution.py:28
  54.9 458.2 %while.12 = (s32[]{:T(128)}, f32[1,8,32,128]{3,2,1,0:T(8,128)S(1)}, f32[8,32,128]{2,1,0:T(8,128)S(1)}, f32[3,8,32,128]{3,2,1,0:T(8,128)S(1)}, f32[1,8,32,128]{3,2,1,0:T(8,128)S(1)}, /*index=5*/s32[]{:T(128)}) while((s32[]{:T(128)}, f32[1,8,32,128]{3,2,1,0:T(8,128)S(1)}, f32[8,32,128]{2,1,0:T(8,128)S(1)}, f32[3,8,32,128]{3,2,1,0:T(8,128)S(1)}, ...), condition=%wide.region_1.2_spmd, body=%wide.region_0.1_spmd.sunk | while | flops 2392066 | bytes 2687245 | solution.py:93
  66.7 5.8 %collective-permute-start.2 = (f32[1,32,128]{2,1,0:T(8,128)S(1)}, f32[1,32,128]{2,1,0:T(8,128)S(1)}, u32[]{:S(2)}, u32[]{:S(2)}) collective-permute-start(f32[1,32,128]{2,1,0:T(8,128)S(1)} %get-tuple-element.137), channel_id=1, source_target_pairs={{1,0},{2,1},{3,2},{4,3},{5,4},{6,5},{7,6},{8,7},{9,8},{10,9},{11,1... | collective-permute-start | bytes 49160 | tf_op jit(solution)/shard_map/while/body/eval_jaxpr/ppermute | solution.py:20
  76.0 5.8 %collective-permute-start.4 = (f32[1,32,128]{2,1,0:T(8,128)S(1)}, f32[1,32,128]{2,1,0:T(8,128)S(1)}, u32[]{:S(2)}, u32[]{:S(2)}) collective-permute-start(f32[1,32,128]{2,1,0:T(8,128)S(1)} %get-tuple-element.139), channel_id=1, source_target_pairs={{1,0},{2,1},{3,2},{4,3},{5,4},{6,5},{7,6},{8,7},{9,8},{10,9},{11,1... | collective-permute-start | bytes 49160 | tf_op jit(solution)/shard_map/while/body/eval_jaxpr/ppermute | solution.py:20
  87.2 6.1 %collective-permute-done = f32[8,32,128]{2,1,0:T(8,128)S(1)} collective-permute-done((f32[8,32,128]{2,1,0:T(8,128)S(1)}, f32[8,32,128]{2,1,0:T(8,128)S(1)}, u32[]{:S(2)}, u32[]{:S(2)}) %collective-permute-start) | collective-permute-done | bytes 131104 | tf_op jit(solution)/shard_map/while/body/eval_jaxpr/ppermute | solution.py:28
  95.2 5.8 %collective-permute-start.2 = (f32[1,32,128]{2,1,0:T(8,128)S(1)}, f32[1,32,128]{2,1,0:T(8,128)S(1)}, u32[]{:S(2)}, u32[]{:S(2)}) collective-permute-start(f32[1,32,128]{2,1,0:T(8,128)S(1)} %get-tuple-element.137), channel_id=1, source_target_pairs={{1,0},{2,1},{3,2},{4,3},{5,4},{6,5},{7,6},{8,7},{9,8},{10,9},{11,1... | collective-permute-start | bytes 49160 | tf_op jit(solution)/shard_map/while/body/eval_jaxpr/ppermute | solution.py:20
  104.5 5.8 %collective-permute-start.4 = (f32[1,32,128]{2,1,0:T(8,128)S(1)}, f32[1,32,128]{2,1,0:T(8,128)S(1)}, u32[]{:S(2)}, u32[]{:S(2)}) collective-permute-start(f32[1,32,128]{2,1,0:T(8,128)S(1)} %get-tuple-element.139), channel_id=1, source_target_pairs={{1,0},{2,1},{3,2},{4,3},{5,4},{6,5},{7,6},{8,7},{9,8},{10,9},{11,1... | collective-permute-start | bytes 49160 | tf_op jit(solution)/shard_map/while/body/eval_jaxpr/ppermute | solution.py:20
  114.8 7.0 %collective-permute-done = f32[8,32,128]{2,1,0:T(8,128)S(1)} collective-permute-done((f32[8,32,128]{2,1,0:T(8,128)S(1)}, f32[8,32,128]{2,1,0:T(8,128)S(1)}, u32[]{:S(2)}, u32[]{:S(2)}) %collective-permute-start) | collective-permute-done | bytes 131104 | tf_op jit(solution)/shard_map/while/body/eval_jaxpr/ppermute | solution.py:28
  142.4 7.9 %collective-permute-done = f32[8,32,128]{2,1,0:T(8,128)S(1)} collective-permute-done((f32[8,32,128]{2,1,0:T(8,128)S(1)}, f32[8,32,128]{2,1,0:T(8,128)S(1)}, u32[]{:S(2)}, u32[]{:S(2)}) %collective-permute-start) | collective-permute-done | bytes 131104 | tf_op jit(solution)/shard_map/while/body/eval_jaxpr/ppermute | solution.py:28
  152.2 7.5 %collective-permute-start.2 = (f32[1,32,128]{2,1,0:T(8,128)S(1)}, f32[1,32,128]{2,1,0:T(8,128)S(1)}, u32[]{:S(2)}, u32[]{:S(2)}) collective-permute-start(f32[1,32,128]{2,1,0:T(8,128)S(1)} %get-tuple-element.137), channel_id=1, source_target_pairs={{1,0},{2,1},{3,2},{4,3},{5,4},{6,5},{7,6},{8,7},{9,8},{10,9},{11,1... | collective-permute-start | bytes 49160 | tf_op jit(solution)/shard_map/while/body/eval_jaxpr/ppermute | solution.py:20
  172.5 8.1 %collective-permute-done = f32[8,32,128]{2,1,0:T(8,128)S(1)} collective-permute-done((f32[8,32,128]{2,1,0:T(8,128)S(1)}, f32[8,32,128]{2,1,0:T(8,128)S(1)}, u32[]{:S(2)}, u32[]{:S(2)}) %collective-permute-start) | collective-permute-done | bytes 131104 | tf_op jit(solution)/shard_map/while/body/eval_jaxpr/ppermute | solution.py:28
  201.2 7.9 %collective-permute-done = f32[8,32,128]{2,1,0:T(8,128)S(1)} collective-permute-done((f32[8,32,128]{2,1,0:T(8,128)S(1)}, f32[8,32,128]{2,1,0:T(8,128)S(1)}, u32[]{:S(2)}, u32[]{:S(2)}) %collective-permute-start) | collective-permute-done | bytes 131104 | tf_op jit(solution)/shard_map/while/body/eval_jaxpr/ppermute | solution.py:28
  229.7 7.9 %collective-permute-done = f32[8,32,128]{2,1,0:T(8,128)S(1)} collective-permute-done((f32[8,32,128]{2,1,0:T(8,128)S(1)}, f32[8,32,128]{2,1,0:T(8,128)S(1)}, u32[]{:S(2)}, u32[]{:S(2)}) %collective-permute-start) | collective-permute-done | bytes 131104 | tf_op jit(solution)/shard_map/while/body/eval_jaxpr/ppermute | solution.py:28
  258.2 7.9 %collective-permute-done = f32[8,32,128]{2,1,0:T(8,128)S(1)} collective-permute-done((f32[8,32,128]{2,1,0:T(8,128)S(1)}, f32[8,32,128]{2,1,0:T(8,128)S(1)}, u32[]{:S(2)}, u32[]{:S(2)}) %collective-permute-start) | collective-permute-done | bytes 131104 | tf_op jit(solution)/shard_map/while/body/eval_jaxpr/ppermute | solution.py:28
  286.7 7.9 %collective-permute-done = f32[8,32,128]{2,1,0:T(8,128)S(1)} collective-permute-done((f32[8,32,128]{2,1,0:T(8,128)S(1)}, f32[8,32,128]{2,1,0:T(8,128)S(1)}, u32[]{:S(2)}, u32[]{:S(2)}) %collective-permute-start) | collective-permute-done | bytes 131104 | tf_op jit(solution)/shard_map/while/body/eval_jaxpr/ppermute | solution.py:28
  315.2 8.0 %collective-permute-done = f32[8,32,128]{2,1,0:T(8,128)S(1)} collective-permute-done((f32[8,32,128]{2,1,0:T(8,128)S(1)}, f32[8,32,128]{2,1,0:T(8,128)S(1)}, u32[]{:S(2)}, u32[]{:S(2)}) %collective-permute-start) | collective-permute-done | bytes 131104 | tf_op jit(solution)/shard_map/while/body/eval_jaxpr/ppermute | solution.py:28
  343.7 8.0 %collective-permute-done = f32[8,32,128]{2,1,0:T(8,128)S(1)} collective-permute-done((f32[8,32,128]{2,1,0:T(8,128)S(1)}, f32[8,32,128]{2,1,0:T(8,128)S(1)}, u32[]{:S(2)}, u32[]{:S(2)}) %collective-permute-start) | collective-permute-done | bytes 131104 | tf_op jit(solution)/shard_map/while/body/eval_jaxpr/ppermute | solution.py:28
  372.3 8.0 %collective-permute-done = f32[8,32,128]{2,1,0:T(8,128)S(1)} collective-permute-done((f32[8,32,128]{2,1,0:T(8,128)S(1)}, f32[8,32,128]{2,1,0:T(8,128)S(1)}, u32[]{:S(2)}, u32[]{:S(2)}) %collective-permute-start) | collective-permute-done | bytes 131104 | tf_op jit(solution)/shard_map/while/body/eval_jaxpr/ppermute | solution.py:28
  400.8 8.0 %collective-permute-done = f32[8,32,128]{2,1,0:T(8,128)S(1)} collective-permute-done((f32[8,32,128]{2,1,0:T(8,128)S(1)}, f32[8,32,128]{2,1,0:T(8,128)S(1)}, u32[]{:S(2)}, u32[]{:S(2)}) %collective-permute-start) | collective-permute-done | bytes 131104 | tf_op jit(solution)/shard_map/while/body/eval_jaxpr/ppermute | solution.py:28
  429.3 8.0 %collective-permute-done = f32[8,32,128]{2,1,0:T(8,128)S(1)} collective-permute-done((f32[8,32,128]{2,1,0:T(8,128)S(1)}, f32[8,32,128]{2,1,0:T(8,128)S(1)}, u32[]{:S(2)}, u32[]{:S(2)}) %collective-permute-start) | collective-permute-done | bytes 131104 | tf_op jit(solution)/shard_map/while/body/eval_jaxpr/ppermute | solution.py:28
  457.9 8.0 %collective-permute-done = f32[8,32,128]{2,1,0:T(8,128)S(1)} collective-permute-done((f32[8,32,128]{2,1,0:T(8,128)S(1)}, f32[8,32,128]{2,1,0:T(8,128)S(1)}, u32[]{:S(2)}, u32[]{:S(2)}) %collective-permute-start) | collective-permute-done | bytes 131104 | tf_op jit(solution)/shard_map/while/body/eval_jaxpr/ppermute | solution.py:28
  486.5 8.0 %collective-permute-done = f32[8,32,128]{2,1,0:T(8,128)S(1)} collective-permute-done((f32[8,32,128]{2,1,0:T(8,128)S(1)}, f32[8,32,128]{2,1,0:T(8,128)S(1)}, u32[]{:S(2)}, u32[]{:S(2)}) %collective-permute-start) | collective-permute-done | bytes 131104 | tf_op jit(solution)/shard_map/while/body/eval_jaxpr/ppermute | solution.py:28
  515.3 7.9 %collective-permute-done.14 = f32[8,32,128]{2,1,0:T(8,128)S(1)} collective-permute-done((f32[8,32,128]{2,1,0:T(8,128)S(1)}, f32[8,32,128]{2,1,0:T(8,128)S(1)}, u32[]{:S(2)}, u32[]{:S(2)}) %collective-permute-start.14) | collective-permute-done | bytes 131104 | tf_op jit(solution)/shard_map/ppermute | solution.py:28
  (262 shorter events, 381.1 us)
Async XLA Ops:
  0.0 16.6 %collective-permute-start.5 = (f32[8,32,128]{2,1,0:T(8,128)}, f32[8,32,128]{2,1,0:T(8,128)S(1)}, u32[]{:S(2)}, u32[]{:S(2)}) collective-permute-start(f32[8,32,128]{2,1,0:T(8,128)} %bitcast.98), channel_id=1, source_target_pairs={{0,32},{32,64},{64,96},{96,128},{128,160},{160,192},{192,224},{224... | collective-permute-start | bytes 393224 | tf_op jit(solution)/shard_map/ppermute | solution.py:28
  54.9 9.9 %collective-permute-start = (f32[8,32,128]{2,1,0:T(8,128)S(1)}, f32[8,32,128]{2,1,0:T(8,128)S(1)}, u32[]{:S(2)}, u32[]{:S(2)}) collective-permute-start(f32[8,32,128]{2,1,0:T(8,128)S(1)} %bitcast.99), channel_id=1, source_target_pairs={{0,32},{32,64},{64,96},{96,128},{128,160},{160,192},{192,224},{224... | collective-permute-start | bytes 393224 | tf_op jit(solution)/shard_map/while/body/eval_jaxpr/ppermute | solution.py:28
  83.4 9.9 %collective-permute-start = (f32[8,32,128]{2,1,0:T(8,128)S(1)}, f32[8,32,128]{2,1,0:T(8,128)S(1)}, u32[]{:S(2)}, u32[]{:S(2)}) collective-permute-start(f32[8,32,128]{2,1,0:T(8,128)S(1)} %bitcast.99), channel_id=1, source_target_pairs={{0,32},{32,64},{64,96},{96,128},{128,160},{160,192},{192,224},{224... | collective-permute-start | bytes 393224 | tf_op jit(solution)/shard_map/while/body/eval_jaxpr/ppermute | solution.py:28
  111.9 9.9 %collective-permute-start = (f32[8,32,128]{2,1,0:T(8,128)S(1)}, f32[8,32,128]{2,1,0:T(8,128)S(1)}, u32[]{:S(2)}, u32[]{:S(2)}) collective-permute-start(f32[8,32,128]{2,1,0:T(8,128)S(1)} %bitcast.99), channel_id=1, source_target_pairs={{0,32},{32,64},{64,96},{96,128},{128,160},{160,192},{192,224},{224... | collective-permute-start | bytes 393224 | tf_op jit(solution)/shard_map/while/body/eval_jaxpr/ppermute | solution.py:28
  140.4 9.9 %collective-permute-start = (f32[8,32,128]{2,1,0:T(8,128)S(1)}, f32[8,32,128]{2,1,0:T(8,128)S(1)}, u32[]{:S(2)}, u32[]{:S(2)}) collective-permute-start(f32[8,32,128]{2,1,0:T(8,128)S(1)} %bitcast.99), channel_id=1, source_target_pairs={{0,32},{32,64},{64,96},{96,128},{128,160},{160,192},{192,224},{224... | collective-permute-start | bytes 393224 | tf_op jit(solution)/shard_map/while/body/eval_jaxpr/ppermute | solution.py:28
  150.3 9.4 %collective-permute-start.1 = (f32[1,32,128]{2,1,0:T(8,128)S(1)}, f32[1,32,128]{2,1,0:T(8,128)S(1)}, u32[]{:S(2)}, u32[]{:S(2)}) collective-permute-start(f32[1,32,128]{2,1,0:T(8,128)S(1)} %get-tuple-element.136), channel_id=1, source_target_pairs={{0,1},{1,2},{2,3},{3,4},{4,5},{5,6},{6,7},{7,8},{8,9},{9,10},{10,1... | collective-permute-start | bytes 49160 | tf_op jit(solution)/shard_map/while/body/eval_jaxpr/ppermute | solution.py:19
  152.2 8.9 %collective-permute-start.2 = (f32[1,32,128]{2,1,0:T(8,128)S(1)}, f32[1,32,128]{2,1,0:T(8,128)S(1)}, u32[]{:S(2)}, u32[]{:S(2)}) collective-permute-start(f32[1,32,128]{2,1,0:T(8,128)S(1)} %get-tuple-element.137), channel_id=1, source_target_pairs={{1,0},{2,1},{3,2},{4,3},{5,4},{6,5},{7,6},{8,7},{9,8},{10,9},{11,1... | collective-permute-start | bytes 49160 | tf_op jit(solution)/shard_map/while/body/eval_jaxpr/ppermute | solution.py:20
  170.6 10.0 %collective-permute-start = (f32[8,32,128]{2,1,0:T(8,128)S(1)}, f32[8,32,128]{2,1,0:T(8,128)S(1)}, u32[]{:S(2)}, u32[]{:S(2)}) collective-permute-start(f32[8,32,128]{2,1,0:T(8,128)S(1)} %bitcast.99), channel_id=1, source_target_pairs={{0,32},{32,64},{64,96},{96,128},{128,160},{160,192},{192,224},{224... | collective-permute-start | bytes 393224 | tf_op jit(solution)/shard_map/while/body/eval_jaxpr/ppermute | solution.py:28
  190.0 7.7 %collective-permute-start.3 = (f32[1,32,128]{2,1,0:T(8,128)S(1)}, f32[1,32,128]{2,1,0:T(8,128)S(1)}, u32[]{:S(2)}, u32[]{:S(2)}) collective-permute-start(f32[1,32,128]{2,1,0:T(8,128)S(1)} %get-tuple-element.138), channel_id=1, source_target_pairs={{0,1},{1,2},{2,3},{3,4},{4,5},{5,6},{6,7},{7,8},{8,9},{9,10},{10,1... | collective-permute-start | bytes 49160 | tf_op jit(solution)/shard_map/while/body/eval_jaxpr/ppermute | solution.py:19
  199.3 9.9 %collective-permute-start = (f32[8,32,128]{2,1,0:T(8,128)S(1)}, f32[8,32,128]{2,1,0:T(8,128)S(1)}, u32[]{:S(2)}, u32[]{:S(2)}) collective-permute-start(f32[8,32,128]{2,1,0:T(8,128)S(1)} %bitcast.99), channel_id=1, source_target_pairs={{0,32},{32,64},{64,96},{96,128},{128,160},{160,192},{192,224},{224... | collective-permute-start | bytes 393224 | tf_op jit(solution)/shard_map/while/body/eval_jaxpr/ppermute | solution.py:28
  218.4 7.7 %collective-permute-start.3 = (f32[1,32,128]{2,1,0:T(8,128)S(1)}, f32[1,32,128]{2,1,0:T(8,128)S(1)}, u32[]{:S(2)}, u32[]{:S(2)}) collective-permute-start(f32[1,32,128]{2,1,0:T(8,128)S(1)} %get-tuple-element.138), channel_id=1, source_target_pairs={{0,1},{1,2},{2,3},{3,4},{4,5},{5,6},{6,7},{7,8},{8,9},{9,10},{10,1... | collective-permute-start | bytes 49160 | tf_op jit(solution)/shard_map/while/body/eval_jaxpr/ppermute | solution.py:19
  227.8 9.9 %collective-permute-start = (f32[8,32,128]{2,1,0:T(8,128)S(1)}, f32[8,32,128]{2,1,0:T(8,128)S(1)}, u32[]{:S(2)}, u32[]{:S(2)}) collective-permute-start(f32[8,32,128]{2,1,0:T(8,128)S(1)} %bitcast.99), channel_id=1, source_target_pairs={{0,32},{32,64},{64,96},{96,128},{128,160},{160,192},{192,224},{224... | collective-permute-start | bytes 393224 | tf_op jit(solution)/shard_map/while/body/eval_jaxpr/ppermute | solution.py:28
  246.9 7.7 %collective-permute-start.3 = (f32[1,32,128]{2,1,0:T(8,128)S(1)}, f32[1,32,128]{2,1,0:T(8,128)S(1)}, u32[]{:S(2)}, u32[]{:S(2)}) collective-permute-start(f32[1,32,128]{2,1,0:T(8,128)S(1)} %get-tuple-element.138), channel_id=1, source_target_pairs={{0,1},{1,2},{2,3},{3,4},{4,5},{5,6},{6,7},{7,8},{8,9},{9,10},{10,1... | collective-permute-start | bytes 49160 | tf_op jit(solution)/shard_map/while/body/eval_jaxpr/ppermute | solution.py:19
  256.2 9.9 %collective-permute-start = (f32[8,32,128]{2,1,0:T(8,128)S(1)}, f32[8,32,128]{2,1,0:T(8,128)S(1)}, u32[]{:S(2)}, u32[]{:S(2)}) collective-permute-start(f32[8,32,128]{2,1,0:T(8,128)S(1)} %bitcast.99), channel_id=1, source_target_pairs={{0,32},{32,64},{64,96},{96,128},{128,160},{160,192},{192,224},{224... | collective-permute-start | bytes 393224 | tf_op jit(solution)/shard_map/while/body/eval_jaxpr/ppermute | solution.py:28
  275.4 7.7 %collective-permute-start.3 = (f32[1,32,128]{2,1,0:T(8,128)S(1)}, f32[1,32,128]{2,1,0:T(8,128)S(1)}, u32[]{:S(2)}, u32[]{:S(2)}) collective-permute-start(f32[1,32,128]{2,1,0:T(8,128)S(1)} %get-tuple-element.138), channel_id=1, source_target_pairs={{0,1},{1,2},{2,3},{3,4},{4,5},{5,6},{6,7},{7,8},{8,9},{9,10},{10,1... | collective-permute-start | bytes 49160 | tf_op jit(solution)/shard_map/while/body/eval_jaxpr/ppermute | solution.py:19
  284.7 9.9 %collective-permute-start = (f32[8,32,128]{2,1,0:T(8,128)S(1)}, f32[8,32,128]{2,1,0:T(8,128)S(1)}, u32[]{:S(2)}, u32[]{:S(2)}) collective-permute-start(f32[8,32,128]{2,1,0:T(8,128)S(1)} %bitcast.99), channel_id=1, source_target_pairs={{0,32},{32,64},{64,96},{96,128},{128,160},{160,192},{192,224},{224... | collective-permute-start | bytes 393224 | tf_op jit(solution)/shard_map/while/body/eval_jaxpr/ppermute | solution.py:28
  313.2 9.9 %collective-permute-start = (f32[8,32,128]{2,1,0:T(8,128)S(1)}, f32[8,32,128]{2,1,0:T(8,128)S(1)}, u32[]{:S(2)}, u32[]{:S(2)}) collective-permute-start(f32[8,32,128]{2,1,0:T(8,128)S(1)} %bitcast.99), channel_id=1, source_target_pairs={{0,32},{32,64},{64,96},{96,128},{128,160},{160,192},{192,224},{224... | collective-permute-start | bytes 393224 | tf_op jit(solution)/shard_map/while/body/eval_jaxpr/ppermute | solution.py:28
  341.8 10.0 %collective-permute-start = (f32[8,32,128]{2,1,0:T(8,128)S(1)}, f32[8,32,128]{2,1,0:T(8,128)S(1)}, u32[]{:S(2)}, u32[]{:S(2)}) collective-permute-start(f32[8,32,128]{2,1,0:T(8,128)S(1)} %bitcast.99), channel_id=1, source_target_pairs={{0,32},{32,64},{64,96},{96,128},{128,160},{160,192},{192,224},{224... | collective-permute-start | bytes 393224 | tf_op jit(solution)/shard_map/while/body/eval_jaxpr/ppermute | solution.py:28
  370.4 9.9 %collective-permute-start = (f32[8,32,128]{2,1,0:T(8,128)S(1)}, f32[8,32,128]{2,1,0:T(8,128)S(1)}, u32[]{:S(2)}, u32[]{:S(2)}) collective-permute-start(f32[8,32,128]{2,1,0:T(8,128)S(1)} %bitcast.99), channel_id=1, source_target_pairs={{0,32},{32,64},{64,96},{96,128},{128,160},{160,192},{192,224},{224... | collective-permute-start | bytes 393224 | tf_op jit(solution)/shard_map/while/body/eval_jaxpr/ppermute | solution.py:28
  398.9 9.9 %collective-permute-start = (f32[8,32,128]{2,1,0:T(8,128)S(1)}, f32[8,32,128]{2,1,0:T(8,128)S(1)}, u32[]{:S(2)}, u32[]{:S(2)}) collective-permute-start(f32[8,32,128]{2,1,0:T(8,128)S(1)} %bitcast.99), channel_id=1, source_target_pairs={{0,32},{32,64},{64,96},{96,128},{128,160},{160,192},{192,224},{224... | collective-permute-start | bytes 393224 | tf_op jit(solution)/shard_map/while/body/eval_jaxpr/ppermute | solution.py:28
  427.4 10.0 %collective-permute-start = (f32[8,32,128]{2,1,0:T(8,128)S(1)}, f32[8,32,128]{2,1,0:T(8,128)S(1)}, u32[]{:S(2)}, u32[]{:S(2)}) collective-permute-start(f32[8,32,128]{2,1,0:T(8,128)S(1)} %bitcast.99), channel_id=1, source_target_pairs={{0,32},{32,64},{64,96},{96,128},{128,160},{160,192},{192,224},{224... | collective-permute-start | bytes 393224 | tf_op jit(solution)/shard_map/while/body/eval_jaxpr/ppermute | solution.py:28
  456.0 10.0 %collective-permute-start = (f32[8,32,128]{2,1,0:T(8,128)S(1)}, f32[8,32,128]{2,1,0:T(8,128)S(1)}, u32[]{:S(2)}, u32[]{:S(2)}) collective-permute-start(f32[8,32,128]{2,1,0:T(8,128)S(1)} %bitcast.99), channel_id=1, source_target_pairs={{0,32},{32,64},{64,96},{96,128},{128,160},{160,192},{192,224},{224... | collective-permute-start | bytes 393224 | tf_op jit(solution)/shard_map/while/body/eval_jaxpr/ppermute | solution.py:28
  484.6 10.0 %collective-permute-start = (f32[8,32,128]{2,1,0:T(8,128)S(1)}, f32[8,32,128]{2,1,0:T(8,128)S(1)}, u32[]{:S(2)}, u32[]{:S(2)}) collective-permute-start(f32[8,32,128]{2,1,0:T(8,128)S(1)} %bitcast.99), channel_id=1, source_target_pairs={{0,32},{32,64},{64,96},{96,128},{128,160},{160,192},{192,224},{224... | collective-permute-start | bytes 393224 | tf_op jit(solution)/shard_map/while/body/eval_jaxpr/ppermute | solution.py:28
  513.2 10.0 %collective-permute-start.14 = (f32[8,32,128]{2,1,0:T(8,128)S(1)}, f32[8,32,128]{2,1,0:T(8,128)S(1)}, u32[]{:S(2)}, u32[]{:S(2)}) collective-permute-start(f32[8,32,128]{2,1,0:T(8,128)S(1)} %get-tuple-element.85), channel_id=1, source_target_pairs={{0,32},{32,64},{64,96},{96,128},{128,160},{160,192},{192,224},{224... | collective-permute-start | bytes 393224 | tf_op jit(solution)/shard_map/ppermute | solution.py:28
  (77 other events, 578.6 us)
where the time goes:
time: 557 us; the launch traced here: 555 us
  starting transfers between devices  324 us (58%)
  waiting for transfers between devices  219 us (39%)
  other arithmetic  9.32 us (2%)
    ppermute x39, starting transfers between devices, padded_2(): after = lax.ppermute(initial, axis, down)  202 us
    ppermute x18, waiting for transfers between devices, from_behind(): lax.ppermute(value, axis, [(source, source + steps) for source in range(i...  140 us
    ppermute x39, starting transfers between devices, padded_2(): before = lax.ppermute(last, axis, up)  77.6 us
    ppermute x39, waiting for transfers between devices, padded_2(): after = lax.ppermute(initial, axis, down)  45.2 us
    ppermute x18, starting transfers between devices, from_behind(): lax.ppermute(value, axis, [(source, source + steps) for source in range(i...  44.7 us
    ppermute x39, waiting for transfers between devices, padded_2(): before = lax.ppermute(last, axis, up)  33.8 us
  transfers between devices with their start and end apart: 96, of which 57 were waited for; matrix products, arithmetic and copies ran while one was open for 0% of the time, Pallas kernels for 0%

commit v1 on v0

v1 whole, which is shorter than its diff:
```python
import functools

import jax
import jax.numpy as jnp
from jax import lax
from jax.experimental import pallas as pl
from jax.experimental.pallas import tpu as pltpu
from jax.sharding import PartitionSpec as P


L = 8
NY, NX = 32, 128
STEP = 0.3
FINE_HALO = 5
COARSE_HALO = 7
SENT = (4, 6, 5, FINE_HALO)
FIRST = SENT[0] + SENT[1] + SENT[2] + 4 * FINE_HALO
MORE = 4 * (COARSE_HALO - FINE_HALO)
VMEM = pltpu.VMEM


def call(kernel, outs, scratch=()):
    return pl.pallas_call(
        kernel,
        out_shape=[jax.ShapeDtypeStruct((n, NY, NX) if isinstance(n, int) else n + (NY, NX), jnp.float32) for n in outs],
        scratch_shapes=[VMEM((n, NY, NX), jnp.float32) for n in scratch],
        compiler_params=pltpu.CompilerParams(vmem_limit_bytes=40 << 20),
    )


def stencil(u, at, cur, prev, nxt, coef, k):
    return (
        coef[0, k] * nxt
        + coef[1, k] * prev
        + coef[2, k] * pltpu.roll(cur, NY - 1, 0)
        + coef[3, k] * pltpu.roll(cur, 1, 0)
        + coef[4, k] * pltpu.roll(cur, NX - 1, 1)
        + coef[5, k] * pltpu.roll(cur, 1, 1)
        + coef[6, k] * cur
    )


def sweep(u, base, coef, coef_base, lo, hi, after=None):
    prev, cur = u[lo - 1 + base], u[lo + base]
    for z in range(lo, hi):
        nxt = u[z + 1 + base]
        new = stencil(u, z, cur, prev, nxt, coef, z + coef_base)
        u[z + base] = new if after is None else after(z, cur, new)
        prev, cur = cur, nxt


def coarse_twice(u, base, coef, halo):
    sweep(u, base, coef, COARSE_HALO, 1 - halo, L + halo - 1)
    sweep(u, base, coef, COARSE_HALO, 2 - halo, L + halo - 2)


def ext(own, outer, inner, z, outer_at=0, inner_at=0, own_at=0):
    if z < 0:
        return outer[outer_at - 1 - z]
    if z >= L:
        return inner[inner_at + z - L]
    return own[own_at + z]


def write_coefs(out, index, diffuse, vz, vy, vx, h):
    row = lax.broadcasted_iota(jnp.int32, (NY, NX), 0)
    lane = lax.broadcasted_iota(jnp.int32, (NY, NX), 1)
    zero = jnp.zeros((NY, NX), jnp.float32)

    def pair(v):
        return h * (diffuse - jnp.minimum(v, 0.0)), h * (diffuse + jnp.maximum(v, 0.0))

    (above_z, below_z), (above_y, below_y), (above_x, below_x) = pair(vz), pair(vy), pair(vx)
    out[0, index] = above_z
    out[1, index] = below_z
    out[2, index] = jnp.where(row == NY - 1, zero, above_y)
    out[3, index] = jnp.where(row == 0, zero, below_y)
    out[4, index] = jnp.where(lane == NX - 1, zero, above_x)
    out[5, index] = jnp.where(lane == 0, zero, below_x)
    out[6, index] = 1.0 - (above_z + below_z + above_y + below_y + above_x + below_x)


def pack_kernel(guesses, forcing, initial, kappa, velocity, own, outer, inner, more_outer, more_inner):
    odd = lax.axis_index("space") % 2
    first = (lax.axis_index("tm") == 0).astype(jnp.float32)
    sign = (1 - 2 * odd).astype(jnp.float32)
    for z in range(L):
        i = z + odd * (L - 1 - 2 * z)
        own[z] = guesses[0, i]
        own[L + z] = first * initial[i]
        own[2 * L + z] = STEP * forcing[0, i]
        own[3 * L + z] = kappa[i]
        own[4 * L + z] = sign * velocity[0, i]
        own[5 * L + z] = velocity[1, i]
        own[6 * L + z] = velocity[2, i]
    at = 0
    for field in range(7):
        count = SENT[min(field, 3)]
        for i in range(count):
            outer[at + i] = own[field * L + i]
            inner[at + i] = own[field * L + L - 1 - i]
        at += count
    at = 0
    for field in range(3, 7):
        for i in range(FINE_HALO, COARSE_HALO):
            more_outer[at] = own[field * L + i]
            more_inner[at] = own[field * L + L - 1 - i]
            at += 1


def local_kernel(own, outer, inner, d, phi, coef, c, y, b):
    starts = (0, SENT[0], SENT[0] + SENT[1], SENT[0] + SENT[1] + SENT[2])

    def get(field, z):
        at = starts[min(field, 3)] + max(field - 3, 0) * FINE_HALO
        return ext(own, outer, inner, z, at, at, field * L)

    for z in range(-FINE_HALO, L + FINE_HALO):
        vz = get(4, z)
        if not 0 <= z < L:
            vz = -vz
        write_coefs(coef, z + FINE_HALO, get(3, z), vz, get(5, z), get(6, z), STEP)
    for z in range(-6, L + 6):
        y[z + 6] = get(1, z)
    for z in range(-4, L + 4):
        c[z + 4] = get(0, z)
    for step in range(4):
        halo = 5 - step
        sweep(y, 6, coef, FINE_HALO, -halo, L + halo, lambda z, cur, new: new + get(2, z))
        halo = 3 - step
        sweep(c, 4, coef, FINE_HALO, -halo, L + halo)
    for z in range(-2, L + 2):
        b[z + 2] = y[z + 6] - get(0, z)
    for z in range(L):
        phi[z] = y[z + 6]
    for halo in (1, 0):
        sweep(b, 2, coef, FINE_HALO, -halo, L + halo, lambda z, cur, new: 2.0 * new - cur)
    for z in range(L):
        d[z] = c[z + 4] + b[z + 2]


def coarse_kernel(own, outer, inner, more_outer, more_inner, coef):
    start = FIRST - 4 * FINE_HALO
    more = COARSE_HALO - FINE_HALO

    def get(k, z):
        beyond = -1 - z if z < 0 else z - L
        if beyond < FINE_HALO:
            return ext(own, outer, inner, z, start + k * FINE_HALO, start + k * FINE_HALO, (3 + k) * L)
        return (more_outer if z < 0 else more_inner)[k * more + beyond - FINE_HALO]

    for z in range(-COARSE_HALO, L + COARSE_HALO):
        vz = get(1, z)
        if not 0 <= z < L:
            vz = -vz
        write_coefs(coef, z + COARSE_HALO, get(0, z), vz, get(2, z), get(3, z), 2.0 * STEP)


def slab_pack_kernel(g, outer, inner):
    at = 0
    for k, count in enumerate((6, 4, 2)):
        for i in range(count):
            outer[at] = g[k, i]
            inner[at] = g[k, L - 1 - i]
            at += 1


def slab_kernel(g, outer, inner, coef, total, relay, prefix, v):
    place = lax.axis_index("tm") % 4
    for z in range(-6, L + 6):
        v[z + 6] = ext(g.at[0], outer, inner, z)

    def keep(wanted):
        @pl.when(place == wanted)
        def _():
            for z in range(-3, L + 3):
                prefix[z + 3] = v[z + 6]

    @pl.when(place < 2)
    def _():
        for z in range(L + 6):
            prefix[z] = jnp.zeros((NY, NX), jnp.float32)

    keep(2)
    coarse_twice(v, 6, coef, 6)
    for z in range(-4, L + 4):
        v[z + 6] += ext(g.at[1], outer, inner, z, 6, 6)
    keep(3)
    coarse_twice(v, 6, coef, 4)
    for z in range(-2, L + 2):
        v[z + 6] += ext(g.at[2], outer, inner, z, 10, 10)

    @pl.when(place == 0)
    def _():
        for z in range(L):
            relay[z] = v[z + 6]

    coarse_twice(v, 6, coef, 2)
    for z in range(L):
        total[z] = v[z + 6] + g[3, z]
        relay[L + z] = g[3, z]

    @pl.when(place > 0)
    def _():
        for z in range(L):
            relay[z] = total[z]


def chain1_kernel(far, far_outer, far_inner, middle, coef, outer, inner, u):
    place = lax.axis_index("tm") % 4
    for i in range(L):
        u[L - 1 - i] = far_outer[i]
        u[L + i] = far[i]
        u[2 * L + i] = far_inner[L - 1 - i]
    for i in range(4):
        if i < 3:

            @pl.when(place >= 3 - i)
            def _():
                coarse_twice(u, L, coef, 8 - 2 * i)
        else:
            coarse_twice(u, L, coef, 2)

    @pl.when(place == 3)
    def _():
        for z in range(L):
            u[L + z] += middle[z]

    for z in range(L):
        outer[z] = u[L + z]
        inner[z] = u[L + L - 1 - z]
    for i in range(6):
        outer[L + i] = middle[i]
        inner[L + i] = middle[L - 1 - i]


def chain2_kernel(held, outer, inner, middle, relay, shifted, own, coef, mine, to_outer, to_inner, u):
    place = lax.axis_index("tm") % 4
    first = (lax.axis_index("tm") == 0).astype(jnp.float32)
    for z in range(-L, 2 * L):
        u[L + z] = ext(held, outer, inner, z)
    for i in range(4):
        halo = 6 - 2 * i
        coarse_twice(u, L, coef, halo + 2)

        @pl.when(place == (2 - i) % 4)
        def _():
            for z in range(-halo, L + halo):
                u[L + z] += ext(relay, None, None, z) if i == 3 else ext(middle, outer, inner, z, L, L)

    for z in range(L):
        mine[z] = u[L + z]
        mine[L + z] = shifted[z] + own[L + z]
    for i in range(7):
        to_outer[i] = u[L + i]
        to_inner[i] = u[2 * L - 1 - i]
    for i in range(5):
        to_outer[7 + i] = relay[i]
        to_inner[7 + i] = relay[L - 1 - i]
    for i in range(3):
        to_outer[12 + i] = mine[L + i]
        to_inner[12 + i] = mine[2 * L - 1 - i]


def finish_kernel(mine, outer, inner, relay, prefix, g, phi, own, f_outer, f_inner, coef, fine, out, u, w):
    place = lax.axis_index("tm") % 4
    odd = lax.axis_index("space") % 2
    for z in range(-7, L + 7):
        u[7 + z] = ext(mine, outer, inner, z)

    def add_relay(halo):
        for z in range(-halo, L + halo):
            u[7 + z] += ext(relay, outer, inner, z, 7, 7)

    sweep(u, 7, coef, COARSE_HALO, -6, L + 6)
    sweep(u, 7, coef, COARSE_HALO, -5, L + 5)

    @pl.when(place == 2)
    def _():
        add_relay(5)

    sweep(u, 7, coef, COARSE_HALO, -4, L + 4)
    sweep(u, 7, coef, COARSE_HALO, -3, L + 3)

    @pl.when(place < 2)
    def _():
        add_relay(3)

    for z in range(-3, L + 3):
        g_t = u[7 + z] + prefix[3 + z]
        w[3 + z] = g_t
        u[7 + z] = g_t + ext(mine, outer, inner, z, 12, 12, L)
    coarse_twice(w, 3, coef, 2)

    @pl.when(place == 0)
    def _():
        for z in range(L):
            out[3, z + odd * (L - 1 - 2 * z)] = w[3 + z] + phi[z] + relay[L + z]

    @pl.when(place > 0)
    def _():
        for z in range(L):
            out[3, z + odd * (L - 1 - 2 * z)] = w[3 + z] + phi[z] + g[place - 1, z]

    at = SENT[0] + SENT[1]
    for step in range(3):
        halo = 2 - step
        sweep(u, 7, fine, FINE_HALO, -halo, L + halo,
              lambda z, cur, new: new + ext(own, f_outer, f_inner, z, at, at, 2 * L))
        for z in range(L):
            out[step, z + odd * (L - 1 - 2 * z)] = u[7 + z]


def body(guesses, forcing, initial, kappa, velocity):
    count, times = lax.axis_size("space"), lax.axis_size("tm")
    facing = [(i, i + 1) for i in range(1, count - 1, 2)]
    facing += [(b, a) for a, b in facing]
    paired = [(i, i ^ 1) for i in range(count)]

    def from_outer(x):
        return lax.ppermute(x, "space", facing)

    def from_inner(x):
        return lax.ppermute(x, "space", paired)

    def later(x, steps, moves=None):
        moves = [(i, i) for i in range(count)] if moves is None else moves
        pairs = [(t * count + a, (t + steps) * count + b) for t in range(times - steps) for a, b in moves]
        return lax.ppermute(x, ("tm", "space"), pairs)

    own, outer, inner, more_outer, more_inner = call(pack_kernel, (7 * L, FIRST, FIRST, MORE, MORE))(
        guesses, forcing, initial, kappa, velocity
    )
    outer, inner = from_outer(outer), from_inner(inner)
    more_outer, more_inner = from_outer(more_outer), from_inner(more_inner)
    d, phi, fine = call(local_kernel, (L, L, (7, L + 2 * FINE_HALO)), (L + 8, L + 12, L + 4))(own, outer, inner)
    (coef,) = call(coarse_kernel, ((7, L + 2 * COARSE_HALO),))(own, outer, inner, more_outer, more_inner)
    groups = [[4 * a + b for b in range(4)] for a in range(times // 4)]
    g = lax.all_gather(d, "tm", axis_index_groups=groups)
    shifted = later(phi, 1)
    slab_outer, slab_inner = call(slab_pack_kernel, (12, 12))(g)
    slab_outer, slab_inner = from_outer(slab_outer), from_inner(slab_inner)
    total, relay, prefix = call(slab_kernel, (L, 2 * L, L + 6), (L + 12,))(g, slab_outer, slab_inner, coef)
    far = later(total, 12)
    far_outer = later(total, 12, facing)
    far_inner = later(total, 12, paired)
    middle = later(total, 8)
    relay = later(relay, 4)
    c1_outer, c1_inner = call(chain1_kernel, (L + 6, L + 6), (3 * L,))(far, far_outer, far_inner, middle, coef)
    mine, c2_outer, c2_inner = call(chain2_kernel, (2 * L, 15, 15), (3 * L,))(
        c1_outer, from_outer(c1_outer), from_inner(c1_inner), middle, relay, shifted, own, coef
    )
    (out,) = call(finish_kernel, ((4, L),), (L + 14, L + 6))(
        mine, from_outer(c2_outer), from_inner(c2_inner), relay, prefix, g, phi, own, outer, inner, coef, fine
    )
    return out


def solution(mesh):
    placed = (
        P("tm", "space", None, None),
        P("tm", "space", None, None),
        P("space", None, None),
        P("space", None, None),
        P(None, "space", None, None),
    )
    return jax.shard_map(
        body, mesh=mesh, in_specs=placed, out_specs=P("tm", "space", None, None), check_vma=False
    )
```

time: 557 us -> 103 us (0.18)
  the two profiles are of different devices: /device:TPU:66 before, /device:TPU:95 now
where the time goes in v1:
time: 103 us; the launch traced here: 102 us
  starting transfers between devices  37.6 us (37%)
  waiting for transfers between devices  31.4 us (30%)
  blocking collectives  21.6 us (21%)
  Pallas kernels  6.81 us (7%)
  local copies, waits for them, and re-layouts  4.61 us (4%)
    all_gather x1, blocking collectives, body(): g = lax.all_gather(d, 'tm', axis_index_groups=groups)  21.6 us
    ppermute x6, waiting for transfers between devices, later(): return lax.ppermute(x, ('tm', 'space'), pairs)  18.4 us
    ppermute x5, starting transfers between devices, from_outer(): return lax.ppermute(x, 'space', facing)  16.7 us
    ppermute x5, waiting for transfers between devices, from_outer(): return lax.ppermute(x, 'space', facing)  13 us
    ppermute x5, starting transfers between devices, from_inner(): return lax.ppermute(x, 'space', paired)  10.5 us
    ppermute x6, starting transfers between devices, later(): return lax.ppermute(x, ('tm', 'space'), pairs)  10.5 us
    unnamed x10, local copies, waits for them, and re-layouts  4.61 us
    pallas_call x1, Pallas kernels, body(): call(finish_kernel, ((4, L),), (L + 14, L + 6))  2.17 us
  transfers between devices with their start and end apart: 16, of which 7 were waited for; matrix products, arithmetic and copies ran while one was open for 0% of the time, Pallas kernels for 1%

profile of v1, /device:TPU:95, one launch (start us, length us, event | category | flops | bytes accessed | tf_op | source)
XLA Modules:
  0.0 102.2 jit_solution(3572498171092674674)
XLA Ops:
  4.8 5.0 %collective-permute-start = (f32[35,32,128]{2,1,0:T(8,128)S(1)}, f32[35,32,128]{2,1,0:T(8,128)S(1)}, u32[]{:S(2)}, u32[]{:S(2)}) collective-permute-start(f32[35,32,128]{2,1,0:T(8,128)S(1)} %get-tuple-element.24), channel_id=1, source_target_pairs={{1,2},{3,4},{5,6},{7,8},{9,10},{11,12},{13,14},{15,16},{17,18},{19... | collective-permute-start | bytes 1720328 | tf_op jit(solution)/shard_map/ppermute | solution.py:321
  9.8 1.9 %collective-permute-start.1 = (f32[35,32,128]{2,1,0:T(8,128)S(1)}, f32[35,32,128]{2,1,0:T(8,128)S(1)}, u32[]{:S(2)}, u32[]{:S(2)}) collective-permute-start(f32[35,32,128]{2,1,0:T(8,128)S(1)} %get-tuple-element.25), channel_id=1, source_target_pairs={{0,1},{1,0},{2,3},{3,2},{4,5},{5,4},{6,7},{7,6},{8,9},{9,8},{10,11... | collective-permute-start | bytes 1720328 | tf_op jit(solution)/shard_map/ppermute | solution.py:324
  11.7 5.4 %collective-permute-done.outer.f_outer = f32[35,32,128]{2,1,0:T(8,128)S(1)} collective-permute-done((f32[35,32,128]{2,1,0:T(8,128)S(1)}, f32[35,32,128]{2,1,0:T(8,128)S(1)}, u32[]{:S(2)}, u32[]{:S(2)}) %collective-permute-start) | collective-permute-done | bytes 573472 | tf_op jit(solution)/shard_map/ppermute | solution.py:321
  17.1 1.5 %shard_map.56 = (f32[8,32,128]{2,1,0:T(8,128)S(1)}, f32[8,32,128]{2,1,0:T(8,128)S(1)}, f32[7,18,32,128]{3,2,1,0:T(8,128)S(1)}) custom-call(f32[56,32,128]{2,1,0:T(8,128)S(1)} %get-tuple-element.23.own, f32[35,32,128]{2,1,0:T(8,128)S(1)} %collective-permute-done.outer.f_outer, f32[35,32,128]{2,1,0:T(8,128)S(1)} %collective-permute-done.1.inner.f_inner), custom_call_target="tpu_custom_call" | custom-call | tf_op jit(solution)/shard_map/pallas_call | solution.py:336
  18.6 21.6 %all-gather = f32[32,32,128]{2,1,0:T(8,128)S(1)} all-gather(f32[8,32,128]{2,1,0:T(8,128)S(1)} %get-tuple-element.26), channel_id=2, replica_groups={{0,32,64,96},{128,160,192,224},{256,288,320,352},{384,416,448,480},{1,3..., dimensions={0}, use_global_device_ids=true | all-gather | bytes 655360 | tf_op jit(solution)/shard_map/all_gather | solution.py:339
  40.2 4.9 %collective-permute-start.2 = (f32[12,32,128]{2,1,0:T(8,128)S(1)}, f32[12,32,128]{2,1,0:T(8,128)S(1)}, u32[]{:S(2)}, u32[]{:S(2)}) collective-permute-start(f32[12,32,128]{2,1,0:T(8,128)S(1)} %get-tuple-element.27), channel_id=1, source_target_pairs={{1,2},{3,4},{5,6},{7,8},{9,10},{11,12},{13,14},{15,16},{17,18},{19... | collective-permute-start | bytes 589832 | tf_op jit(solution)/shard_map/ppermute | solution.py:321
  45.2 1.9 %collective-permute-start.3 = (f32[12,32,128]{2,1,0:T(8,128)S(1)}, f32[12,32,128]{2,1,0:T(8,128)S(1)}, u32[]{:S(2)}, u32[]{:S(2)}) collective-permute-start(f32[12,32,128]{2,1,0:T(8,128)S(1)} %get-tuple-element.28), channel_id=1, source_target_pairs={{0,1},{1,0},{2,3},{3,2},{4,5},{5,4},{6,7},{7,6},{8,9},{9,8},{10,11... | collective-permute-start | bytes 589832 | tf_op jit(solution)/shard_map/ppermute | solution.py:324
  47.1 1.9 %collective-permute-start.4 = (f32[8,32,128]{2,1,0:T(8,128)S(1)}, f32[8,32,128]{2,1,0:T(8,128)S(1)}, u32[]{:S(2)}, u32[]{:S(2)}) collective-permute-start(f32[8,32,128]{2,1,0:T(8,128)S(1)} %get-tuple-element.29), channel_id=1, source_target_pairs={{1,2},{3,4},{5,6},{7,8},{9,10},{11,12},{13,14},{15,16},{17,18},{19... | collective-permute-start | bytes 393224 | tf_op jit(solution)/shard_map/ppermute | solution.py:321
  49.0 2.4 %collective-permute-start.5 = (f32[8,32,128]{2,1,0:T(8,128)S(1)}, f32[8,32,128]{2,1,0:T(8,128)S(1)}, u32[]{:S(2)}, u32[]{:S(2)}) collective-permute-start(f32[8,32,128]{2,1,0:T(8,128)S(1)} %get-tuple-element.30), channel_id=1, source_target_pairs={{0,1},{1,0},{2,3},{3,2},{4,5},{5,4},{6,7},{7,6},{8,9},{9,8},{10,11... | collective-permute-start | bytes 393224 | tf_op jit(solution)/shard_map/ppermute | solution.py:324
  51.4 3.2 %collective-permute-done.4.more_outer = f32[8,32,128]{2,1,0:T(8,128)S(1)} collective-permute-done((f32[8,32,128]{2,1,0:T(8,128)S(1)}, f32[8,32,128]{2,1,0:T(8,128)S(1)}, u32[]{:S(2)}, u32[]{:S(2)}) %collective-permute-start.4) | collective-permute-done | bytes 131104 | tf_op jit(solution)/shard_map/ppermute | solution.py:321
  55.9 1.3 %collective-permute-start.9 = (f32[8,32,128]{2,1,0:T(8,128)S(1)}, f32[8,32,128]{2,1,0:T(8,128)S(1)}, u32[]{:S(2)}, u32[]{:S(2)}) collective-permute-start(f32[8,32,128]{2,1,0:T(8,128)S(1)} %get-tuple-element.31), channel_id=1, source_target_pairs={{0,256},{1,257},{2,258},{3,259},{4,260},{5,261},{6,262},{7,263},{8... | collective-permute-start | bytes 393224 | tf_op jit(solution)/shard_map/ppermute | solution.py:329
  57.2 1.3 %collective-permute-start.8 = (f32[8,32,128]{2,1,0:T(8,128)S(1)}, f32[8,32,128]{2,1,0:T(8,128)S(1)}, u32[]{:S(2)}, u32[]{:S(2)}) collective-permute-start(f32[8,32,128]{2,1,0:T(8,128)S(1)} %get-tuple-element.31), channel_id=1, source_target_pairs={{0,385},{1,384},{2,387},{3,386},{4,389},{5,388},{6,391},{7,390},{8... | collective-permute-start | bytes 393224 | tf_op jit(solution)/shard_map/ppermute | solution.py:329
  62.4 2.2 %collective-permute-done.9.middle = f32[8,32,128]{2,1,0:T(8,128)S(1)} collective-permute-done((f32[8,32,128]{2,1,0:T(8,128)S(1)}, f32[8,32,128]{2,1,0:T(8,128)S(1)}, u32[]{:S(2)}, u32[]{:S(2)}) %collective-permute-start.9) | collective-permute-done | bytes 131104 | tf_op jit(solution)/shard_map/ppermute | solution.py:329
  64.6 5.6 %collective-permute-done.8.far_inner = f32[8,32,128]{2,1,0:T(8,128)S(1)} collective-permute-done((f32[8,32,128]{2,1,0:T(8,128)S(1)}, f32[8,32,128]{2,1,0:T(8,128)S(1)}, u32[]{:S(2)}, u32[]{:S(2)}) %collective-permute-start.8) | collective-permute-done | bytes 131104 | tf_op jit(solution)/shard_map/ppermute | solution.py:329
  70.2 2.8 %collective-permute-done.6.far = f32[8,32,128]{2,1,0:T(8,128)S(1)} collective-permute-done((f32[8,32,128]{2,1,0:T(8,128)S(1)}, f32[8,32,128]{2,1,0:T(8,128)S(1)}, u32[]{:S(2)}, u32[]{:S(2)}) %collective-permute-start.6) | collective-permute-done | bytes 131104 | tf_op jit(solution)/shard_map/ppermute | solution.py:329
  73.3 2.3 %collective-permute-start.11 = (f32[14,32,128]{2,1,0:T(8,128)S(1)}, f32[14,32,128]{2,1,0:T(8,128)S(1)}, u32[]{:S(2)}, u32[]{:S(2)}) collective-permute-start(f32[14,32,128]{2,1,0:T(8,128)S(1)} %get-tuple-element.33), channel_id=1, source_target_pairs={{0,1},{1,0},{2,3},{3,2},{4,5},{5,4},{6,7},{7,6},{8,9},{9,8},{10,11... | collective-permute-start | bytes 688136 | tf_op jit(solution)/shard_map/ppermute | solution.py:324
  75.6 2.5 %collective-permute-start.10 = (f32[14,32,128]{2,1,0:T(8,128)S(1)}, f32[14,32,128]{2,1,0:T(8,128)S(1)}, u32[]{:S(2)}, u32[]{:S(2)}) collective-permute-start(f32[14,32,128]{2,1,0:T(8,128)S(1)} %get-tuple-element.32.held), channel_id=1, source_target_pairs={{1,2},{3,4},{5,6},{7,8},{9,10},{11,12},{13,14},{15,16},{17,18},{19... | collective-permute-start | bytes 688136 | tf_op jit(solution)/shard_map/ppermute | solution.py:321
  78.1 4.0 %collective-permute-start.13 = (f32[8,32,128]{2,1,0:T(8,128)S(1)}, f32[8,32,128]{2,1,0:T(8,128)S(1)}, u32[]{:S(2)}, u32[]{:S(2)}) collective-permute-start(f32[8,32,128]{2,1,0:T(8,128)S(1)} %get-tuple-element.35.phi), channel_id=1, source_target_pairs={{0,32},{1,33},{2,34},{3,35},{4,36},{5,37},{6,38},{7,39},{8,40},{9,... | collective-permute-start | bytes 393224 | tf_op jit(solution)/shard_map/ppermute | solution.py:329
  82.1 7.8 %collective-permute-done.13.shifted = f32[8,32,128]{2,1,0:T(8,128)S(1)} collective-permute-done((f32[8,32,128]{2,1,0:T(8,128)S(1)}, f32[8,32,128]{2,1,0:T(8,128)S(1)}, u32[]{:S(2)}, u32[]{:S(2)}) %collective-permute-start.13) | collective-permute-done | bytes 131104 | tf_op jit(solution)/shard_map/ppermute | solution.py:329
  89.9 1.4 %shard_map.61 = (f32[16,32,128]{2,1,0:T(8,128)S(1)}, f32[15,32,128]{2,1,0:T(8,128)S(1)}, f32[15,32,128]{2,1,0:T(8,128)S(1)}) custom-call(f32[14,32,128]{2,1,0:T(8,128)S(1)} %get-tuple-element.32.held, f32[14,32,128]{2,1,0:T(8,128)S(1)} %collective-permute-done.10.outer, f32[14,32,128]{2,1,0:T(8,128)S(1)} %collective-permute-done.11.inner, ...), custom_call_target="tpu_custom_call" | custom-call | tf_op jit(solution)/shard_map/pallas_call | solution.py:350
  91.3 2.4 %collective-permute-start.14 = (f32[15,32,128]{2,1,0:T(8,128)S(1)}, f32[15,32,128]{2,1,0:T(8,128)S(1)}, u32[]{:S(2)}, u32[]{:S(2)}) collective-permute-start(f32[15,32,128]{2,1,0:T(8,128)S(1)} %get-tuple-element.37), channel_id=1, source_target_pairs={{1,2},{3,4},{5,6},{7,8},{9,10},{11,12},{13,14},{15,16},{17,18},{19... | collective-permute-start | bytes 737288 | tf_op jit(solution)/shard_map/ppermute | solution.py:321
  93.7 1.9 %collective-permute-start.15 = (f32[15,32,128]{2,1,0:T(8,128)S(1)}, f32[15,32,128]{2,1,0:T(8,128)S(1)}, u32[]{:S(2)}, u32[]{:S(2)}) collective-permute-start(f32[15,32,128]{2,1,0:T(8,128)S(1)} %get-tuple-element.38), channel_id=1, source_target_pairs={{0,1},{1,0},{2,3},{3,2},{4,5},{5,4},{6,7},{7,6},{8,9},{9,8},{10,11... | collective-permute-start | bytes 737288 | tf_op jit(solution)/shard_map/ppermute | solution.py:324
  95.6 4.4 %collective-permute-done.14.outer = f32[15,32,128]{2,1,0:T(8,128)S(1)} collective-permute-done((f32[15,32,128]{2,1,0:T(8,128)S(1)}, f32[15,32,128]{2,1,0:T(8,128)S(1)}, u32[]{:S(2)}, u32[]{:S(2)}) %collective-permute-start.14) | collective-permute-done | bytes 245792 | tf_op jit(solution)/shard_map/ppermute | solution.py:321
  100.1 2.2 %shard_map.62 = f32[4,8,32,128]{3,2,1,0:T(8,128)} custom-call(f32[16,32,128]{2,1,0:T(8,128)S(1)} %get-tuple-element.36.mine, f32[15,32,128]{2,1,0:T(8,128)S(1)} %collective-permute-done.14.outer, f32[15,32,128]{2,1,0:T(8,128)S(1)} %collective-permute-done.15.inner, f32[16,32,128]{2,1,0:T(8,128)S(1)} %collective-permute-done.12.relay, ...), custom_call_target="tpu_custom_call" | custom-call | tf_op jit(solution)/shard_map/pallas_call | solution.py:353
  (27 shorter events, 10.3 us)
Async XLA Ops:
  0.0 1.0 copy-start
  1.0 0.9 copy-start.1
  1.9 0.9 copy-start.2
  2.8 0.9 copy-start.3
  3.7 0.9 copy-start.4
  4.8 12.4 %collective-permute-start = (f32[35,32,128]{2,1,0:T(8,128)S(1)}, f32[35,32,128]{2,1,0:T(8,128)S(1)}, u32[]{:S(2)}, u32[]{:S(2)}) collective-permute-start(f32[35,32,128]{2,1,0:T(8,128)S(1)} %get-tuple-element.24), channel_id=1, source_target_pairs={{1,2},{3,4},{5,6},{7,8},{9,10},{11,12},{13,14},{15,16},{17,18},{19... | collective-permute-start | bytes 1720328 | tf_op jit(solution)/shard_map/ppermute | solution.py:321
  9.8 7.4 %collective-permute-start.1 = (f32[35,32,128]{2,1,0:T(8,128)S(1)}, f32[35,32,128]{2,1,0:T(8,128)S(1)}, u32[]{:S(2)}, u32[]{:S(2)}) collective-permute-start(f32[35,32,128]{2,1,0:T(8,128)S(1)} %get-tuple-element.25), channel_id=1, source_target_pairs={{0,1},{1,0},{2,3},{3,2},{4,5},{5,4},{6,7},{7,6},{8,9},{9,8},{10,11... | collective-permute-start | bytes 1720328 | tf_op jit(solution)/shard_map/ppermute | solution.py:324
  40.2 14.7 %collective-permute-start.2 = (f32[12,32,128]{2,1,0:T(8,128)S(1)}, f32[12,32,128]{2,1,0:T(8,128)S(1)}, u32[]{:S(2)}, u32[]{:S(2)}) collective-permute-start(f32[12,32,128]{2,1,0:T(8,128)S(1)} %get-tuple-element.27), channel_id=1, source_target_pairs={{1,2},{3,4},{5,6},{7,8},{9,10},{11,12},{13,14},{15,16},{17,18},{19... | collective-permute-start | bytes 589832 | tf_op jit(solution)/shard_map/ppermute | solution.py:321
  45.2 9.8 %collective-permute-start.3 = (f32[12,32,128]{2,1,0:T(8,128)S(1)}, f32[12,32,128]{2,1,0:T(8,128)S(1)}, u32[]{:S(2)}, u32[]{:S(2)}) collective-permute-start(f32[12,32,128]{2,1,0:T(8,128)S(1)} %get-tuple-element.28), channel_id=1, source_target_pairs={{0,1},{1,0},{2,3},{3,2},{4,5},{5,4},{6,7},{7,6},{8,9},{9,8},{10,11... | collective-permute-start | bytes 589832 | tf_op jit(solution)/shard_map/ppermute | solution.py:324
  47.1 7.5 %collective-permute-start.4 = (f32[8,32,128]{2,1,0:T(8,128)S(1)}, f32[8,32,128]{2,1,0:T(8,128)S(1)}, u32[]{:S(2)}, u32[]{:S(2)}) collective-permute-start(f32[8,32,128]{2,1,0:T(8,128)S(1)} %get-tuple-element.29), channel_id=1, source_target_pairs={{1,2},{3,4},{5,6},{7,8},{9,10},{11,12},{13,14},{15,16},{17,18},{19... | collective-permute-start | bytes 393224 | tf_op jit(solution)/shard_map/ppermute | solution.py:321
  49.0 5.6 %collective-permute-start.5 = (f32[8,32,128]{2,1,0:T(8,128)S(1)}, f32[8,32,128]{2,1,0:T(8,128)S(1)}, u32[]{:S(2)}, u32[]{:S(2)}) collective-permute-start(f32[8,32,128]{2,1,0:T(8,128)S(1)} %get-tuple-element.30), channel_id=1, source_target_pairs={{0,1},{1,0},{2,3},{3,2},{4,5},{5,4},{6,7},{7,6},{8,9},{9,8},{10,11... | collective-permute-start | bytes 393224 | tf_op jit(solution)/shard_map/ppermute | solution.py:324
  55.9 8.7 %collective-permute-start.9 = (f32[8,32,128]{2,1,0:T(8,128)S(1)}, f32[8,32,128]{2,1,0:T(8,128)S(1)}, u32[]{:S(2)}, u32[]{:S(2)}) collective-permute-start(f32[8,32,128]{2,1,0:T(8,128)S(1)} %get-tuple-element.31), channel_id=1, source_target_pairs={{0,256},{1,257},{2,258},{3,259},{4,260},{5,261},{6,262},{7,263},{8... | collective-permute-start | bytes 393224 | tf_op jit(solution)/shard_map/ppermute | solution.py:329
  57.2 13.0 %collective-permute-start.8 = (f32[8,32,128]{2,1,0:T(8,128)S(1)}, f32[8,32,128]{2,1,0:T(8,128)S(1)}, u32[]{:S(2)}, u32[]{:S(2)}) collective-permute-start(f32[8,32,128]{2,1,0:T(8,128)S(1)} %get-tuple-element.31), channel_id=1, source_target_pairs={{0,385},{1,384},{2,387},{3,386},{4,389},{5,388},{6,391},{7,390},{8... | collective-permute-start | bytes 393224 | tf_op jit(solution)/shard_map/ppermute | solution.py:329
  58.5 11.7 %collective-permute-start.7 = (f32[8,32,128]{2,1,0:T(8,128)S(1)}, f32[8,32,128]{2,1,0:T(8,128)S(1)}, u32[]{:S(2)}, u32[]{:S(2)}) collective-permute-start(f32[8,32,128]{2,1,0:T(8,128)S(1)} %get-tuple-element.31), channel_id=1, source_target_pairs={{1,386},{3,388},{5,390},{7,392},{9,394},{11,396},{13,398},{15,400}... | collective-permute-start | bytes 393224 | tf_op jit(solution)/shard_map/ppermute | solution.py:329
  59.8 13.2 %collective-permute-start.6 = (f32[8,32,128]{2,1,0:T(8,128)S(1)}, f32[8,32,128]{2,1,0:T(8,128)S(1)}, u32[]{:S(2)}, u32[]{:S(2)}) collective-permute-start(f32[8,32,128]{2,1,0:T(8,128)S(1)} %get-tuple-element.31), channel_id=1, source_target_pairs={{0,384},{1,385},{2,386},{3,387},{4,388},{5,389},{6,390},{7,391},{8... | collective-permute-start | bytes 393224 | tf_op jit(solution)/shard_map/ppermute | solution.py:329
  61.1 28.8 %collective-permute-start.12 = (f32[16,32,128]{2,1,0:T(8,128)S(1)}, f32[16,32,128]{2,1,0:T(8,128)S(1)}, u32[]{:S(2)}, u32[]{:S(2)}) collective-permute-start(f32[16,32,128]{2,1,0:T(8,128)S(1)} %get-tuple-element.34), channel_id=1, source_target_pairs={{0,128},{1,129},{2,130},{3,131},{4,132},{5,133},{6,134},{7,135},{8... | collective-permute-start | bytes 786440 | tf_op jit(solution)/shard_map/ppermute | solution.py:329
  73.3 16.6 %collective-permute-start.11 = (f32[14,32,128]{2,1,0:T(8,128)S(1)}, f32[14,32,128]{2,1,0:T(8,128)S(1)}, u32[]{:S(2)}, u32[]{:S(2)}) collective-permute-start(f32[14,32,128]{2,1,0:T(8,128)S(1)} %get-tuple-element.33), channel_id=1, source_target_pairs={{0,1},{1,0},{2,3},{3,2},{4,5},{5,4},{6,7},{7,6},{8,9},{9,8},{10,11... | collective-permute-start | bytes 688136 | tf_op jit(solution)/shard_map/ppermute | solution.py:324
  75.6 14.3 %collective-permute-start.10 = (f32[14,32,128]{2,1,0:T(8,128)S(1)}, f32[14,32,128]{2,1,0:T(8,128)S(1)}, u32[]{:S(2)}, u32[]{:S(2)}) collective-permute-start(f32[14,32,128]{2,1,0:T(8,128)S(1)} %get-tuple-element.32.held), channel_id=1, source_target_pairs={{1,2},{3,4},{5,6},{7,8},{9,10},{11,12},{13,14},{15,16},{17,18},{19... | collective-permute-start | bytes 688136 | tf_op jit(solution)/shard_map/ppermute | solution.py:321
  78.1 11.8 %collective-permute-start.13 = (f32[8,32,128]{2,1,0:T(8,128)S(1)}, f32[8,32,128]{2,1,0:T(8,128)S(1)}, u32[]{:S(2)}, u32[]{:S(2)}) collective-permute-start(f32[8,32,128]{2,1,0:T(8,128)S(1)} %get-tuple-element.35.phi), channel_id=1, source_target_pairs={{0,32},{1,33},{2,34},{3,35},{4,36},{5,37},{6,38},{7,39},{8,40},{9,... | collective-permute-start | bytes 393224 | tf_op jit(solution)/shard_map/ppermute | solution.py:329
  91.3 8.7 %collective-permute-start.14 = (f32[15,32,128]{2,1,0:T(8,128)S(1)}, f32[15,32,128]{2,1,0:T(8,128)S(1)}, u32[]{:S(2)}, u32[]{:S(2)}) collective-permute-start(f32[15,32,128]{2,1,0:T(8,128)S(1)} %get-tuple-element.37), channel_id=1, source_target_pairs={{1,2},{3,4},{5,6},{7,8},{9,10},{11,12},{13,14},{15,16},{17,18},{19... | collective-permute-start | bytes 737288 | tf_op jit(solution)/shard_map/ppermute | solution.py:321
  93.7 6.3 %collective-permute-start.15 = (f32[15,32,128]{2,1,0:T(8,128)S(1)}, f32[15,32,128]{2,1,0:T(8,128)S(1)}, u32[]{:S(2)}, u32[]{:S(2)}) collective-permute-start(f32[15,32,128]{2,1,0:T(8,128)S(1)} %get-tuple-element.38), channel_id=1, source_target_pairs={{0,1},{1,0},{2,3},{3,2},{4,5},{5,4},{6,7},{7,6},{8,9},{9,8},{10,11... | collective-permute-start | bytes 737288 | tf_op jit(solution)/shard_map/ppermute | solution.py:324

commit v2 on v1

--- a/solution.py
+++ b/solution.py
@@ -13,9 +13,8 @@
 STEP = 0.3
 FINE_HALO = 5
 COARSE_HALO = 7
-SENT = (4, 6, 5, FINE_HALO)
-FIRST = SENT[0] + SENT[1] + SENT[2] + 4 * FINE_HALO
-MORE = 4 * (COARSE_HALO - FINE_HALO)
+SENT = (4, 6, 5, COARSE_HALO)
+FIRST = SENT[0] + SENT[1] + SENT[2] + 4 * COARSE_HALO
 VMEM = pltpu.VMEM
 
 
@@ -80,39 +79,39 @@
     out[6, index] = 1.0 - (above_z + below_z + above_y + below_y + above_x + below_x)
 
 
-def pack_kernel(guesses, forcing, initial, kappa, velocity, own, outer, inner, more_outer, more_inner):
+def pack_kernel(guesses, forcing, initial, kappa, velocity, own, outer, inner, held, sems):
     odd = lax.axis_index("space") % 2
     first = (lax.axis_index("tm") == 0).astype(jnp.float32)
     sign = (1 - 2 * odd).astype(jnp.float32)
-    for z in range(L):
-        i = z + odd * (L - 1 - 2 * z)
-        own[z] = guesses[0, i]
-        own[L + z] = first * initial[i]
-        own[2 * L + z] = STEP * forcing[0, i]
-        own[3 * L + z] = kappa[i]
-        own[4 * L + z] = sign * velocity[0, i]
-        own[5 * L + z] = velocity[1, i]
-        own[6 * L + z] = velocity[2, i]
+    sources = (guesses.at[0], initial, forcing.at[0], kappa, velocity.at[0], velocity.at[1], velocity.at[2])
+    copies = [pltpu.make_async_copy(source, held.at[k], sems.at[k]) for k, source in enumerate(sources)]
+    for copy in copies:
+        copy.start()
     at = 0
-    for field in range(7):
+    for field, copy in enumerate(copies):
+        copy.wait()
+        for z in range(L):
+            value = held[field, z + odd * (L - 1 - 2 * z)]
+            if field in (1, 2, 4):
+                value = (None, first, STEP, None, sign)[field] * value
+            own[field * L + z] = value
         count = SENT[min(field, 3)]
         for i in range(count):
             outer[at + i] = own[field * L + i]
             inner[at + i] = own[field * L + L - 1 - i]
         at += count
-    at = 0
-    for field in range(3, 7):
-        for i in range(FINE_HALO, COARSE_HALO):
-            more_outer[at] = own[field * L + i]
-            more_inner[at] = own[field * L + L - 1 - i]
-            at += 1
+
+
+def settle_kernel(held, own):
+    for i in range(7 * L):
+        own[i] = held[i]
 
 
 def local_kernel(own, outer, inner, d, phi, coef, c, y, b):
     starts = (0, SENT[0], SENT[0] + SENT[1], SENT[0] + SENT[1] + SENT[2])
 
     def get(field, z):
-        at = starts[min(field, 3)] + max(field - 3, 0) * FINE_HALO
+        at = starts[min(field, 3)] + max(field - 3, 0) * COARSE_HALO
         return ext(own, outer, inner, z, at, at, field * L)
 
     for z in range(-FINE_HALO, L + FINE_HALO):
@@ -139,15 +138,10 @@
         d[z] = c[z + 4] + b[z + 2]
 
 
-def coarse_kernel(own, outer, inner, more_outer, more_inner, coef):
-    start = FIRST - 4 * FINE_HALO
-    more = COARSE_HALO - FINE_HALO
-
+def coarse_kernel(own, outer, inner, coef):
     def get(k, z):
-        beyond = -1 - z if z < 0 else z - L
-        if beyond < FINE_HALO:
-            return ext(own, outer, inner, z, start + k * FINE_HALO, start + k * FINE_HALO, (3 + k) * L)
-        return (more_outer if z < 0 else more_inner)[k * more + beyond - FINE_HALO]
+        at = FIRST - (4 - k) * COARSE_HALO
+        return ext(own, outer, inner, z, at, at, (3 + k) * L)
 
     for z in range(-COARSE_HALO, L + COARSE_HALO):
         vz = get(1, z)
@@ -165,10 +159,12 @@
             at += 1
 
 
-def slab_kernel(g, outer, inner, coef, total, relay, prefix, v):
+def slab_kernel(g, outer, inner, coef, phi, total, relay, prefix, leaving, v):
     place = lax.axis_index("tm") % 4
     for z in range(-6, L + 6):
         v[z + 6] = ext(g.at[0], outer, inner, z)
+    for z in range(L):
+        leaving[z] = phi[z]
 
     def keep(wanted):
         @pl.when(place == wanted)
@@ -206,12 +202,14 @@
             relay[z] = total[z]
 
 
-def chain1_kernel(far, far_outer, far_inner, middle, coef, outer, inner, u):
+def chain1_kernel(far, pair, middle, shifted, own, coef, far_outer, outer, inner, psi, u):
     place = lax.axis_index("tm") % 4
+    other = 1 - lax.axis_index("space") % 2
     for i in range(L):
         u[L - 1 - i] = far_outer[i]
         u[L + i] = far[i]
-        u[2 * L + i] = far_inner[L - 1 - i]
+        u[2 * L + i] = pair[other, L - 1 - i]
+        psi[i] = shifted[i] + own[L + i]
     for i in range(4):
         if i < 3:
 
@@ -234,9 +232,8 @@
         inner[L + i] = middle[L - 1 - i]
 
 
-def chain2_kernel(held, outer, inner, middle, relay, shifted, own, coef, mine, to_outer, to_inner, u):
+def chain2_kernel(held, outer, inner, middle, relay, psi, coef, mine, to_outer, to_inner, u):
     place = lax.axis_index("tm") % 4
-    first = (lax.axis_index("tm") == 0).astype(jnp.float32)
     for z in range(-L, 2 * L):
         u[L + z] = ext(held, outer, inner, z)
     for i in range(4):
@@ -250,7 +247,7 @@
 
     for z in range(L):
         mine[z] = u[L + z]
-        mine[L + z] = shifted[z] + own[L + z]
+        mine[L + z] = psi[z]
     for i in range(7):
         to_outer[i] = u[L + i]
         to_inner[i] = u[2 * L - 1 - i]
@@ -328,27 +325,34 @@
         pairs = [(t * count + a, (t + steps) * count + b) for t in range(times - steps) for a, b in moves]
         return lax.ppermute(x, ("tm", "space"), pairs)
 
-    own, outer, inner, more_outer, more_inner = call(pack_kernel, (7 * L, FIRST, FIRST, MORE, MORE))(
-        guesses, forcing, initial, kappa, velocity
-    )
+    own, outer, inner = pl.pallas_call(
+        pack_kernel,
+        out_shape=[jax.ShapeDtypeStruct((n, NY, NX), jnp.float32) for n in (7 * L, FIRST, FIRST)],
+        in_specs=[pl.BlockSpec(memory_space=pltpu.HBM)] * 5,
+        scratch_shapes=[VMEM((7, L, NY, NX), jnp.float32), pltpu.SemaphoreType.DMA((7,))],
+    )(guesses, forcing, initial, kappa, velocity)
     outer, inner = from_outer(outer), from_inner(inner)
-    more_outer, more_inner = from_outer(more_outer), from_inner(more_inner)
+    (own,) = call(settle_kernel, (7 * L,))(own)
     d, phi, fine = call(local_kernel, (L, L, (7, L + 2 * FINE_HALO)), (L + 8, L + 12, L + 4))(own, outer, inner)
-    (coef,) = call(coarse_kernel, ((7, L + 2 * COARSE_HALO),))(own, outer, inner, more_outer, more_inner)
+    (coef,) = call(coarse_kernel, ((7, L + 2 * COARSE_HALO),))(own, outer, inner)
     groups = [[4 * a + b for b in range(4)] for a in range(times // 4)]
     g = lax.all_gather(d, "tm", axis_index_groups=groups)
-    shifted = later(phi, 1)
     slab_outer, slab_inner = call(slab_pack_kernel, (12, 12))(g)
     slab_outer, slab_inner = from_outer(slab_outer), from_inner(slab_inner)
-    total, relay, prefix = call(slab_kernel, (L, 2 * L, L + 6), (L + 12,))(g, slab_outer, slab_inner, coef)
+    total, relay, prefix, leaving = call(slab_kernel, (L, 2 * L, L + 6, L), (L + 12,))(
+        g, slab_outer, slab_inner, coef, phi
+    )
+    shifted = later(leaving, 1)
+    relay = later(relay, 4)
+    middle = later(total, 8)
+    far_outer = later(total, 12, facing)
     far = later(total, 12)
-    far_outer = later(total, 12, facing)
-    far_inner = later(total, 12, paired)
-    middle = later(total, 8)
-    relay = later(relay, 4)
-    c1_outer, c1_inner = call(chain1_kernel, (L + 6, L + 6), (3 * L,))(far, far_outer, far_inner, middle, coef)
+    pair = lax.all_gather(far, "space", axis_index_groups=[[i, i + 1] for i in range(0, count, 2)])
+    c1_outer, c1_inner, psi = call(chain1_kernel, (L + 6, L + 6, L), (3 * L,))(
+        far, pair, middle, shifted, own, coef, far_outer
+    )
     mine, c2_outer, c2_inner = call(chain2_kernel, (2 * L, 15, 15), (3 * L,))(
-        c1_outer, from_outer(c1_outer), from_inner(c1_inner), middle, relay, shifted, own, coef
+        c1_outer, from_outer(c1_outer), from_inner(c1_inner), middle, relay, psi, coef
     )
     (out,) = call(finish_kernel, ((4, L),), (L + 14, L + 6))(
         mine, from_outer(c2_outer), from_inner(c2_inner), relay, prefix, g, phi, own, outer, inner, coef, fine

time: 103 us -> 92 us (0.89)
  the two profiles are of different devices: /device:TPU:95 before, /device:TPU:61 now
where the time goes in v2:
time: 92 us; the launch traced here: 91.5 us
  starting transfers between devices  33.5 us (36%)
  waiting for transfers between devices  25.8 us (28%)
  blocking collectives  21.4 us (23%)
  Pallas kernels  9.43 us (10%)
  local copies, waits for them, and re-layouts  1.17 us (1%)
    ppermute x4, waiting for transfers between devices, from_outer(): return lax.ppermute(x, 'space', facing)  20.3 us
    all_gather x1, blocking collectives, body(): g = lax.all_gather(d, 'tm', axis_index_groups=groups)  19.4 us
    ppermute x4, starting transfers between devices, from_outer(): return lax.ppermute(x, 'space', facing)  15.2 us
    ppermute x5, starting transfers between devices, later(): return lax.ppermute(x, ('tm', 'space'), pairs)  10.6 us
    ppermute x4, starting transfers between devices, from_inner(): return lax.ppermute(x, 'space', paired)  7.68 us
    ppermute x5, waiting for transfers between devices, later(): return lax.ppermute(x, ('tm', 'space'), pairs)  5.46 us
    pallas_call x1, Pallas kernels, body(): pl.pallas_call(pack_kernel, out_shape=[jax.ShapeDtypeStruct((n, NY, NX),...  2.7 us
    pallas_call x1, Pallas kernels, body(): call(finish_kernel, ((4, L),), (L + 14, L + 6))  2.17 us
  transfers between devices with their start and end apart: 13, of which 5 were waited for; matrix products, arithmetic and copies ran while one was open for 0% of the time, Pallas kernels for 1%

profile of v2, /device:TPU:61, one launch (start us, length us, event | category | flops | bytes accessed | tf_op | source)
XLA Modules:
  0.0 91.5 jit_solution(9199816980549389089)
XLA Ops:
  0.0 2.7 %shard_map.55 = (f32[56,32,128]{2,1,0:T(8,128)}, f32[43,32,128]{2,1,0:T(8,128)}, f32[43,32,128]{2,1,0:T(8,128)}) custom-call(f32[1,8,32,128]{3,2,1,0:T(8,128)} %guesses.1, f32[1,8,32,128]{3,2,1,0:T(8,128)} %forcing.1, f32[8,32,128]{2,1,0:T(8,128)} %initial.1, f32[8,32,128]{2,1,0:T(8,128)} %kappa.1, f32[3,8,32,128]{3,2,1,0:T(8,128)} %velocity.1), custom_call_target="tpu_custom_call" | custom-call | tf_op jit(solution)/shard_map/pallas_call | solution.py:328
  2.7 3.8 %collective-permute-start = (f32[43,32,128]{2,1,0:T(8,128)}, f32[43,32,128]{2,1,0:T(8,128)S(1)}, u32[]{:S(2)}, u32[]{:S(2)}) collective-permute-start(f32[43,32,128]{2,1,0:T(8,128)} %get-tuple-element.24), channel_id=1, source_target_pairs={{1,2},{3,4},{5,6},{7,8},{9,10},{11,12},{13,14},{15,16},{17,18},{19... | collective-permute-start | bytes 2113544 | tf_op jit(solution)/shard_map/ppermute | solution.py:318
  6.5 1.9 %collective-permute-start.1 = (f32[43,32,128]{2,1,0:T(8,128)}, f32[43,32,128]{2,1,0:T(8,128)S(1)}, u32[]{:S(2)}, u32[]{:S(2)}) collective-permute-start(f32[43,32,128]{2,1,0:T(8,128)} %get-tuple-element.25), channel_id=1, source_target_pairs={{0,1},{1,0},{2,3},{3,2},{4,5},{5,4},{6,7},{7,6},{8,9},{9,8},{10,11... | collective-permute-start | bytes 2113544 | tf_op jit(solution)/shard_map/ppermute | solution.py:321
  8.4 1.2 %copy-done = f32[56,32,128]{2,1,0:T(8,128)S(1)} copy-done((f32[56,32,128]{2,1,0:T(8,128)S(1)}, f32[56,32,128]{2,1,0:T(8,128)}, u32[]{:S(2)}) %copy-start) | copy-done | bytes 917528
  9.7 7.8 %collective-permute-done.outer.f_outer = f32[43,32,128]{2,1,0:T(8,128)S(1)} collective-permute-done((f32[43,32,128]{2,1,0:T(8,128)}, f32[43,32,128]{2,1,0:T(8,128)S(1)}, u32[]{:S(2)}, u32[]{:S(2)}) %collective-permute-start) | collective-permute-done | bytes 704544 | tf_op jit(solution)/shard_map/ppermute | solution.py:318
  17.5 1.5 %shard_map.57 = (f32[8,32,128]{2,1,0:T(8,128)S(1)}, f32[8,32,128]{2,1,0:T(8,128)S(1)}, f32[7,18,32,128]{3,2,1,0:T(8,128)S(1)}) custom-call(f32[56,32,128]{2,1,0:T(8,128)S(1)} %shard_map.56.own, f32[43,32,128]{2,1,0:T(8,128)S(1)} %collective-permute-done.outer.f_outer, f32[43,32,128]{2,1,0:T(8,128)S(1)} %collective-permute-done.1.inner.f_inner), custom_call_target="tpu_custom_call" | custom-call | tf_op jit(solution)/shard_map/pallas_call | solution.py:336
  18.9 19.4 %all-gather = f32[32,32,128]{2,1,0:T(8,128)S(1)} all-gather(f32[8,32,128]{2,1,0:T(8,128)S(1)} %get-tuple-element.26), channel_id=2, replica_groups={{0,32,64,96},{128,160,192,224},{256,288,320,352},{384,416,448,480},{1,3..., dimensions={0}, use_global_device_ids=true | all-gather | bytes 655360 | tf_op jit(solution)/shard_map/all_gather | solution.py:339
  38.4 4.7 %collective-permute-start.2 = (f32[12,32,128]{2,1,0:T(8,128)S(1)}, f32[12,32,128]{2,1,0:T(8,128)S(1)}, u32[]{:S(2)}, u32[]{:S(2)}) collective-permute-start(f32[12,32,128]{2,1,0:T(8,128)S(1)} %get-tuple-element.27), channel_id=1, source_target_pairs={{1,2},{3,4},{5,6},{7,8},{9,10},{11,12},{13,14},{15,16},{17,18},{19... | collective-permute-start | bytes 589832 | tf_op jit(solution)/shard_map/ppermute | solution.py:318
  43.1 1.9 %collective-permute-start.3 = (f32[12,32,128]{2,1,0:T(8,128)S(1)}, f32[12,32,128]{2,1,0:T(8,128)S(1)}, u32[]{:S(2)}, u32[]{:S(2)}) collective-permute-start(f32[12,32,128]{2,1,0:T(8,128)S(1)} %get-tuple-element.28), channel_id=1, source_target_pairs={{0,1},{1,0},{2,3},{3,2},{4,5},{5,4},{6,7},{7,6},{8,9},{9,8},{10,11... | collective-permute-start | bytes 589832 | tf_op jit(solution)/shard_map/ppermute | solution.py:321
  45.4 2.1 %collective-permute-done.2.outer = f32[12,32,128]{2,1,0:T(8,128)S(1)} collective-permute-done((f32[12,32,128]{2,1,0:T(8,128)S(1)}, f32[12,32,128]{2,1,0:T(8,128)S(1)}, u32[]{:S(2)}, u32[]{:S(2)}) %collective-permute-start.2) | collective-permute-done | bytes 196640 | tf_op jit(solution)/shard_map/ppermute | solution.py:318
  47.5 1.0 %shard_map.60 = (f32[8,32,128]{2,1,0:T(8,128)S(1)}, f32[16,32,128]{2,1,0:T(8,128)S(1)}, f32[14,32,128]{2,1,0:T(8,128)S(1)}, f32[8,32,128]{2,1,0:T(8,128)S(1)}) custom-call(f32[4,8,32,128]{3,2,1,0:T(8,128)S(1)} %bitcast.3, f32[12,32,128]{2,1,0:T(8,128)S(1)} %collective-permute-done.2.outer, f32[12,32,128]{2,1,0:T(8,128)S(1)} %collective-permute-done.3.inner, ...), custom_call_target="tpu_custom_call" | custom-call | tf_op jit(solution)/shard_map/pallas_call | solution.py:342
  49.2 3.9 %collective-permute-start.6 = (f32[8,32,128]{2,1,0:T(8,128)S(1)}, f32[8,32,128]{2,1,0:T(8,128)S(1)}, u32[]{:S(2)}, u32[]{:S(2)}) collective-permute-start(f32[8,32,128]{2,1,0:T(8,128)S(1)} %get-tuple-element.31), channel_id=1, source_target_pairs={{0,32},{1,33},{2,34},{3,35},{4,36},{5,37},{6,38},{7,39},{8,40},{9,... | collective-permute-start | bytes 393224 | tf_op jit(solution)/shard_map/ppermute | solution.py:326
  53.8 1.3 %collective-permute-start.5 = (f32[8,32,128]{2,1,0:T(8,128)S(1)}, f32[8,32,128]{2,1,0:T(8,128)S(1)}, u32[]{:S(2)}, u32[]{:S(2)}) collective-permute-start(f32[8,32,128]{2,1,0:T(8,128)S(1)} %get-tuple-element.30), channel_id=1, source_target_pairs={{0,256},{1,257},{2,258},{3,259},{4,260},{5,261},{6,262},{7,263},{8... | collective-permute-start | bytes 393224 | tf_op jit(solution)/shard_map/ppermute | solution.py:326
  55.1 4.1 %collective-permute-start.10 = (f32[16,32,128]{2,1,0:T(8,128)S(1)}, f32[16,32,128]{2,1,0:T(8,128)S(1)}, u32[]{:S(2)}, u32[]{:S(2)}) collective-permute-start(f32[16,32,128]{2,1,0:T(8,128)S(1)} %get-tuple-element.34), channel_id=1, source_target_pairs={{0,128},{1,129},{2,130},{3,131},{4,132},{5,133},{6,134},{7,135},{8... | collective-permute-start | bytes 786440 | tf_op jit(solution)/shard_map/ppermute | solution.py:326
  59.2 2.0 %all-gather.1 = f32[16,32,128]{2,1,0:T(8,128)S(1)} all-gather(f32[8,32,128]{2,1,0:T(8,128)S(1)} %collective-permute-done.4.far), channel_id=3, replica_groups={{0,1},{2,3},{4,5},{6,7},{8,9},{10,11},{12,13},{14,15},{16,17},{18,19},{..., dimensions={0}, use_global_device_ids=true | all-gather | bytes 393216 | tf_op jit(solution)/shard_map/all_gather | solution.py:350
  61.2 5.4 %collective-permute-done.5.middle = f32[8,32,128]{2,1,0:T(8,128)S(1)} collective-permute-done((f32[8,32,128]{2,1,0:T(8,128)S(1)}, f32[8,32,128]{2,1,0:T(8,128)S(1)}, u32[]{:S(2)}, u32[]{:S(2)}) %collective-permute-start.5) | collective-permute-done | bytes 131104 | tf_op jit(solution)/shard_map/ppermute | solution.py:326
  66.9 1.9 %collective-permute-start.9 = (f32[14,32,128]{2,1,0:T(8,128)S(1)}, f32[14,32,128]{2,1,0:T(8,128)S(1)}, u32[]{:S(2)}, u32[]{:S(2)}) collective-permute-start(f32[14,32,128]{2,1,0:T(8,128)S(1)} %get-tuple-element.33), channel_id=1, source_target_pairs={{0,1},{1,0},{2,3},{3,2},{4,5},{5,4},{6,7},{7,6},{8,9},{9,8},{10,11... | collective-permute-start | bytes 688136 | tf_op jit(solution)/shard_map/ppermute | solution.py:321
  68.9 3.3 %collective-permute-start.8 = (f32[14,32,128]{2,1,0:T(8,128)S(1)}, f32[14,32,128]{2,1,0:T(8,128)S(1)}, u32[]{:S(2)}, u32[]{:S(2)}) collective-permute-start(f32[14,32,128]{2,1,0:T(8,128)S(1)} %get-tuple-element.32.held), channel_id=1, source_target_pairs={{1,2},{3,4},{5,6},{7,8},{9,10},{11,12},{13,14},{15,16},{17,18},{19... | collective-permute-start | bytes 688136 | tf_op jit(solution)/shard_map/ppermute | solution.py:318
  72.3 6.1 %collective-permute-done.8.outer = f32[14,32,128]{2,1,0:T(8,128)S(1)} collective-permute-done((f32[14,32,128]{2,1,0:T(8,128)S(1)}, f32[14,32,128]{2,1,0:T(8,128)S(1)}, u32[]{:S(2)}, u32[]{:S(2)}) %collective-permute-start.8) | collective-permute-done | bytes 229408 | tf_op jit(solution)/shard_map/ppermute | solution.py:318
  78.3 1.4 %shard_map.62 = (f32[16,32,128]{2,1,0:T(8,128)S(1)}, f32[15,32,128]{2,1,0:T(8,128)S(1)}, f32[15,32,128]{2,1,0:T(8,128)S(1)}) custom-call(f32[14,32,128]{2,1,0:T(8,128)S(1)} %get-tuple-element.32.held, f32[14,32,128]{2,1,0:T(8,128)S(1)} %collective-permute-done.8.outer, f32[14,32,128]{2,1,0:T(8,128)S(1)} %collective-permute-done.9.inner, ...), custom_call_target="tpu_custom_call" | custom-call | tf_op jit(solution)/shard_map/pallas_call | solution.py:354
  79.7 3.3 %collective-permute-start.11 = (f32[15,32,128]{2,1,0:T(8,128)S(1)}, f32[15,32,128]{2,1,0:T(8,128)S(1)}, u32[]{:S(2)}, u32[]{:S(2)}) collective-permute-start(f32[15,32,128]{2,1,0:T(8,128)S(1)} %get-tuple-element.37), channel_id=1, source_target_pairs={{1,2},{3,4},{5,6},{7,8},{9,10},{11,12},{13,14},{15,16},{17,18},{19... | collective-permute-start | bytes 737288 | tf_op jit(solution)/shard_map/ppermute | solution.py:318
  83.1 1.9 %collective-permute-start.12 = (f32[15,32,128]{2,1,0:T(8,128)S(1)}, f32[15,32,128]{2,1,0:T(8,128)S(1)}, u32[]{:S(2)}, u32[]{:S(2)}) collective-permute-start(f32[15,32,128]{2,1,0:T(8,128)S(1)} %get-tuple-element.38), channel_id=1, source_target_pairs={{0,1},{1,0},{2,3},{3,2},{4,5},{5,4},{6,7},{7,6},{8,9},{9,8},{10,11... | collective-permute-start | bytes 737288 | tf_op jit(solution)/shard_map/ppermute | solution.py:321
  85.0 4.3 %collective-permute-done.11.outer = f32[15,32,128]{2,1,0:T(8,128)S(1)} collective-permute-done((f32[15,32,128]{2,1,0:T(8,128)S(1)}, f32[15,32,128]{2,1,0:T(8,128)S(1)}, u32[]{:S(2)}, u32[]{:S(2)}) %collective-permute-start.11) | collective-permute-done | bytes 245792 | tf_op jit(solution)/shard_map/ppermute | solution.py:318
  89.4 2.2 %shard_map.63 = f32[4,8,32,128]{3,2,1,0:T(8,128)} custom-call(f32[16,32,128]{2,1,0:T(8,128)S(1)} %get-tuple-element.36.mine, f32[15,32,128]{2,1,0:T(8,128)S(1)} %collective-permute-done.11.outer, f32[15,32,128]{2,1,0:T(8,128)S(1)} %collective-permute-done.12.inner, f32[16,32,128]{2,1,0:T(8,128)S(1)} %collective-permute-done.10.relay, ...), custom_call_target="tpu_custom_call" | custom-call | tf_op jit(solution)/shard_map/pallas_call | solution.py:357
  (15 shorter events, 2.1 us)
Async XLA Ops:
  2.7 14.8 %collective-permute-start = (f32[43,32,128]{2,1,0:T(8,128)}, f32[43,32,128]{2,1,0:T(8,128)S(1)}, u32[]{:S(2)}, u32[]{:S(2)}) collective-permute-start(f32[43,32,128]{2,1,0:T(8,128)} %get-tuple-element.24), channel_id=1, source_target_pairs={{1,2},{3,4},{5,6},{7,8},{9,10},{11,12},{13,14},{15,16},{17,18},{19... | collective-permute-start | bytes 2113544 | tf_op jit(solution)/shard_map/ppermute | solution.py:318
  6.5 11.0 %collective-permute-start.1 = (f32[43,32,128]{2,1,0:T(8,128)}, f32[43,32,128]{2,1,0:T(8,128)S(1)}, u32[]{:S(2)}, u32[]{:S(2)}) collective-permute-start(f32[43,32,128]{2,1,0:T(8,128)} %get-tuple-element.25), channel_id=1, source_target_pairs={{0,1},{1,0},{2,3},{3,2},{4,5},{5,4},{6,7},{7,6},{8,9},{9,8},{10,11... | collective-permute-start | bytes 2113544 | tf_op jit(solution)/shard_map/ppermute | solution.py:321
  8.4 1.2 %copy-start = (f32[56,32,128]{2,1,0:T(8,128)S(1)}, f32[56,32,128]{2,1,0:T(8,128)}, u32[]{:S(2)}) copy-start(f32[56,32,128]{2,1,0:T(8,128)} %get-tuple-element.23.held) | copy-start | bytes 2752516
  38.4 9.1 %collective-permute-start.2 = (f32[12,32,128]{2,1,0:T(8,128)S(1)}, f32[12,32,128]{2,1,0:T(8,128)S(1)}, u32[]{:S(2)}, u32[]{:S(2)}) collective-permute-start(f32[12,32,128]{2,1,0:T(8,128)S(1)} %get-tuple-element.27), channel_id=1, source_target_pairs={{1,2},{3,4},{5,6},{7,8},{9,10},{11,12},{13,14},{15,16},{17,18},{19... | collective-permute-start | bytes 589832 | tf_op jit(solution)/shard_map/ppermute | solution.py:318
  43.1 4.4 %collective-permute-start.3 = (f32[12,32,128]{2,1,0:T(8,128)S(1)}, f32[12,32,128]{2,1,0:T(8,128)S(1)}, u32[]{:S(2)}, u32[]{:S(2)}) collective-permute-start(f32[12,32,128]{2,1,0:T(8,128)S(1)} %get-tuple-element.28), channel_id=1, source_target_pairs={{0,1},{1,0},{2,3},{3,2},{4,5},{5,4},{6,7},{7,6},{8,9},{9,8},{10,11... | collective-permute-start | bytes 589832 | tf_op jit(solution)/shard_map/ppermute | solution.py:321
  48.5 10.7 %collective-permute-start.4 = (f32[8,32,128]{2,1,0:T(8,128)S(1)}, f32[8,32,128]{2,1,0:T(8,128)S(1)}, u32[]{:S(2)}, u32[]{:S(2)}) collective-permute-start(f32[8,32,128]{2,1,0:T(8,128)S(1)} %get-tuple-element.30), channel_id=1, source_target_pairs={{0,384},{1,385},{2,386},{3,387},{4,388},{5,389},{6,390},{7,391},{8... | collective-permute-start | bytes 393224 | tf_op jit(solution)/shard_map/ppermute | solution.py:326
  49.2 12.0 %collective-permute-start.6 = (f32[8,32,128]{2,1,0:T(8,128)S(1)}, f32[8,32,128]{2,1,0:T(8,128)S(1)}, u32[]{:S(2)}, u32[]{:S(2)}) collective-permute-start(f32[8,32,128]{2,1,0:T(8,128)S(1)} %get-tuple-element.31), channel_id=1, source_target_pairs={{0,32},{1,33},{2,34},{3,35},{4,36},{5,37},{6,38},{7,39},{8,40},{9,... | collective-permute-start | bytes 393224 | tf_op jit(solution)/shard_map/ppermute | solution.py:326
  53.1 8.1 %collective-permute-start.7 = (f32[8,32,128]{2,1,0:T(8,128)S(1)}, f32[8,32,128]{2,1,0:T(8,128)S(1)}, u32[]{:S(2)}, u32[]{:S(2)}) collective-permute-start(f32[8,32,128]{2,1,0:T(8,128)S(1)} %get-tuple-element.30), channel_id=1, source_target_pairs={{1,386},{3,388},{5,390},{7,392},{9,394},{11,396},{13,398},{15,400}... | collective-permute-start | bytes 393224 | tf_op jit(solution)/shard_map/ppermute | solution.py:326
  53.8 12.8 %collective-permute-start.5 = (f32[8,32,128]{2,1,0:T(8,128)S(1)}, f32[8,32,128]{2,1,0:T(8,128)S(1)}, u32[]{:S(2)}, u32[]{:S(2)}) collective-permute-start(f32[8,32,128]{2,1,0:T(8,128)S(1)} %get-tuple-element.30), channel_id=1, source_target_pairs={{0,256},{1,257},{2,258},{3,259},{4,260},{5,261},{6,262},{7,263},{8... | collective-permute-start | bytes 393224 | tf_op jit(solution)/shard_map/ppermute | solution.py:326
  55.1 17.1 %collective-permute-start.10 = (f32[16,32,128]{2,1,0:T(8,128)S(1)}, f32[16,32,128]{2,1,0:T(8,128)S(1)}, u32[]{:S(2)}, u32[]{:S(2)}) collective-permute-start(f32[16,32,128]{2,1,0:T(8,128)S(1)} %get-tuple-element.34), channel_id=1, source_target_pairs={{0,128},{1,129},{2,130},{3,131},{4,132},{5,133},{6,134},{7,135},{8... | collective-permute-start | bytes 786440 | tf_op jit(solution)/shard_map/ppermute | solution.py:326
  66.9 5.3 %collective-permute-start.9 = (f32[14,32,128]{2,1,0:T(8,128)S(1)}, f32[14,32,128]{2,1,0:T(8,128)S(1)}, u32[]{:S(2)}, u32[]{:S(2)}) collective-permute-start(f32[14,32,128]{2,1,0:T(8,128)S(1)} %get-tuple-element.33), channel_id=1, source_target_pairs={{0,1},{1,0},{2,3},{3,2},{4,5},{5,4},{6,7},{7,6},{8,9},{9,8},{10,11... | collective-permute-start | bytes 688136 | tf_op jit(solution)/shard_map/ppermute | solution.py:321
  68.9 9.4 %collective-permute-start.8 = (f32[14,32,128]{2,1,0:T(8,128)S(1)}, f32[14,32,128]{2,1,0:T(8,128)S(1)}, u32[]{:S(2)}, u32[]{:S(2)}) collective-permute-start(f32[14,32,128]{2,1,0:T(8,128)S(1)} %get-tuple-element.32.held), channel_id=1, source_target_pairs={{1,2},{3,4},{5,6},{7,8},{9,10},{11,12},{13,14},{15,16},{17,18},{19... | collective-permute-start | bytes 688136 | tf_op jit(solution)/shard_map/ppermute | solution.py:318
  79.7 9.6 %collective-permute-start.11 = (f32[15,32,128]{2,1,0:T(8,128)S(1)}, f32[15,32,128]{2,1,0:T(8,128)S(1)}, u32[]{:S(2)}, u32[]{:S(2)}) collective-permute-start(f32[15,32,128]{2,1,0:T(8,128)S(1)} %get-tuple-element.37), channel_id=1, source_target_pairs={{1,2},{3,4},{5,6},{7,8},{9,10},{11,12},{13,14},{15,16},{17,18},{19... | collective-permute-start | bytes 737288 | tf_op jit(solution)/shard_map/ppermute | solution.py:318
  83.1 6.3 %collective-permute-start.12 = (f32[15,32,128]{2,1,0:T(8,128)S(1)}, f32[15,32,128]{2,1,0:T(8,128)S(1)}, u32[]{:S(2)}, u32[]{:S(2)}) collective-permute-start(f32[15,32,128]{2,1,0:T(8,128)S(1)} %get-tuple-element.38), channel_id=1, source_target_pairs={{0,1},{1,0},{2,3},{3,2},{4,5},{5,4},{6,7},{7,6},{8,9},{9,8},{10,11... | collective-permute-start | bytes 737288 | tf_op jit(solution)/shard_map/ppermute | solution.py:321

commit v3 on v2

--- a/solution.py
+++ b/solution.py
@@ -11,9 +11,9 @@
 L = 8
 NY, NX = 32, 128
 STEP = 0.3
-FINE_HALO = 5
+FINE_HALO = 6
 COARSE_HALO = 7
-SENT = (4, 6, 5, COARSE_HALO)
+SENT = (4, 7, 6, COARSE_HALO)
 FIRST = SENT[0] + SENT[1] + SENT[2] + 4 * COARSE_HALO
 VMEM = pltpu.VMEM
 
@@ -119,23 +119,24 @@
         if not 0 <= z < L:
             vz = -vz
         write_coefs(coef, z + FINE_HALO, get(3, z), vz, get(5, z), get(6, z), STEP)
-    for z in range(-6, L + 6):
-        y[z + 6] = get(1, z)
+    for z in range(-7, L + 7):
+        y[z + 7] = get(1, z)
     for z in range(-4, L + 4):
         c[z + 4] = get(0, z)
     for step in range(4):
-        halo = 5 - step
-        sweep(y, 6, coef, FINE_HALO, -halo, L + halo, lambda z, cur, new: new + get(2, z))
+        halo = 6 - step
+        sweep(y, 7, coef, FINE_HALO, -halo, L + halo, lambda z, cur, new: new + get(2, z))
         halo = 3 - step
         sweep(c, 4, coef, FINE_HALO, -halo, L + halo)
     for z in range(-2, L + 2):
-        b[z + 2] = y[z + 6] - get(0, z)
-    for z in range(L):
-        phi[z] = y[z + 6]
+        b[z + 2] = y[z + 7] - get(0, z)
+    for z in range(-3, L + 3):
+        phi[z + 3] = y[z + 7]
     for halo in (1, 0):
         sweep(b, 2, coef, FINE_HALO, -halo, L + halo, lambda z, cur, new: 2.0 * new - cur)
     for z in range(L):
         d[z] = c[z + 4] + b[z + 2]
+        phi[L + 6 + z] = d[z]
 
 
 def coarse_kernel(own, outer, inner, coef):
@@ -159,12 +160,10 @@
             at += 1
 
 
-def slab_kernel(g, outer, inner, coef, phi, total, relay, prefix, leaving, v):
+def slab_kernel(g, outer, inner, coef, total, partial, prefix, v):
     place = lax.axis_index("tm") % 4
     for z in range(-6, L + 6):
         v[z + 6] = ext(g.at[0], outer, inner, z)
-    for z in range(L):
-        leaving[z] = phi[z]
 
     def keep(wanted):
         @pl.when(place == wanted)
@@ -185,125 +184,119 @@
     coarse_twice(v, 6, coef, 4)
     for z in range(-2, L + 2):
         v[z + 6] += ext(g.at[2], outer, inner, z, 10, 10)
-
-    @pl.when(place == 0)
-    def _():
-        for z in range(L):
-            relay[z] = v[z + 6]
-
+    for z in range(L):
+        partial[z] = v[z + 6]
     coarse_twice(v, 6, coef, 2)
     for z in range(L):
         total[z] = v[z + 6] + g[3, z]
-        relay[L + z] = g[3, z]
-
-    @pl.when(place > 0)
-    def _():
-        for z in range(L):
-            relay[z] = total[z]
-
-
-def chain1_kernel(far, pair, middle, shifted, own, coef, far_outer, outer, inner, psi, u):
-    place = lax.axis_index("tm") % 4
+
+
+def arrived(block, outer, pair):
     other = 1 - lax.axis_index("space") % 2
-    for i in range(L):
-        u[L - 1 - i] = far_outer[i]
-        u[L + i] = far[i]
-        u[2 * L + i] = pair[other, L - 1 - i]
-        psi[i] = shifted[i] + own[L + i]
-    for i in range(4):
-        if i < 3:
-
-            @pl.when(place >= 3 - i)
-            def _():
-                coarse_twice(u, L, coef, 8 - 2 * i)
-        else:
+    return lambda z: outer[-1 - z] if z < 0 else pair[other, 2 * L - 1 - z] if z >= L else block[z]
+
+
+def chain1_kernel(block, outer, pair, total, partial, leaving, coef, to_next, opening, left, u):
+    here = lax.axis_index("tm") // 4 == 1
+    get = arrived(block, outer, pair)
+    for i in range(2 * L + 6):
+        left[i] = leaving[i]
+
+    @pl.when(here)
+    def _():
+        for z in range(-L, 2 * L):
+            u[L + z] = get(z)
+        for i in range(3):
+            coarse_twice(u, L, coef, 8 - 2 * i)
+        for z in range(L):
+            opening[z] = u[L + z] + partial[z]
+        coarse_twice(u, L, coef, 2)
+        for z in range(L):
+            to_next[z] = u[L + z] + total[z]
+
+    @pl.when(jnp.logical_not(here))
+    def _():
+        for z in range(L):
+            opening[z] = partial[z]
+            to_next[z] = total[z]
+
+
+def chain2_kernel(block, outer, pair, total, partial, opening, coef, to_next, u):
+    here = lax.axis_index("tm") // 4 == 2
+    leads = lax.axis_index("tm") % 4 == 0
+    get = arrived(block, outer, pair)
+
+    @pl.when(here)
+    def _():
+        for z in range(-L, 2 * L):
+            u[L + z] = get(z)
+        for i in range(3):
+            coarse_twice(u, L, coef, 8 - 2 * i)
+
+        @pl.when(leads)
+        def _():
+            for z in range(L):
+                to_next[z] = u[L + z] + partial[z]
+
+        @pl.when(jnp.logical_not(leads))
+        def _():
             coarse_twice(u, L, coef, 2)
+            for z in range(L):
+                to_next[z] = u[L + z] + total[z]
+
+    @pl.when(jnp.logical_not(here))
+    def _():
+        for z in range(L):
+            to_next[z] = opening[z]
+
+
+def finish_kernel(b1, o1, p1, b2, o2, p2, b3, o3, p3, before, prefix, phi, own, outer, inner, coef, fine, out, u, w):
+    group, place = lax.axis_index("tm") // 4, lax.axis_index("tm") % 4
+    first = lax.axis_index("tm") == 0
+    odd = lax.axis_index("space") % 2
+
+    def load(wanted, get):
+        @pl.when(wanted)
+        def _():
+            for z in range(-7, L + 7):
+                u[7 + z] = get(z)
+
+    last = jnp.logical_or(place == 0, jnp.logical_or(group == 0, group == 3))
+    load(last, arrived(b3, o3, p3))
+    load(jnp.logical_and(jnp.logical_not(last), group == 1), arrived(b1, o1, p1))
+    load(jnp.logical_and(jnp.logical_not(last), group == 2), arrived(b2, o2, p2))
 
     @pl.when(place == 3)
     def _():
-        for z in range(L):
-            u[L + z] += middle[z]
-
+        sweep(u, 7, coef, COARSE_HALO, -6, L + 6)
+        sweep(u, 7, coef, COARSE_HALO, -5, L + 5)
+
+    @pl.when(place >= 2)
+    def _():
+        sweep(u, 7, coef, COARSE_HALO, -4, L + 4)
+        sweep(u, 7, coef, COARSE_HALO, -3, L + 3)
+
+    for z in range(-3, L + 3):
+        w[3 + z] = u[7 + z] + prefix[3 + z]
+
+    @pl.when(first)
+    def _():
+        for z in range(-3, L + 3):
+            u[7 + z] = w[3 + z] + ext(own, outer, inner, z, SENT[0], SENT[0], L)
+
+    @pl.when(jnp.logical_not(first))
+    def _():
+        for z in range(-3, L + 3):
+            u[7 + z] = w[3 + z] + before[3 + z]
+
+    coarse_twice(w, 3, coef, 2)
     for z in range(L):
-        outer[z] = u[L + z]
-        inner[z] = u[L + L - 1 - z]
-    for i in range(6):
-        outer[L + i] = middle[i]
-        inner[L + i] = middle[L - 1 - i]
-
-
-def chain2_kernel(held, outer, inner, middle, relay, psi, coef, mine, to_outer, to_inner, u):
-    place = lax.axis_index("tm") % 4
-    for z in range(-L, 2 * L):
-        u[L + z] = ext(held, outer, inner, z)
-    for i in range(4):
-        halo = 6 - 2 * i
-        coarse_twice(u, L, coef, halo + 2)
-
-        @pl.when(place == (2 - i) % 4)
-        def _():
-            for z in range(-halo, L + halo):
-                u[L + z] += ext(relay, None, None, z) if i == 3 else ext(middle, outer, inner, z, L, L)
-
-    for z in range(L):
-        mine[z] = u[L + z]
-        mine[L + z] = psi[z]
-    for i in range(7):
-        to_outer[i] = u[L + i]
-        to_inner[i] = u[2 * L - 1 - i]
-    for i in range(5):
-        to_outer[7 + i] = relay[i]
-        to_inner[7 + i] = relay[L - 1 - i]
-    for i in range(3):
-        to_outer[12 + i] = mine[L + i]
-        to_inner[12 + i] = mine[2 * L - 1 - i]
-
-
-def finish_kernel(mine, outer, inner, relay, prefix, g, phi, own, f_outer, f_inner, coef, fine, out, u, w):
-    place = lax.axis_index("tm") % 4
-    odd = lax.axis_index("space") % 2
-    for z in range(-7, L + 7):
-        u[7 + z] = ext(mine, outer, inner, z)
-
-    def add_relay(halo):
-        for z in range(-halo, L + halo):
-            u[7 + z] += ext(relay, outer, inner, z, 7, 7)
-
-    sweep(u, 7, coef, COARSE_HALO, -6, L + 6)
-    sweep(u, 7, coef, COARSE_HALO, -5, L + 5)
-
-    @pl.when(place == 2)
-    def _():
-        add_relay(5)
-
-    sweep(u, 7, coef, COARSE_HALO, -4, L + 4)
-    sweep(u, 7, coef, COARSE_HALO, -3, L + 3)
-
-    @pl.when(place < 2)
-    def _():
-        add_relay(3)
-
-    for z in range(-3, L + 3):
-        g_t = u[7 + z] + prefix[3 + z]
-        w[3 + z] = g_t
-        u[7 + z] = g_t + ext(mine, outer, inner, z, 12, 12, L)
-    coarse_twice(w, 3, coef, 2)
-
-    @pl.when(place == 0)
-    def _():
-        for z in range(L):
-            out[3, z + odd * (L - 1 - 2 * z)] = w[3 + z] + phi[z] + relay[L + z]
-
-    @pl.when(place > 0)
-    def _():
-        for z in range(L):
-            out[3, z + odd * (L - 1 - 2 * z)] = w[3 + z] + phi[z] + g[place - 1, z]
-
+        out[3, z + odd * (L - 1 - 2 * z)] = w[3 + z] + before[L + 6 + z] + phi[3 + z]
     at = SENT[0] + SENT[1]
     for step in range(3):
         halo = 2 - step
         sweep(u, 7, fine, FINE_HALO, -halo, L + halo,
-              lambda z, cur, new: new + ext(own, f_outer, f_inner, z, at, at, 2 * L))
+              lambda z, cur, new: new + ext(own, outer, inner, z, at, at, 2 * L))
         for z in range(L):
             out[step, z + odd * (L - 1 - 2 * z)] = u[7 + z]
 
@@ -320,10 +313,15 @@
     def from_inner(x):
         return lax.ppermute(x, "space", paired)
 
-    def later(x, steps, moves=None):
+    def later(x, steps, moves=None, leaving=range(times)):
         moves = [(i, i) for i in range(count)] if moves is None else moves
-        pairs = [(t * count + a, (t + steps) * count + b) for t in range(times - steps) for a, b in moves]
+        pairs = [(t * count + a, (t + steps) * count + b) for t in leaving if t + steps < times for a, b in moves]
         return lax.ppermute(x, ("tm", "space"), pairs)
+
+    def hand_on(x, leaving):
+        block, outer = later(x, 4, None, leaving), later(x, 4, facing, leaving)
+        pair = lax.all_gather(block, "space", axis_index_groups=[[i, i + 1] for i in range(0, count, 2)])
+        return block, outer, pair
 
     own, outer, inner = pl.pallas_call(
         pack_kernel,
@@ -333,29 +331,20 @@
     )(guesses, forcing, initial, kappa, velocity)
     outer, inner = from_outer(outer), from_inner(inner)
     (own,) = call(settle_kernel, (7 * L,))(own)
-    d, phi, fine = call(local_kernel, (L, L, (7, L + 2 * FINE_HALO)), (L + 8, L + 12, L + 4))(own, outer, inner)
+    d, phi, fine = call(local_kernel, (L, 2 * L + 6, (7, L + 2 * FINE_HALO)), (L + 8, L + 14, L + 4))(own, outer, inner)
     (coef,) = call(coarse_kernel, ((7, L + 2 * COARSE_HALO),))(own, outer, inner)
-    groups = [[4 * a + b for b in range(4)] for a in range(times // 4)]
-    g = lax.all_gather(d, "tm", axis_index_groups=groups)
+    g = lax.all_gather(d, "tm", axis_index_groups=[[4 * a + b for b in range(4)] for a in range(times // 4)])
     slab_outer, slab_inner = call(slab_pack_kernel, (12, 12))(g)
     slab_outer, slab_inner = from_outer(slab_outer), from_inner(slab_inner)
-    total, relay, prefix, leaving = call(slab_kernel, (L, 2 * L, L + 6, L), (L + 12,))(
-        g, slab_outer, slab_inner, coef, phi
-    )
-    shifted = later(leaving, 1)
-    relay = later(relay, 4)
-    middle = later(total, 8)
-    far_outer = later(total, 12, facing)
-    far = later(total, 12)
-    pair = lax.all_gather(far, "space", axis_index_groups=[[i, i + 1] for i in range(0, count, 2)])
-    c1_outer, c1_inner, psi = call(chain1_kernel, (L + 6, L + 6, L), (3 * L,))(
-        far, pair, middle, shifted, own, coef, far_outer
-    )
-    mine, c2_outer, c2_inner = call(chain2_kernel, (2 * L, 15, 15), (3 * L,))(
-        c1_outer, from_outer(c1_outer), from_inner(c1_inner), middle, relay, psi, coef
-    )
+    total, partial, prefix = call(slab_kernel, (L, L, L + 6), (L + 12,))(g, slab_outer, slab_inner, coef)
+    one = hand_on(total, range(4))
+    to_two, opening, left = call(chain1_kernel, (L, L, 2 * L + 6), (3 * L,))(*one, total, partial, phi, coef)
+    before = later(left, 1)
+    two = hand_on(to_two, range(4, 8))
+    (to_three,) = call(chain2_kernel, (L,), (3 * L,))(*two, total, partial, opening, coef)
+    three = hand_on(to_three, (0, 4, 8, 9, 10, 11))
     (out,) = call(finish_kernel, ((4, L),), (L + 14, L + 6))(
-        mine, from_outer(c2_outer), from_inner(c2_inner), relay, prefix, g, phi, own, outer, inner, coef, fine
+        *one, *two, *three, before, prefix, phi, own, outer, inner, coef, fine
     )
     return out
 

time: 92 us -> 93.2 us (1.013)
  the two profiles are of different devices: /device:TPU:61 before, /device:TPU:115 now
where the time goes in v3:
time: 93.2 us; the launch traced here: 92.8 us
  blocking collectives  31.9 us (34%)
  waiting for transfers between devices  26.7 us (29%)
  starting transfers between devices  24.7 us (27%)
  Pallas kernels  8.2 us (9%)
  local copies, waits for them, and re-layouts  1.17 us (1%)
    all_gather x1, blocking collectives, body(): lax.all_gather(d, 'tm', axis_index_groups=[[4 * a + b for b in range(4)]...  21.6 us
    ppermute x7, waiting for transfers between devices, later(): return lax.ppermute(x, ('tm', 'space'), pairs)  18.6 us
    ppermute x7, starting transfers between devices, later(): return lax.ppermute(x, ('tm', 'space'), pairs)  14.1 us
    all_gather x3, blocking collectives, hand_on(): lax.all_gather(block, 'space', axis_index_groups=[[i, i + 1] for i in ran...  10.2 us
    ppermute x2, waiting for transfers between devices, from_outer(): return lax.ppermute(x, 'space', facing)  8.1 us
    ppermute x2, starting transfers between devices, from_outer(): return lax.ppermute(x, 'space', facing)  5.41 us
    ppermute x2, starting transfers between devices, from_inner(): return lax.ppermute(x, 'space', paired)  5.15 us
    pallas_call x1, Pallas kernels, body(): pl.pallas_call(pack_kernel, out_shape=[jax.ShapeDtypeStruct((n, NY, NX),...  2.7 us
  transfers between devices with their start and end apart: 11, of which 6 were waited for; matrix products, arithmetic and copies ran while one was open for 0% of the time, Pallas kernels for 0%

profile of v3, /device:TPU:115, one launch (start us, length us, event | category | flops | bytes accessed | tf_op | source)
XLA Modules:
  0.0 92.8 jit_solution(2110468024726188642)
XLA Ops:
  0.0 2.7 %shard_map.55 = (f32[56,32,128]{2,1,0:T(8,128)}, f32[45,32,128]{2,1,0:T(8,128)}, f32[45,32,128]{2,1,0:T(8,128)}) custom-call(f32[1,8,32,128]{3,2,1,0:T(8,128)} %guesses.1, f32[1,8,32,128]{3,2,1,0:T(8,128)} %forcing.1, f32[8,32,128]{2,1,0:T(8,128)} %initial.1, f32[8,32,128]{2,1,0:T(8,128)} %kappa.1, f32[3,8,32,128]{3,2,1,0:T(8,128)} %velocity.1), custom_call_target="tpu_custom_call" | custom-call | tf_op jit(solution)/shard_map/pallas_call | solution.py:326
  2.7 2.9 %collective-permute-start = (f32[45,32,128]{2,1,0:T(8,128)}, f32[45,32,128]{2,1,0:T(8,128)S(1)}, u32[]{:S(2)}, u32[]{:S(2)}) collective-permute-start(f32[45,32,128]{2,1,0:T(8,128)} %get-tuple-element.20), channel_id=1, source_target_pairs={{1,2},{3,4},{5,6},{7,8},{9,10},{11,12},{13,14},{15,16},{17,18},{19... | collective-permute-start | bytes 2211848 | tf_op jit(solution)/shard_map/ppermute | solution.py:311
  5.6 2.4 %collective-permute-start.1 = (f32[45,32,128]{2,1,0:T(8,128)}, f32[45,32,128]{2,1,0:T(8,128)S(1)}, u32[]{:S(2)}, u32[]{:S(2)}) collective-permute-start(f32[45,32,128]{2,1,0:T(8,128)} %get-tuple-element.21), channel_id=1, source_target_pairs={{0,1},{1,0},{2,3},{3,2},{4,5},{5,4},{6,7},{7,6},{8,9},{9,8},{10,11... | collective-permute-start | bytes 2211848 | tf_op jit(solution)/shard_map/ppermute | solution.py:314
  9.3 6.7 %collective-permute-done.outer = f32[45,32,128]{2,1,0:T(8,128)S(1)} collective-permute-done((f32[45,32,128]{2,1,0:T(8,128)}, f32[45,32,128]{2,1,0:T(8,128)S(1)}, u32[]{:S(2)}, u32[]{:S(2)}) %collective-permute-start) | collective-permute-done | bytes 737312 | tf_op jit(solution)/shard_map/ppermute | solution.py:311
  16.0 1.6 %shard_map.57 = (f32[8,32,128]{2,1,0:T(8,128)S(1)}, f32[22,32,128]{2,1,0:T(8,128)S(1)}, f32[7,20,32,128]{3,2,1,0:T(8,128)S(1)}) custom-call(f32[56,32,128]{2,1,0:T(8,128)S(1)} %shard_map.56.own, f32[45,32,128]{2,1,0:T(8,128)S(1)} %collective-permute-done.outer, f32[45,32,128]{2,1,0:T(8,128)S(1)} %collective-permute-done.1.inner), custom_call_target="tpu_custom_call" | custom-call | tf_op jit(solution)/shard_map/pallas_call | solution.py:334
  17.6 21.6 %all-gather = f32[32,32,128]{2,1,0:T(8,128)S(1)} all-gather(f32[8,32,128]{2,1,0:T(8,128)S(1)} %get-tuple-element.22), channel_id=2, replica_groups={{0,32,64,96},{128,160,192,224},{256,288,320,352},{384,416,448,480},{1,3..., dimensions={0}, use_global_device_ids=true | all-gather | bytes 655360 | tf_op jit(solution)/shard_map/all_gather | solution.py:336
  39.2 2.5 %collective-permute-start.2 = (f32[12,32,128]{2,1,0:T(8,128)S(1)}, f32[12,32,128]{2,1,0:T(8,128)S(1)}, u32[]{:S(2)}, u32[]{:S(2)}) collective-permute-start(f32[12,32,128]{2,1,0:T(8,128)S(1)} %get-tuple-element.23), channel_id=1, source_target_pairs={{1,2},{3,4},{5,6},{7,8},{9,10},{11,12},{13,14},{15,16},{17,18},{19... | collective-permute-start | bytes 589832 | tf_op jit(solution)/shard_map/ppermute | solution.py:311
  41.8 2.7 %collective-permute-start.3 = (f32[12,32,128]{2,1,0:T(8,128)S(1)}, f32[12,32,128]{2,1,0:T(8,128)S(1)}, u32[]{:S(2)}, u32[]{:S(2)}) collective-permute-start(f32[12,32,128]{2,1,0:T(8,128)S(1)} %get-tuple-element.24), channel_id=1, source_target_pairs={{0,1},{1,0},{2,3},{3,2},{4,5},{5,4},{6,7},{7,6},{8,9},{9,8},{10,11... | collective-permute-start | bytes 589832 | tf_op jit(solution)/shard_map/ppermute | solution.py:314
  44.9 1.4 %collective-permute-done.2.outer = f32[12,32,128]{2,1,0:T(8,128)S(1)} collective-permute-done((f32[12,32,128]{2,1,0:T(8,128)S(1)}, f32[12,32,128]{2,1,0:T(8,128)S(1)}, u32[]{:S(2)}, u32[]{:S(2)}) %collective-permute-start.2) | collective-permute-done | bytes 196640 | tf_op jit(solution)/shard_map/ppermute | solution.py:311
  47.1 1.3 %collective-permute-start.4 = (f32[8,32,128]{2,1,0:T(8,128)S(1)}, f32[8,32,128]{2,1,0:T(8,128)S(1)}, u32[]{:S(2)}, u32[]{:S(2)}) collective-permute-start(f32[8,32,128]{2,1,0:T(8,128)S(1)} %get-tuple-element.25.total), channel_id=1, source_target_pairs={{0,128},{1,129},{2,130},{3,131},{4,132},{5,133},{6,134},{7,135},{8... | collective-permute-start | bytes 393224 | tf_op jit(solution)/shard_map/ppermute | solution.py:319
  48.4 1.3 %collective-permute-start.5 = (f32[8,32,128]{2,1,0:T(8,128)S(1)}, f32[8,32,128]{2,1,0:T(8,128)S(1)}, u32[]{:S(2)}, u32[]{:S(2)}) collective-permute-start(f32[8,32,128]{2,1,0:T(8,128)S(1)} %get-tuple-element.25.total), channel_id=1, source_target_pairs={{1,130},{3,132},{5,134},{7,136},{9,138},{11,140},{13,142},{15,144}... | collective-permute-start | bytes 393224 | tf_op jit(solution)/shard_map/ppermute | solution.py:319
  49.7 4.0 %collective-permute-done.4.block.b1 = f32[8,32,128]{2,1,0:T(8,128)S(1)} collective-permute-done((f32[8,32,128]{2,1,0:T(8,128)S(1)}, f32[8,32,128]{2,1,0:T(8,128)S(1)}, u32[]{:S(2)}, u32[]{:S(2)}) %collective-permute-start.4) | collective-permute-done | bytes 131104 | tf_op jit(solution)/shard_map/ppermute | solution.py:319
  53.7 5.7 %all-gather.1 = f32[16,32,128]{2,1,0:T(8,128)S(1)} all-gather(f32[8,32,128]{2,1,0:T(8,128)S(1)} %collective-permute-done.4.block.b1), channel_id=3, replica_groups={{0,1},{2,3},{4,5},{6,7},{8,9},{10,11},{12,13},{14,15},{16,17},{18,19},{..., dimensions={0}, use_global_device_ids=true | all-gather | bytes 393216 | tf_op jit(solution)/shard_map/all_gather | solution.py:323
  60.6 1.3 %collective-permute-start.6 = (f32[8,32,128]{2,1,0:T(8,128)S(1)}, f32[8,32,128]{2,1,0:T(8,128)S(1)}, u32[]{:S(2)}, u32[]{:S(2)}) collective-permute-start(f32[8,32,128]{2,1,0:T(8,128)S(1)} %get-tuple-element.28), channel_id=1, source_target_pairs={{128,256},{129,257},{130,258},{131,259},{132,260},{133,261},{134,2... | collective-permute-start | bytes 393224 | tf_op jit(solution)/shard_map/ppermute | solution.py:319
  61.9 1.9 %collective-permute-start.10 = (f32[22,32,128]{2,1,0:T(8,128)S(1)}, f32[22,32,128]{2,1,0:T(8,128)S(1)}, u32[]{:S(2)}, u32[]{:S(2)}) collective-permute-start(f32[22,32,128]{2,1,0:T(8,128)S(1)} %get-tuple-element.30), channel_id=1, source_target_pairs={{0,32},{1,33},{2,34},{3,35},{4,36},{5,37},{6,38},{7,39},{8,40},{9,... | collective-permute-start | bytes 1081352 | tf_op jit(solution)/shard_map/ppermute | solution.py:319
  63.8 1.3 %collective-permute-start.7 = (f32[8,32,128]{2,1,0:T(8,128)S(1)}, f32[8,32,128]{2,1,0:T(8,128)S(1)}, u32[]{:S(2)}, u32[]{:S(2)}) collective-permute-start(f32[8,32,128]{2,1,0:T(8,128)S(1)} %get-tuple-element.28), channel_id=1, source_target_pairs={{129,258},{131,260},{133,262},{135,264},{137,266},{139,268},{141,2... | collective-permute-start | bytes 393224 | tf_op jit(solution)/shard_map/ppermute | solution.py:319
  65.1 10.1 %collective-permute-done.6.block.b2 = f32[8,32,128]{2,1,0:T(8,128)S(1)} collective-permute-done((f32[8,32,128]{2,1,0:T(8,128)S(1)}, f32[8,32,128]{2,1,0:T(8,128)S(1)}, u32[]{:S(2)}, u32[]{:S(2)}) %collective-permute-start.6) | collective-permute-done | bytes 131104 | tf_op jit(solution)/shard_map/ppermute | solution.py:319
  75.2 2.5 %all-gather.2 = f32[16,32,128]{2,1,0:T(8,128)S(1)} all-gather(f32[8,32,128]{2,1,0:T(8,128)S(1)} %collective-permute-done.6.block.b2), channel_id=4, replica_groups={{0,1},{2,3},{4,5},{6,7},{8,9},{10,11},{12,13},{14,15},{16,17},{18,19},{..., dimensions={0}, use_global_device_ids=true | all-gather | bytes 393216 | tf_op jit(solution)/shard_map/all_gather | solution.py:323
  77.7 5.1 %collective-permute-start.8 = (f32[8,32,128]{2,1,0:T(8,128)S(1)}, f32[8,32,128]{2,1,0:T(8,128)S(1)}, u32[]{:S(2)}, u32[]{:S(2)}) collective-permute-start(f32[8,32,128]{2,1,0:T(8,128)S(1)} %shard_map.62), channel_id=1, source_target_pairs={{0,128},{1,129},{2,130},{3,131},{4,132},{5,133},{6,134},{7,135},{8... | collective-permute-start | bytes 393224 | tf_op jit(solution)/shard_map/ppermute | solution.py:319
  82.8 1.9 %collective-permute-start.9 = (f32[8,32,128]{2,1,0:T(8,128)S(1)}, f32[8,32,128]{2,1,0:T(8,128)S(1)}, u32[]{:S(2)}, u32[]{:S(2)}) collective-permute-start(f32[8,32,128]{2,1,0:T(8,128)S(1)} %shard_map.62), channel_id=1, source_target_pairs={{1,130},{3,132},{5,134},{7,136},{9,138},{11,140},{13,142},{15,144}... | collective-permute-start | bytes 393224 | tf_op jit(solution)/shard_map/ppermute | solution.py:319
  84.7 2.9 %collective-permute-done.8.b3 = f32[8,32,128]{2,1,0:T(8,128)S(1)} collective-permute-done((f32[8,32,128]{2,1,0:T(8,128)S(1)}, f32[8,32,128]{2,1,0:T(8,128)S(1)}, u32[]{:S(2)}, u32[]{:S(2)}) %collective-permute-start.8) | collective-permute-done | bytes 131104 | tf_op jit(solution)/shard_map/ppermute | solution.py:319
  87.6 2.1 %all-gather.3 = f32[16,32,128]{2,1,0:T(8,128)S(1)} all-gather(f32[8,32,128]{2,1,0:T(8,128)S(1)} %collective-permute-done.8.b3), channel_id=5, replica_groups={{0,1},{2,3},{4,5},{6,7},{8,9},{10,11},{12,13},{14,15},{16,17},{18,19},{..., dimensions={0}, use_global_device_ids=true | all-gather | bytes 393216 | tf_op jit(solution)/shard_map/all_gather | solution.py:323
  89.7 1.7 %collective-permute-done.9.o3 = f32[8,32,128]{2,1,0:T(8,128)S(1)} collective-permute-done((f32[8,32,128]{2,1,0:T(8,128)S(1)}, f32[8,32,128]{2,1,0:T(8,128)S(1)}, u32[]{:S(2)}, u32[]{:S(2)}) %collective-permute-start.9) | collective-permute-done | bytes 131104 | tf_op jit(solution)/shard_map/ppermute | solution.py:319
  91.4 1.4 %shard_map.63 = f32[4,8,32,128]{3,2,1,0:T(8,128)} custom-call(f32[8,32,128]{2,1,0:T(8,128)S(1)} %collective-permute-done.4.block.b1, f32[8,32,128]{2,1,0:T(8,128)S(1)} %collective-permute-done.5.outer.o1, f32[2,8,32,128]{3,2,1,0:T(8,128)S(1)} %bitcast.7, f32[8,32,128]{2,1,0:T(8,128)S(1)} %collective-permute-done.6.block.b2, ...), custom_call_target="tpu_custom_call" | custom-call | tf_op jit(solution)/shard_map/pallas_call | solution.py:346
  (13 shorter events, 3.7 us)
Async XLA Ops:
  2.7 13.3 %collective-permute-start = (f32[45,32,128]{2,1,0:T(8,128)}, f32[45,32,128]{2,1,0:T(8,128)S(1)}, u32[]{:S(2)}, u32[]{:S(2)}) collective-permute-start(f32[45,32,128]{2,1,0:T(8,128)} %get-tuple-element.20), channel_id=1, source_target_pairs={{1,2},{3,4},{5,6},{7,8},{9,10},{11,12},{13,14},{15,16},{17,18},{19... | collective-permute-start | bytes 2211848 | tf_op jit(solution)/shard_map/ppermute | solution.py:311
  5.6 10.4 %collective-permute-start.1 = (f32[45,32,128]{2,1,0:T(8,128)}, f32[45,32,128]{2,1,0:T(8,128)S(1)}, u32[]{:S(2)}, u32[]{:S(2)}) collective-permute-start(f32[45,32,128]{2,1,0:T(8,128)} %get-tuple-element.21), channel_id=1, source_target_pairs={{0,1},{1,0},{2,3},{3,2},{4,5},{5,4},{6,7},{7,6},{8,9},{9,8},{10,11... | collective-permute-start | bytes 2211848 | tf_op jit(solution)/shard_map/ppermute | solution.py:314
  8.0 1.2 %copy-start = (f32[56,32,128]{2,1,0:T(8,128)S(1)}, f32[56,32,128]{2,1,0:T(8,128)}, u32[]{:S(2)}) copy-start(f32[56,32,128]{2,1,0:T(8,128)} %get-tuple-element.19.held) | copy-start | bytes 2752516
  39.2 7.0 %collective-permute-start.2 = (f32[12,32,128]{2,1,0:T(8,128)S(1)}, f32[12,32,128]{2,1,0:T(8,128)S(1)}, u32[]{:S(2)}, u32[]{:S(2)}) collective-permute-start(f32[12,32,128]{2,1,0:T(8,128)S(1)} %get-tuple-element.23), channel_id=1, source_target_pairs={{1,2},{3,4},{5,6},{7,8},{9,10},{11,12},{13,14},{15,16},{17,18},{19... | collective-permute-start | bytes 589832 | tf_op jit(solution)/shard_map/ppermute | solution.py:311
  41.8 4.4 %collective-permute-start.3 = (f32[12,32,128]{2,1,0:T(8,128)S(1)}, f32[12,32,128]{2,1,0:T(8,128)S(1)}, u32[]{:S(2)}, u32[]{:S(2)}) collective-permute-start(f32[12,32,128]{2,1,0:T(8,128)S(1)} %get-tuple-element.24), channel_id=1, source_target_pairs={{0,1},{1,0},{2,3},{3,2},{4,5},{5,4},{6,7},{7,6},{8,9},{9,8},{10,11... | collective-permute-start | bytes 589832 | tf_op jit(solution)/shard_map/ppermute | solution.py:314
  47.1 6.6 %collective-permute-start.4 = (f32[8,32,128]{2,1,0:T(8,128)S(1)}, f32[8,32,128]{2,1,0:T(8,128)S(1)}, u32[]{:S(2)}, u32[]{:S(2)}) collective-permute-start(f32[8,32,128]{2,1,0:T(8,128)S(1)} %get-tuple-element.25.total), channel_id=1, source_target_pairs={{0,128},{1,129},{2,130},{3,131},{4,132},{5,133},{6,134},{7,135},{8... | collective-permute-start | bytes 393224 | tf_op jit(solution)/shard_map/ppermute | solution.py:319
  48.4 10.9 %collective-permute-start.5 = (f32[8,32,128]{2,1,0:T(8,128)S(1)}, f32[8,32,128]{2,1,0:T(8,128)S(1)}, u32[]{:S(2)}, u32[]{:S(2)}) collective-permute-start(f32[8,32,128]{2,1,0:T(8,128)S(1)} %get-tuple-element.25.total), channel_id=1, source_target_pairs={{1,130},{3,132},{5,134},{7,136},{9,138},{11,140},{13,142},{15,144}... | collective-permute-start | bytes 393224 | tf_op jit(solution)/shard_map/ppermute | solution.py:319
  60.6 14.7 %collective-permute-start.6 = (f32[8,32,128]{2,1,0:T(8,128)S(1)}, f32[8,32,128]{2,1,0:T(8,128)S(1)}, u32[]{:S(2)}, u32[]{:S(2)}) collective-permute-start(f32[8,32,128]{2,1,0:T(8,128)S(1)} %get-tuple-element.28), channel_id=1, source_target_pairs={{128,256},{129,257},{130,258},{131,259},{132,260},{133,261},{134,2... | collective-permute-start | bytes 393224 | tf_op jit(solution)/shard_map/ppermute | solution.py:319
  61.9 29.5 %collective-permute-start.10 = (f32[22,32,128]{2,1,0:T(8,128)S(1)}, f32[22,32,128]{2,1,0:T(8,128)S(1)}, u32[]{:S(2)}, u32[]{:S(2)}) collective-permute-start(f32[22,32,128]{2,1,0:T(8,128)S(1)} %get-tuple-element.30), channel_id=1, source_target_pairs={{0,32},{1,33},{2,34},{3,35},{4,36},{5,37},{6,38},{7,39},{8,40},{9,... | collective-permute-start | bytes 1081352 | tf_op jit(solution)/shard_map/ppermute | solution.py:319
  63.8 13.9 %collective-permute-start.7 = (f32[8,32,128]{2,1,0:T(8,128)S(1)}, f32[8,32,128]{2,1,0:T(8,128)S(1)}, u32[]{:S(2)}, u32[]{:S(2)}) collective-permute-start(f32[8,32,128]{2,1,0:T(8,128)S(1)} %get-tuple-element.28), channel_id=1, source_target_pairs={{129,258},{131,260},{133,262},{135,264},{137,266},{139,268},{141,2... | collective-permute-start | bytes 393224 | tf_op jit(solution)/shard_map/ppermute | solution.py:319
  77.7 9.9 %collective-permute-start.8 = (f32[8,32,128]{2,1,0:T(8,128)S(1)}, f32[8,32,128]{2,1,0:T(8,128)S(1)}, u32[]{:S(2)}, u32[]{:S(2)}) collective-permute-start(f32[8,32,128]{2,1,0:T(8,128)S(1)} %shard_map.62), channel_id=1, source_target_pairs={{0,128},{1,129},{2,130},{3,131},{4,132},{5,133},{6,134},{7,135},{8... | collective-permute-start | bytes 393224 | tf_op jit(solution)/shard_map/ppermute | solution.py:319
  82.8 8.5 %collective-permute-start.9 = (f32[8,32,128]{2,1,0:T(8,128)S(1)}, f32[8,32,128]{2,1,0:T(8,128)S(1)}, u32[]{:S(2)}, u32[]{:S(2)}) collective-permute-start(f32[8,32,128]{2,1,0:T(8,128)S(1)} %shard_map.62), channel_id=1, source_target_pairs={{1,130},{3,132},{5,134},{7,136},{9,138},{11,140},{13,142},{15,144}... | collective-permute-start | bytes 393224 | tf_op jit(solution)/shard_map/ppermute | solution.py:319

commit v4 on v3

--- a/solution.py
+++ b/solution.py
@@ -13,8 +13,10 @@
 STEP = 0.3
 FINE_HALO = 6
 COARSE_HALO = 7
-SENT = (4, 7, 6, COARSE_HALO)
-FIRST = SENT[0] + SENT[1] + SENT[2] + 4 * COARSE_HALO
+SENT = (4, 6, COARSE_HALO)
+COEFS = SENT[0] + SENT[1]
+FIRST = COEFS + 4 * COARSE_HALO
+OPEN = 7
 VMEM = pltpu.VMEM
 
 
@@ -79,27 +81,37 @@
     out[6, index] = 1.0 - (above_z + below_z + above_y + below_y + above_x + below_x)
 
 
-def pack_kernel(guesses, forcing, initial, kappa, velocity, own, outer, inner, held, sems):
+def pack_kernel(
+    guesses, forcing, kappa, velocity, initial, own, outer, inner, open_outer, open_inner, held, kept, low, high, sems, out_sems
+):
     odd = lax.axis_index("space") % 2
     first = (lax.axis_index("tm") == 0).astype(jnp.float32)
-    sign = (1 - 2 * odd).astype(jnp.float32)
-    sources = (guesses.at[0], initial, forcing.at[0], kappa, velocity.at[0], velocity.at[1], velocity.at[2])
+    scale = (None, STEP, None, (1 - 2 * odd).astype(jnp.float32), None, None, first)
+    sources = (guesses.at[0], forcing.at[0], kappa, velocity.at[0], velocity.at[1], velocity.at[2], initial)
     copies = [pltpu.make_async_copy(source, held.at[k], sems.at[k]) for k, source in enumerate(sources)]
     for copy in copies:
         copy.start()
-    at = 0
+    leaving, at = [], 0
     for field, copy in enumerate(copies):
         copy.wait()
         for z in range(L):
             value = held[field, z + odd * (L - 1 - 2 * z)]
-            if field in (1, 2, 4):
-                value = (None, first, STEP, None, sign)[field] * value
-            own[field * L + z] = value
-        count = SENT[min(field, 3)]
+            kept[field * L + z] = value if scale[field] is None else scale[field] * value
+        count = SENT[min(field, 2)] if field < 6 else OPEN
         for i in range(count):
-            outer[at + i] = own[field * L + i]
-            inner[at + i] = own[field * L + L - 1 - i]
+            low[at + i] = kept[field * L + i]
+            high[at + i] = kept[field * L + L - 1 - i]
+        spots, block = pl.ds(at, count), pl.ds(field * L, L)
+        for k, (source, to) in enumerate((
+            (low.at[spots], outer.at[spots] if field < 6 else open_outer),
+            (high.at[spots], inner.at[spots] if field < 6 else open_inner),
+            (kept.at[block], own.at[block]),
+        )):
+            leaving.append(pltpu.make_async_copy(source, to, out_sems.at[3 * field + k]))
+            leaving[-1].start()
         at += count
+    for copy in leaving:
+        copy.wait()
 
 
 def settle_kernel(held, own):
@@ -107,25 +119,25 @@
         own[i] = held[i]
 
 
-def local_kernel(own, outer, inner, d, phi, coef, c, y, b):
-    starts = (0, SENT[0], SENT[0] + SENT[1], SENT[0] + SENT[1] + SENT[2])
-
+def local_kernel(own, outer, inner, open_outer, open_inner, d, phi, coef, c, y, b):
     def get(field, z):
-        at = starts[min(field, 3)] + max(field - 3, 0) * COARSE_HALO
+        if field == 6:
+            return ext(own, open_outer, open_inner, z, 0, 0, 6 * L)
+        at = (0, SENT[0], *range(COEFS, FIRST, COARSE_HALO))[field]
         return ext(own, outer, inner, z, at, at, field * L)
 
     for z in range(-FINE_HALO, L + FINE_HALO):
-        vz = get(4, z)
+        vz = get(3, z)
         if not 0 <= z < L:
             vz = -vz
-        write_coefs(coef, z + FINE_HALO, get(3, z), vz, get(5, z), get(6, z), STEP)
+        write_coefs(coef, z + FINE_HALO, get(2, z), vz, get(4, z), get(5, z), STEP)
     for z in range(-7, L + 7):
-        y[z + 7] = get(1, z)
+        y[z + 7] = get(6, z)
     for z in range(-4, L + 4):
         c[z + 4] = get(0, z)
     for step in range(4):
         halo = 6 - step
-        sweep(y, 7, coef, FINE_HALO, -halo, L + halo, lambda z, cur, new: new + get(2, z))
+        sweep(y, 7, coef, FINE_HALO, -halo, L + halo, lambda z, cur, new: new + get(1, z))
         halo = 3 - step
         sweep(c, 4, coef, FINE_HALO, -halo, L + halo)
     for z in range(-2, L + 2):
@@ -136,13 +148,12 @@
         sweep(b, 2, coef, FINE_HALO, -halo, L + halo, lambda z, cur, new: 2.0 * new - cur)
     for z in range(L):
         d[z] = c[z + 4] + b[z + 2]
-        phi[L + 6 + z] = d[z]
 
 
 def coarse_kernel(own, outer, inner, coef):
     def get(k, z):
-        at = FIRST - (4 - k) * COARSE_HALO
-        return ext(own, outer, inner, z, at, at, (3 + k) * L)
+        at = COEFS + k * COARSE_HALO
+        return ext(own, outer, inner, z, at, at, (2 + k) * L)
 
     for z in range(-COARSE_HALO, L + COARSE_HALO):
         vz = get(1, z)
@@ -196,11 +207,14 @@
     return lambda z: outer[-1 - z] if z < 0 else pair[other, 2 * L - 1 - z] if z >= L else block[z]
 
 
-def chain1_kernel(block, outer, pair, total, partial, leaving, coef, to_next, opening, left, u):
+def leave_kernel(phi, total, leaving):
+    for i in range(L + 6):
+        leaving[i] = phi[i]
+
+
+def chain1_kernel(block, outer, pair, total, partial, d, coef, opening, send, u):
     here = lax.axis_index("tm") // 4 == 1
     get = arrived(block, outer, pair)
-    for i in range(2 * L + 6):
-        left[i] = leaving[i]
 
     @pl.when(here)
     def _():
@@ -212,18 +226,22 @@
             opening[z] = u[L + z] + partial[z]
         coarse_twice(u, L, coef, 2)
         for z in range(L):
-            to_next[z] = u[L + z] + total[z]
+            send[z] = u[L + z] + total[z]
 
     @pl.when(jnp.logical_not(here))
     def _():
         for z in range(L):
             opening[z] = partial[z]
-            to_next[z] = total[z]
-
-
-def chain2_kernel(block, outer, pair, total, partial, opening, coef, to_next, u):
-    here = lax.axis_index("tm") // 4 == 2
-    leads = lax.axis_index("tm") % 4 == 0
+            send[z] = d[z]
+
+    @pl.when(lax.axis_index("tm") // 4 == 0)
+    def _():
+        for z in range(L):
+            send[z] = partial[z]
+
+
+def chain2_kernel(block, outer, pair, total, partial, opening, coef, send, u):
+    here, place = lax.axis_index("tm") // 4 == 2, lax.axis_index("tm") % 4
     get = arrived(block, outer, pair)
 
     @pl.when(here)
@@ -233,39 +251,39 @@
         for i in range(3):
             coarse_twice(u, L, coef, 8 - 2 * i)
 
-        @pl.when(leads)
+        @pl.when(place == 0)
         def _():
             for z in range(L):
-                to_next[z] = u[L + z] + partial[z]
-
-        @pl.when(jnp.logical_not(leads))
+                send[z] = u[L + z] + partial[z]
+
+        @pl.when(place > 0)
         def _():
             coarse_twice(u, L, coef, 2)
             for z in range(L):
-                to_next[z] = u[L + z] + total[z]
+                send[z] = u[L + z] + total[z]
 
     @pl.when(jnp.logical_not(here))
     def _():
         for z in range(L):
-            to_next[z] = opening[z]
-
-
-def finish_kernel(b1, o1, p1, b2, o2, p2, b3, o3, p3, before, prefix, phi, own, outer, inner, coef, fine, out, u, w):
-    group, place = lax.axis_index("tm") // 4, lax.axis_index("tm") % 4
-    first = lax.axis_index("tm") == 0
+            send[z] = opening[z]
+
+
+def finish_kernel(b1, o1, p1, b2, o2, p2, b3, o3, p3, before, g, prefix, phi, own, outer, inner, open_outer, open_inner, coef, fine, out, u, w):
+    t = lax.axis_index("tm")
+    group, place = t // 4, t % 4
     odd = lax.axis_index("space") % 2
 
-    def load(wanted, get):
+    def put(wanted, into, halo, get):
         @pl.when(wanted)
         def _():
-            for z in range(-7, L + 7):
-                u[7 + z] = get(z)
-
-    last = jnp.logical_or(place == 0, jnp.logical_or(group == 0, group == 3))
-    load(last, arrived(b3, o3, p3))
-    load(jnp.logical_and(jnp.logical_not(last), group == 1), arrived(b1, o1, p1))
-    load(jnp.logical_and(jnp.logical_not(last), group == 2), arrived(b2, o2, p2))
-
+            for z in range(-halo, L + halo):
+                into[halo + z] = get(z)
+
+    source = jnp.where(jnp.logical_and(place == 0, group > 0), jnp.minimum(group + 1, 3), group)
+    put(source == 0, u, 7, lambda z: jnp.zeros((NY, NX), jnp.float32))
+    put(source == 1, u, 7, arrived(b1, o1, p1))
+    put(source == 2, u, 7, arrived(b2, o2, p2))
+    put(source == 3, u, 7, arrived(b3, o3, p3))
     @pl.when(place == 3)
     def _():
         sweep(u, 7, coef, COARSE_HALO, -6, L + 6)
@@ -279,24 +297,34 @@
     for z in range(-3, L + 3):
         w[3 + z] = u[7 + z] + prefix[3 + z]
 
-    @pl.when(first)
+    @pl.when(t == 0)
     def _():
         for z in range(-3, L + 3):
-            u[7 + z] = w[3 + z] + ext(own, outer, inner, z, SENT[0], SENT[0], L)
-
-    @pl.when(jnp.logical_not(first))
+            u[7 + z] = w[3 + z] + ext(own, open_outer, open_inner, z, 0, 0, 6 * L)
+
+    @pl.when(t > 0)
     def _():
         for z in range(-3, L + 3):
             u[7 + z] = w[3 + z] + before[3 + z]
 
     coarse_twice(w, 3, coef, 2)
-    for z in range(L):
-        out[3, z + odd * (L - 1 - 2 * z)] = w[3 + z] + before[L + 6 + z] + phi[3 + z]
-    at = SENT[0] + SENT[1]
+
+    def last(wanted, get):
+        @pl.when(wanted)
+        def _():
+            for z in range(L):
+                out[3, z + odd * (L - 1 - 2 * z)] = get(z) + phi[3 + z]
+
+    last(place > 0, lambda z: w[3 + z] + g[place - 1, z])
+    last(t == 0, lambda z: w[3 + z])
+    last(t == 4, lambda z: b1[z])
+    last(t == 8, lambda z: b2[z])
+    last(t == 12, lambda z: w[3 + z] + b2[z])
+    at = SENT[0]
     for step in range(3):
         halo = 2 - step
         sweep(u, 7, fine, FINE_HALO, -halo, L + halo,
-              lambda z, cur, new: new + ext(own, outer, inner, z, at, at, 2 * L))
+              lambda z, cur, new: new + ext(own, outer, inner, z, at, at, L))
         for z in range(L):
             out[step, z + odd * (L - 1 - 2 * z)] = u[7 + z]
 
@@ -313,38 +341,54 @@
     def from_inner(x):
         return lax.ppermute(x, "space", paired)
 
-    def later(x, steps, moves=None, leaving=range(times)):
-        moves = [(i, i) for i in range(count)] if moves is None else moves
-        pairs = [(t * count + a, (t + steps) * count + b) for t in leaving if t + steps < times for a, b in moves]
+    same = [(i, i) for i in range(count)]
+
+    def move(x, intervals, moves=same):
+        pairs = [(a * count + i, b * count + j) for a, b in intervals for i, j in moves]
         return lax.ppermute(x, ("tm", "space"), pairs)
 
-    def hand_on(x, leaving):
-        block, outer = later(x, 4, None, leaving), later(x, 4, facing, leaving)
+    def hop(x, intervals, others=()):
+        block, outer = move(x, [*intervals, *others]), move(x, intervals, facing)
         pair = lax.all_gather(block, "space", axis_index_groups=[[i, i + 1] for i in range(0, count, 2)])
         return block, outer, pair
 
-    own, outer, inner = pl.pallas_call(
+    hbm = pl.BlockSpec(memory_space=pltpu.HBM)
+    own, outer, inner, open_outer, open_inner = pl.pallas_call(
         pack_kernel,
-        out_shape=[jax.ShapeDtypeStruct((n, NY, NX), jnp.float32) for n in (7 * L, FIRST, FIRST)],
-        in_specs=[pl.BlockSpec(memory_space=pltpu.HBM)] * 5,
-        scratch_shapes=[VMEM((7, L, NY, NX), jnp.float32), pltpu.SemaphoreType.DMA((7,))],
-    )(guesses, forcing, initial, kappa, velocity)
+        out_shape=[jax.ShapeDtypeStruct((n, NY, NX), jnp.float32) for n in (7 * L, FIRST, FIRST, OPEN, OPEN)],
+        in_specs=[hbm] * 5,
+        out_specs=[hbm] * 5,
+        scratch_shapes=[
+            VMEM((7, L, NY, NX), jnp.float32),
+            *[VMEM((n, NY, NX), jnp.float32) for n in (7 * L, FIRST + OPEN, FIRST + OPEN)],
+            pltpu.SemaphoreType.DMA((7,)),
+            pltpu.SemaphoreType.DMA((21,)),
+        ],
+    )(guesses, forcing, kappa, velocity, initial)
     outer, inner = from_outer(outer), from_inner(inner)
+    open_outer, open_inner = move(open_outer, [(0, 0)], facing), move(open_inner, [(0, 0)], paired)
     (own,) = call(settle_kernel, (7 * L,))(own)
-    d, phi, fine = call(local_kernel, (L, 2 * L + 6, (7, L + 2 * FINE_HALO)), (L + 8, L + 14, L + 4))(own, outer, inner)
+    d, phi, fine = call(local_kernel, (L, L + 6, (7, L + 2 * FINE_HALO)), (L + 8, L + 14, L + 4))(
+        own, outer, inner, open_outer, open_inner
+    )
     (coef,) = call(coarse_kernel, ((7, L + 2 * COARSE_HALO),))(own, outer, inner)
     g = lax.all_gather(d, "tm", axis_index_groups=[[4 * a + b for b in range(4)] for a in range(times // 4)])
     slab_outer, slab_inner = call(slab_pack_kernel, (12, 12))(g)
     slab_outer, slab_inner = from_outer(slab_outer), from_inner(slab_inner)
     total, partial, prefix = call(slab_kernel, (L, L, L + 6), (L + 12,))(g, slab_outer, slab_inner, coef)
-    one = hand_on(total, range(4))
-    to_two, opening, left = call(chain1_kernel, (L, L, 2 * L + 6), (3 * L,))(*one, total, partial, phi, coef)
-    before = later(left, 1)
-    two = hand_on(to_two, range(4, 8))
-    (to_three,) = call(chain2_kernel, (L,), (3 * L,))(*two, total, partial, opening, coef)
-    three = hand_on(to_three, (0, 4, 8, 9, 10, 11))
+
+    def after(slab):
+        return [(t, t + 4) for t in range(4 * slab, 4 * slab + 4)]
+
+    one = hop(total, after(0))
+    opening, send = call(chain1_kernel, (L, L), (3 * L,))(*one, total, partial, d, coef)
+    (leaving,) = call(leave_kernel, (L + 6,))(phi, send)
+    before = move(leaving, [(t, t + 1) for t in range(times - 1)])
+    two = hop(send, after(1) + [(0, 4)], [(11, 12)])
+    (send,) = call(chain2_kernel, (L,), (3 * L,))(*two, total, partial, opening, coef)
+    three = hop(send, after(2) + [(4, 8)])
     (out,) = call(finish_kernel, ((4, L),), (L + 14, L + 6))(
-        *one, *two, *three, before, prefix, phi, own, outer, inner, coef, fine
+        *one, *two, *three, before, g, prefix, phi, own, outer, inner, open_outer, open_inner, coef, fine
     )
     return out
 

time: 93.2 us -> 88.9 us (0.954)
  the two profiles are of different devices: /device:TPU:115 before, /device:TPU:87 now
where the time goes in v4:
time: 88.9 us; the launch traced here: 88.5 us
  waiting for transfers between devices  30.1 us (34%)
  blocking collectives  28.3 us (32%)
  starting transfers between devices  21.7 us (24%)
  Pallas kernels  7.01 us (8%)
  local copies, waits for them, and re-layouts  1.17 us (1%)
    ppermute x9, waiting for transfers between devices, move(): return lax.ppermute(x, ('tm', 'space'), pairs)  25.3 us
    all_gather x1, blocking collectives, body(): lax.all_gather(d, 'tm', axis_index_groups=[[4 * a + b for b in range(4)]...  21.6 us
    ppermute x9, starting transfers between devices, move(): return lax.ppermute(x, ('tm', 'space'), pairs)  9.52 us
    ppermute x2, starting transfers between devices, from_outer(): return lax.ppermute(x, 'space', facing)  8.34 us
    all_gather x3, blocking collectives, hop(): lax.all_gather(block, 'space', axis_index_groups=[[i, i + 1] for i in ran...  6.62 us
    ppermute x2, waiting for transfers between devices, from_outer(): return lax.ppermute(x, 'space', facing)  4.81 us
    ppermute x2, starting transfers between devices, from_inner(): return lax.ppermute(x, 'space', paired)  3.84 us
    pallas_call x1, Pallas kernels, body(): pl.pallas_call(pack_kernel, out_shape=[jax.ShapeDtypeStruct((n, NY, NX),...  2.55 us
  transfers between devices with their start and end apart: 13, of which 4 were waited for; matrix products, arithmetic and copies ran while one was open for 0% of the time, Pallas kernels for 0%

profile of v4, /device:TPU:87, one launch (start us, length us, event | category | flops | bytes accessed | tf_op | source)
XLA Modules:
  0.0 88.5 jit_solution(18188575638684860115)
XLA Ops:
  0.0 2.5 %shard_map.55 = (f32[56,32,128]{2,1,0:T(8,128)}, f32[38,32,128]{2,1,0:T(8,128)}, f32[38,32,128]{2,1,0:T(8,128)}, f32[7,32,128]{2,1,0:T(8,128)}, f32[7,32,128]{2,1,0:T(8,128)}) custom-call(f32[1,8,32,128]{3,2,1,0:T(8,128)} %guesses.1, f32[1,8,32,128]{3,2,1,0:T(8,128)} %forcing.1, f32[8,32,128]{2,1,0:T(8,128)} %kappa.1, f32[3,8,32,128]{3,2,1,0:T(8,128)} %velocity.1, ...), custom_call_target="tpu_custom_call" | custom-call | tf_op jit(solution)/shard_map/pallas_call | solution.py:356
  2.6 3.8 %collective-permute-start = (f32[38,32,128]{2,1,0:T(8,128)}, f32[38,32,128]{2,1,0:T(8,128)S(1)}, u32[]{:S(2)}, u32[]{:S(2)}) collective-permute-start(f32[38,32,128]{2,1,0:T(8,128)} %get-tuple-element.21), channel_id=1, source_target_pairs={{1,2},{3,4},{5,6},{7,8},{9,10},{11,12},{13,14},{15,16},{17,18},{19... | collective-permute-start | bytes 1867784 | tf_op jit(solution)/shard_map/ppermute | solution.py:339
  6.3 1.9 %collective-permute-start.1 = (f32[38,32,128]{2,1,0:T(8,128)}, f32[38,32,128]{2,1,0:T(8,128)S(1)}, u32[]{:S(2)}, u32[]{:S(2)}) collective-permute-start(f32[38,32,128]{2,1,0:T(8,128)} %get-tuple-element.22), channel_id=1, source_target_pairs={{0,1},{1,0},{2,3},{3,2},{4,5},{5,4},{6,7},{7,6},{8,9},{9,8},{10,11... | collective-permute-start | bytes 1867784 | tf_op jit(solution)/shard_map/ppermute | solution.py:342
  9.6 1.2 %copy-done = f32[56,32,128]{2,1,0:T(8,128)S(1)} copy-done((f32[56,32,128]{2,1,0:T(8,128)S(1)}, f32[56,32,128]{2,1,0:T(8,128)}, u32[]{:S(2)}) %copy-start) | copy-done | bytes 917528
  10.9 3.7 %collective-permute-done.outer = f32[38,32,128]{2,1,0:T(8,128)S(1)} collective-permute-done((f32[38,32,128]{2,1,0:T(8,128)}, f32[38,32,128]{2,1,0:T(8,128)S(1)}, u32[]{:S(2)}, u32[]{:S(2)}) %collective-permute-start) | collective-permute-done | bytes 622624 | tf_op jit(solution)/shard_map/ppermute | solution.py:339
  14.6 1.6 %shard_map.57 = (f32[8,32,128]{2,1,0:T(8,128)S(1)}, f32[14,32,128]{2,1,0:T(8,128)S(1)}, f32[7,20,32,128]{3,2,1,0:T(8,128)S(1)}) custom-call(f32[56,32,128]{2,1,0:T(8,128)S(1)} %shard_map.56.own, f32[38,32,128]{2,1,0:T(8,128)S(1)} %collective-permute-done.outer, f32[38,32,128]{2,1,0:T(8,128)S(1)} %collective-permute-done.1.inner, ...), custom_call_target="tpu_custom_call" | custom-call | tf_op jit(solution)/shard_map/pallas_call | solution.py:371
  16.2 21.6 %all-gather = f32[32,32,128]{2,1,0:T(8,128)S(1)} all-gather(f32[8,32,128]{2,1,0:T(8,128)S(1)} %get-tuple-element.25.d), channel_id=2, replica_groups={{0,32,64,96},{128,160,192,224},{256,288,320,352},{384,416,448,480},{1,3..., dimensions={0}, use_global_device_ids=true | all-gather | bytes 655360 | tf_op jit(solution)/shard_map/all_gather | solution.py:375
  37.9 4.6 %collective-permute-start.4 = (f32[12,32,128]{2,1,0:T(8,128)S(1)}, f32[12,32,128]{2,1,0:T(8,128)S(1)}, u32[]{:S(2)}, u32[]{:S(2)}) collective-permute-start(f32[12,32,128]{2,1,0:T(8,128)S(1)} %get-tuple-element.26), channel_id=1, source_target_pairs={{1,2},{3,4},{5,6},{7,8},{9,10},{11,12},{13,14},{15,16},{17,18},{19... | collective-permute-start | bytes 589832 | tf_op jit(solution)/shard_map/ppermute | solution.py:339
  42.4 1.9 %collective-permute-start.5 = (f32[12,32,128]{2,1,0:T(8,128)S(1)}, f32[12,32,128]{2,1,0:T(8,128)S(1)}, u32[]{:S(2)}, u32[]{:S(2)}) collective-permute-start(f32[12,32,128]{2,1,0:T(8,128)S(1)} %get-tuple-element.27), channel_id=1, source_target_pairs={{0,1},{1,0},{2,3},{3,2},{4,5},{5,4},{6,7},{7,6},{8,9},{9,8},{10,11... | collective-permute-start | bytes 589832 | tf_op jit(solution)/shard_map/ppermute | solution.py:342
  44.7 1.1 %collective-permute-done.4.outer = f32[12,32,128]{2,1,0:T(8,128)S(1)} collective-permute-done((f32[12,32,128]{2,1,0:T(8,128)S(1)}, f32[12,32,128]{2,1,0:T(8,128)S(1)}, u32[]{:S(2)}, u32[]{:S(2)}) %collective-permute-start.4) | collective-permute-done | bytes 196640 | tf_op jit(solution)/shard_map/ppermute | solution.py:339
  45.8 0.9 %shard_map.60 = (f32[8,32,128]{2,1,0:T(8,128)S(1)}, f32[8,32,128]{2,1,0:T(8,128)S(1)}, f32[14,32,128]{2,1,0:T(8,128)S(1)}) custom-call(f32[4,8,32,128]{3,2,1,0:T(8,128)S(1)} %bitcast.5, f32[12,32,128]{2,1,0:T(8,128)S(1)} %collective-permute-done.4.outer, f32[12,32,128]{2,1,0:T(8,128)S(1)} %collective-permute-done.5.inner, f32[7,22,32,128]{3,2,1,0:T(8,128)S(1)} %shard_map.59.coef), custom_call_target="tpu_custom_call" | custom-call | tf_op jit(solution)/shard_map/pallas_call | solution.py:378
  46.7 0.7 collective-permute-start.6
  47.4 0.7 collective-permute-start.7
  48.0 2.0 %all-gather.1 = f32[16,32,128]{2,1,0:T(8,128)S(1)} all-gather(f32[8,32,128]{2,1,0:T(8,128)S(1)} %collective-permute-done.6.block.b1), channel_id=3, replica_groups={{0,1},{2,3},{4,5},{6,7},{8,9},{10,11},{12,13},{14,15},{16,17},{18,19},{..., dimensions={0}, use_global_device_ids=true | all-gather | bytes 393216 | tf_op jit(solution)/shard_map/all_gather | solution.py:352
  50.1 1.3 %collective-permute-start.8 = (f32[8,32,128]{2,1,0:T(8,128)S(1)}, f32[8,32,128]{2,1,0:T(8,128)S(1)}, u32[]{:S(2)}, u32[]{:S(2)}) collective-permute-start(f32[8,32,128]{2,1,0:T(8,128)S(1)} %get-tuple-element.30.total), channel_id=1, source_target_pairs={{128,256},{129,257},{130,258},{131,259},{132,260},{133,261},{134,2... | collective-permute-start | bytes 393224 | tf_op jit(solution)/shard_map/ppermute | solution.py:348
  51.4 0.7 collective-permute-start.9
  52.1 2.3 %collective-permute-start.12 = (f32[14,32,128]{2,1,0:T(8,128)S(1)}, f32[14,32,128]{2,1,0:T(8,128)S(1)}, u32[]{:S(2)}, u32[]{:S(2)}) collective-permute-start(f32[14,32,128]{2,1,0:T(8,128)S(1)} %shard_map.63), channel_id=1, source_target_pairs={{0,32},{1,33},{2,34},{3,35},{4,36},{5,37},{6,38},{7,39},{8,40},{9,... | collective-permute-start | bytes 688136 | tf_op jit(solution)/shard_map/ppermute | solution.py:348
  54.4 13.0 %collective-permute-done.8.block.b2 = f32[8,32,128]{2,1,0:T(8,128)S(1)} collective-permute-done((f32[8,32,128]{2,1,0:T(8,128)S(1)}, f32[8,32,128]{2,1,0:T(8,128)S(1)}, u32[]{:S(2)}, u32[]{:S(2)}) %collective-permute-start.8) | collective-permute-done | bytes 131104 | tf_op jit(solution)/shard_map/ppermute | solution.py:348
  67.4 2.1 %all-gather.2 = f32[16,32,128]{2,1,0:T(8,128)S(1)} all-gather(f32[8,32,128]{2,1,0:T(8,128)S(1)} %collective-permute-done.8.block.b2), channel_id=4, replica_groups={{0,1},{2,3},{4,5},{6,7},{8,9},{10,11},{12,13},{14,15},{16,17},{18,19},{..., dimensions={0}, use_global_device_ids=true | all-gather | bytes 393216 | tf_op jit(solution)/shard_map/all_gather | solution.py:352
  69.6 1.3 %collective-permute-start.10 = (f32[8,32,128]{2,1,0:T(8,128)S(1)}, f32[8,32,128]{2,1,0:T(8,128)S(1)}, u32[]{:S(2)}, u32[]{:S(2)}) collective-permute-start(f32[8,32,128]{2,1,0:T(8,128)S(1)} %shard_map.62), channel_id=1, source_target_pairs={{256,384},{257,385},{258,386},{259,387},{260,388},{261,389},{262,3... | collective-permute-start | bytes 393224 | tf_op jit(solution)/shard_map/ppermute | solution.py:348
  70.9 1.3 %collective-permute-start.11 = (f32[8,32,128]{2,1,0:T(8,128)S(1)}, f32[8,32,128]{2,1,0:T(8,128)S(1)}, u32[]{:S(2)}, u32[]{:S(2)}) collective-permute-start(f32[8,32,128]{2,1,0:T(8,128)S(1)} %shard_map.62), channel_id=1, source_target_pairs={{257,386},{259,388},{261,390},{263,392},{265,394},{267,396},{269,3... | collective-permute-start | bytes 393224 | tf_op jit(solution)/shard_map/ppermute | solution.py:348
  72.2 12.3 %collective-permute-done.10.b3 = f32[8,32,128]{2,1,0:T(8,128)S(1)} collective-permute-done((f32[8,32,128]{2,1,0:T(8,128)S(1)}, f32[8,32,128]{2,1,0:T(8,128)S(1)}, u32[]{:S(2)}, u32[]{:S(2)}) %collective-permute-start.10) | collective-permute-done | bytes 131104 | tf_op jit(solution)/shard_map/ppermute | solution.py:348
  84.5 2.5 %all-gather.3 = f32[16,32,128]{2,1,0:T(8,128)S(1)} all-gather(f32[8,32,128]{2,1,0:T(8,128)S(1)} %collective-permute-done.10.b3), channel_id=5, replica_groups={{0,1},{2,3},{4,5},{6,7},{8,9},{10,11},{12,13},{14,15},{16,17},{18,19},{..., dimensions={0}, use_global_device_ids=true | all-gather | bytes 393216 | tf_op jit(solution)/shard_map/all_gather | solution.py:352
  87.0 1.5 %shard_map.64 = f32[4,8,32,128]{3,2,1,0:T(8,128)} custom-call(f32[8,32,128]{2,1,0:T(8,128)S(1)} %collective-permute-done.6.block.b1, f32[8,32,128]{2,1,0:T(8,128)S(1)} %collective-permute-done.7.outer.o1, f32[2,8,32,128]{3,2,1,0:T(8,128)S(1)} %bitcast.10, f32[8,32,128]{2,1,0:T(8,128)S(1)} %collective-permute-done.8.block.b2, ...), custom_call_target="tpu_custom_call" | custom-call | tf_op jit(solution)/shard_map/pallas_call | solution.py:390
  (18 shorter events, 1.8 us)
Async XLA Ops:
  2.6 12.0 %collective-permute-start = (f32[38,32,128]{2,1,0:T(8,128)}, f32[38,32,128]{2,1,0:T(8,128)S(1)}, u32[]{:S(2)}, u32[]{:S(2)}) collective-permute-start(f32[38,32,128]{2,1,0:T(8,128)} %get-tuple-element.21), channel_id=1, source_target_pairs={{1,2},{3,4},{5,6},{7,8},{9,10},{11,12},{13,14},{15,16},{17,18},{19... | collective-permute-start | bytes 1867784 | tf_op jit(solution)/shard_map/ppermute | solution.py:339
  6.3 8.3 %collective-permute-start.1 = (f32[38,32,128]{2,1,0:T(8,128)}, f32[38,32,128]{2,1,0:T(8,128)S(1)}, u32[]{:S(2)}, u32[]{:S(2)}) collective-permute-start(f32[38,32,128]{2,1,0:T(8,128)} %get-tuple-element.22), channel_id=1, source_target_pairs={{0,1},{1,0},{2,3},{3,2},{4,5},{5,4},{6,7},{7,6},{8,9},{9,8},{10,11... | collective-permute-start | bytes 1867784 | tf_op jit(solution)/shard_map/ppermute | solution.py:342
  8.3 2.6 %collective-permute-start.2 = (f32[7,32,128]{2,1,0:T(8,128)}, f32[7,32,128]{2,1,0:T(8,128)S(1)}, u32[]{:S(2)}, u32[]{:S(2)}) collective-permute-start(f32[7,32,128]{2,1,0:T(8,128)} %get-tuple-element.23), channel_id=1, source_target_pairs={{1,2},{3,4},{5,6},{7,8},{9,10},{11,12},{13,14},{15,16},{17,18},{19... | collective-permute-start | bytes 344072 | tf_op jit(solution)/shard_map/ppermute | solution.py:348
  8.9 1.9 %collective-permute-start.3 = (f32[7,32,128]{2,1,0:T(8,128)}, f32[7,32,128]{2,1,0:T(8,128)S(1)}, u32[]{:S(2)}, u32[]{:S(2)}) collective-permute-start(f32[7,32,128]{2,1,0:T(8,128)} %get-tuple-element.24), channel_id=1, source_target_pairs={{0,1},{1,0},{2,3},{3,2},{4,5},{5,4},{6,7},{7,6},{8,9},{9,8},{10,11... | collective-permute-start | bytes 344072 | tf_op jit(solution)/shard_map/ppermute | solution.py:348
  9.6 1.2 %copy-start = (f32[56,32,128]{2,1,0:T(8,128)S(1)}, f32[56,32,128]{2,1,0:T(8,128)}, u32[]{:S(2)}) copy-start(f32[56,32,128]{2,1,0:T(8,128)} %get-tuple-element.20.held) | copy-start | bytes 2752516
  37.9 7.9 %collective-permute-start.4 = (f32[12,32,128]{2,1,0:T(8,128)S(1)}, f32[12,32,128]{2,1,0:T(8,128)S(1)}, u32[]{:S(2)}, u32[]{:S(2)}) collective-permute-start(f32[12,32,128]{2,1,0:T(8,128)S(1)} %get-tuple-element.26), channel_id=1, source_target_pairs={{1,2},{3,4},{5,6},{7,8},{9,10},{11,12},{13,14},{15,16},{17,18},{19... | collective-permute-start | bytes 589832 | tf_op jit(solution)/shard_map/ppermute | solution.py:339
  42.4 3.3 %collective-permute-start.5 = (f32[12,32,128]{2,1,0:T(8,128)S(1)}, f32[12,32,128]{2,1,0:T(8,128)S(1)}, u32[]{:S(2)}, u32[]{:S(2)}) collective-permute-start(f32[12,32,128]{2,1,0:T(8,128)S(1)} %get-tuple-element.27), channel_id=1, source_target_pairs={{0,1},{1,0},{2,3},{3,2},{4,5},{5,4},{6,7},{7,6},{8,9},{9,8},{10,11... | collective-permute-start | bytes 589832 | tf_op jit(solution)/shard_map/ppermute | solution.py:342
  46.7 1.4 %collective-permute-start.6 = (f32[8,32,128]{2,1,0:T(8,128)S(1)}, f32[8,32,128]{2,1,0:T(8,128)S(1)}, u32[]{:S(2)}, u32[]{:S(2)}) collective-permute-start(f32[8,32,128]{2,1,0:T(8,128)S(1)} %get-tuple-element.28.total), channel_id=1, source_target_pairs={{0,128},{1,129},{2,130},{3,131},{4,132},{5,133},{6,134},{7,135},{8... | collective-permute-start | bytes 393224 | tf_op jit(solution)/shard_map/ppermute | solution.py:348
  47.4 2.7 %collective-permute-start.7 = (f32[8,32,128]{2,1,0:T(8,128)S(1)}, f32[8,32,128]{2,1,0:T(8,128)S(1)}, u32[]{:S(2)}, u32[]{:S(2)}) collective-permute-start(f32[8,32,128]{2,1,0:T(8,128)S(1)} %get-tuple-element.28.total), channel_id=1, source_target_pairs={{1,130},{3,132},{5,134},{7,136},{9,138},{11,140},{13,142},{15,144}... | collective-permute-start | bytes 393224 | tf_op jit(solution)/shard_map/ppermute | solution.py:348
  50.1 17.4 %collective-permute-start.8 = (f32[8,32,128]{2,1,0:T(8,128)S(1)}, f32[8,32,128]{2,1,0:T(8,128)S(1)}, u32[]{:S(2)}, u32[]{:S(2)}) collective-permute-start(f32[8,32,128]{2,1,0:T(8,128)S(1)} %get-tuple-element.30.total), channel_id=1, source_target_pairs={{128,256},{129,257},{130,258},{131,259},{132,260},{133,261},{134,2... | collective-permute-start | bytes 393224 | tf_op jit(solution)/shard_map/ppermute | solution.py:348
  51.4 18.2 %collective-permute-start.9 = (f32[8,32,128]{2,1,0:T(8,128)S(1)}, f32[8,32,128]{2,1,0:T(8,128)S(1)}, u32[]{:S(2)}, u32[]{:S(2)}) collective-permute-start(f32[8,32,128]{2,1,0:T(8,128)S(1)} %get-tuple-element.30.total), channel_id=1, source_target_pairs={{129,258},{131,260},{133,262},{135,264},{137,266},{139,268},{141,2... | collective-permute-start | bytes 393224 | tf_op jit(solution)/shard_map/ppermute | solution.py:348
  52.1 34.9 %collective-permute-start.12 = (f32[14,32,128]{2,1,0:T(8,128)S(1)}, f32[14,32,128]{2,1,0:T(8,128)S(1)}, u32[]{:S(2)}, u32[]{:S(2)}) collective-permute-start(f32[14,32,128]{2,1,0:T(8,128)S(1)} %shard_map.63), channel_id=1, source_target_pairs={{0,32},{1,33},{2,34},{3,35},{4,36},{5,37},{6,38},{7,39},{8,40},{9,... | collective-permute-start | bytes 688136 | tf_op jit(solution)/shard_map/ppermute | solution.py:348
  69.6 14.9 %collective-permute-start.10 = (f32[8,32,128]{2,1,0:T(8,128)S(1)}, f32[8,32,128]{2,1,0:T(8,128)S(1)}, u32[]{:S(2)}, u32[]{:S(2)}) collective-permute-start(f32[8,32,128]{2,1,0:T(8,128)S(1)} %shard_map.62), channel_id=1, source_target_pairs={{256,384},{257,385},{258,386},{259,387},{260,388},{261,389},{262,3... | collective-permute-start | bytes 393224 | tf_op jit(solution)/shard_map/ppermute | solution.py:348
  70.9 16.1 %collective-permute-start.11 = (f32[8,32,128]{2,1,0:T(8,128)S(1)}, f32[8,32,128]{2,1,0:T(8,128)S(1)}, u32[]{:S(2)}, u32[]{:S(2)}) collective-permute-start(f32[8,32,128]{2,1,0:T(8,128)S(1)} %shard_map.62), channel_id=1, source_target_pairs={{257,386},{259,388},{261,390},{263,392},{265,394},{267,396},{269,3... | collective-permute-start | bytes 393224 | tf_op jit(solution)/shard_map/ppermute | solution.py:348

commit v5 on v4

--- a/solution.py
+++ b/solution.py
@@ -240,7 +240,9 @@
             send[z] = partial[z]
 
 
-def chain2_kernel(block, outer, pair, total, partial, opening, coef, send, u):
+def chain2_kernel(block, outer, pair, total, partial, opening, coef, before, send, kept, u):
+    for i in range(L + 6):
+        kept[i] = before[i]
     here, place = lax.axis_index("tm") // 4 == 2, lax.axis_index("tm") % 4
     get = arrived(block, outer, pair)
 
@@ -382,10 +384,10 @@
 
     one = hop(total, after(0))
     opening, send = call(chain1_kernel, (L, L), (3 * L,))(*one, total, partial, d, coef)
-    (leaving,) = call(leave_kernel, (L + 6,))(phi, send)
+    (leaving,) = call(leave_kernel, (L + 6,))(phi, total)
     before = move(leaving, [(t, t + 1) for t in range(times - 1)])
     two = hop(send, after(1) + [(0, 4)], [(11, 12)])
-    (send,) = call(chain2_kernel, (L,), (3 * L,))(*two, total, partial, opening, coef)
+    send, before = call(chain2_kernel, (L, L + 6), (3 * L,))(*two, total, partial, opening, coef, before)
     three = hop(send, after(2) + [(4, 8)])
     (out,) = call(finish_kernel, ((4, L),), (L + 14, L + 6))(
         *one, *two, *three, before, g, prefix, phi, own, outer, inner, open_outer, open_inner, coef, fine

time: 88.9 us -> 87.7 us (0.987)
  the two profiles are of different devices: /device:TPU:87 before, /device:TPU:95 now
where the time goes in v5:
time: 87.7 us; the launch traced here: 87.3 us
  blocking collectives  28.2 us (32%)
  waiting for transfers between devices  26 us (30%)
  starting transfers between devices  24.7 us (28%)
  Pallas kernels  7.03 us (8%)
  local copies, waits for them, and re-layouts  1.17 us (1%)
    all_gather x1, blocking collectives, body(): lax.all_gather(d, 'tm', axis_index_groups=[[4 * a + b for b in range(4)]...  21.6 us
    ppermute x9, waiting for transfers between devices, move(): return lax.ppermute(x, ('tm', 'space'), pairs)  21.3 us
    ppermute x9, starting transfers between devices, move(): return lax.ppermute(x, ('tm', 'space'), pairs)  10.9 us
    ppermute x2, starting transfers between devices, from_outer(): return lax.ppermute(x, 'space', facing)  9.9 us
    all_gather x3, blocking collectives, hop(): lax.all_gather(block, 'space', axis_index_groups=[[i, i + 1] for i in ran...  6.63 us
    ppermute x2, waiting for transfers between devices, from_outer(): return lax.ppermute(x, 'space', facing)  4.65 us
    ppermute x2, starting transfers between devices, from_inner(): return lax.ppermute(x, 'space', paired)  3.84 us
    pallas_call x1, Pallas kernels, body(): pl.pallas_call(pack_kernel, out_shape=[jax.ShapeDtypeStruct((n, NY, NX),...  2.54 us
  transfers between devices with their start and end apart: 13, of which 4 were waited for; matrix products, arithmetic and copies ran while one was open for 0% of the time, Pallas kernels for 0%

profile of v5, /device:TPU:95, one launch (start us, length us, event | category | flops | bytes accessed | tf_op | source)
XLA Modules:
  0.0 87.3 jit_solution(4535692103160029768)
XLA Ops:
  0.0 2.5 %shard_map.55 = (f32[56,32,128]{2,1,0:T(8,128)}, f32[38,32,128]{2,1,0:T(8,128)}, f32[38,32,128]{2,1,0:T(8,128)}, f32[7,32,128]{2,1,0:T(8,128)}, f32[7,32,128]{2,1,0:T(8,128)}) custom-call(f32[1,8,32,128]{3,2,1,0:T(8,128)} %guesses.1, f32[1,8,32,128]{3,2,1,0:T(8,128)} %forcing.1, f32[8,32,128]{2,1,0:T(8,128)} %kappa.1, f32[3,8,32,128]{3,2,1,0:T(8,128)} %velocity.1, ...), custom_call_target="tpu_custom_call" | custom-call | tf_op jit(solution)/shard_map/pallas_call | solution.py:358
  2.6 5.0 %collective-permute-start = (f32[38,32,128]{2,1,0:T(8,128)}, f32[38,32,128]{2,1,0:T(8,128)S(1)}, u32[]{:S(2)}, u32[]{:S(2)}) collective-permute-start(f32[38,32,128]{2,1,0:T(8,128)} %get-tuple-element.23), channel_id=1, source_target_pairs={{1,2},{3,4},{5,6},{7,8},{9,10},{11,12},{13,14},{15,16},{17,18},{19... | collective-permute-start | bytes 1867784 | tf_op jit(solution)/shard_map/ppermute | solution.py:341
  7.5 1.9 %collective-permute-start.1 = (f32[38,32,128]{2,1,0:T(8,128)}, f32[38,32,128]{2,1,0:T(8,128)S(1)}, u32[]{:S(2)}, u32[]{:S(2)}) collective-permute-start(f32[38,32,128]{2,1,0:T(8,128)} %get-tuple-element.24), channel_id=1, source_target_pairs={{0,1},{1,0},{2,3},{3,2},{4,5},{5,4},{6,7},{7,6},{8,9},{9,8},{10,11... | collective-permute-start | bytes 1867784 | tf_op jit(solution)/shard_map/ppermute | solution.py:344
  10.8 1.2 %copy-done = f32[56,32,128]{2,1,0:T(8,128)S(1)} copy-done((f32[56,32,128]{2,1,0:T(8,128)S(1)}, f32[56,32,128]{2,1,0:T(8,128)}, u32[]{:S(2)}) %copy-start) | copy-done | bytes 917528
  12.1 3.6 %collective-permute-done.outer = f32[38,32,128]{2,1,0:T(8,128)S(1)} collective-permute-done((f32[38,32,128]{2,1,0:T(8,128)}, f32[38,32,128]{2,1,0:T(8,128)S(1)}, u32[]{:S(2)}, u32[]{:S(2)}) %collective-permute-start) | collective-permute-done | bytes 622624 | tf_op jit(solution)/shard_map/ppermute | solution.py:341
  15.7 1.6 %shard_map.57 = (f32[8,32,128]{2,1,0:T(8,128)S(1)}, f32[14,32,128]{2,1,0:T(8,128)S(1)}, f32[7,20,32,128]{3,2,1,0:T(8,128)S(1)}) custom-call(f32[56,32,128]{2,1,0:T(8,128)S(1)} %shard_map.56.own, f32[38,32,128]{2,1,0:T(8,128)S(1)} %collective-permute-done.outer, f32[38,32,128]{2,1,0:T(8,128)S(1)} %collective-permute-done.1.inner, ...), custom_call_target="tpu_custom_call" | custom-call | tf_op jit(solution)/shard_map/pallas_call | solution.py:373
  17.2 21.6 %all-gather = f32[32,32,128]{2,1,0:T(8,128)S(1)} all-gather(f32[8,32,128]{2,1,0:T(8,128)S(1)} %get-tuple-element.27.d), channel_id=2, replica_groups={{0,32,64,96},{128,160,192,224},{256,288,320,352},{384,416,448,480},{1,3..., dimensions={0}, use_global_device_ids=true | all-gather | bytes 655360 | tf_op jit(solution)/shard_map/all_gather | solution.py:377
  38.8 4.9 %collective-permute-start.4 = (f32[12,32,128]{2,1,0:T(8,128)S(1)}, f32[12,32,128]{2,1,0:T(8,128)S(1)}, u32[]{:S(2)}, u32[]{:S(2)}) collective-permute-start(f32[12,32,128]{2,1,0:T(8,128)S(1)} %get-tuple-element.28), channel_id=1, source_target_pairs={{1,2},{3,4},{5,6},{7,8},{9,10},{11,12},{13,14},{15,16},{17,18},{19... | collective-permute-start | bytes 589832 | tf_op jit(solution)/shard_map/ppermute | solution.py:341
  43.8 1.9 %collective-permute-start.5 = (f32[12,32,128]{2,1,0:T(8,128)S(1)}, f32[12,32,128]{2,1,0:T(8,128)S(1)}, u32[]{:S(2)}, u32[]{:S(2)}) collective-permute-start(f32[12,32,128]{2,1,0:T(8,128)S(1)} %get-tuple-element.29), channel_id=1, source_target_pairs={{0,1},{1,0},{2,3},{3,2},{4,5},{5,4},{6,7},{7,6},{8,9},{9,8},{10,11... | collective-permute-start | bytes 589832 | tf_op jit(solution)/shard_map/ppermute | solution.py:344
  46.0 1.1 %collective-permute-done.4.outer = f32[12,32,128]{2,1,0:T(8,128)S(1)} collective-permute-done((f32[12,32,128]{2,1,0:T(8,128)S(1)}, f32[12,32,128]{2,1,0:T(8,128)S(1)}, u32[]{:S(2)}, u32[]{:S(2)}) %collective-permute-start.4) | collective-permute-done | bytes 196640 | tf_op jit(solution)/shard_map/ppermute | solution.py:341
  47.1 0.9 %shard_map.60 = (f32[8,32,128]{2,1,0:T(8,128)S(1)}, f32[8,32,128]{2,1,0:T(8,128)S(1)}, f32[14,32,128]{2,1,0:T(8,128)S(1)}) custom-call(f32[4,8,32,128]{3,2,1,0:T(8,128)S(1)} %bitcast.5, f32[12,32,128]{2,1,0:T(8,128)S(1)} %collective-permute-done.4.outer, f32[12,32,128]{2,1,0:T(8,128)S(1)} %collective-permute-done.5.inner, f32[7,22,32,128]{3,2,1,0:T(8,128)S(1)} %shard_map.59.coef), custom_call_target="tpu_custom_call" | custom-call | tf_op jit(solution)/shard_map/pallas_call | solution.py:380
  48.0 0.7 collective-permute-start.6
  48.7 0.7 collective-permute-start.7
  49.4 3.7 %collective-permute-start.10 = (f32[14,32,128]{2,1,0:T(8,128)S(1)}, f32[14,32,128]{2,1,0:T(8,128)S(1)}, u32[]{:S(2)}, u32[]{:S(2)}) collective-permute-start(f32[14,32,128]{2,1,0:T(8,128)S(1)} %shard_map.62), channel_id=1, source_target_pairs={{0,32},{1,33},{2,34},{3,35},{4,36},{5,37},{6,38},{7,39},{8,40},{9,... | collective-permute-start | bytes 688136 | tf_op jit(solution)/shard_map/ppermute | solution.py:350
  53.1 2.1 %all-gather.1 = f32[16,32,128]{2,1,0:T(8,128)S(1)} all-gather(f32[8,32,128]{2,1,0:T(8,128)S(1)} %collective-permute-done.6.block.b1), channel_id=3, replica_groups={{0,1},{2,3},{4,5},{6,7},{8,9},{10,11},{12,13},{14,15},{16,17},{18,19},{..., dimensions={0}, use_global_device_ids=true | all-gather | bytes 393216 | tf_op jit(solution)/shard_map/all_gather | solution.py:354
  55.2 1.3 %collective-permute-start.8 = (f32[8,32,128]{2,1,0:T(8,128)S(1)}, f32[8,32,128]{2,1,0:T(8,128)S(1)}, u32[]{:S(2)}, u32[]{:S(2)}) collective-permute-start(f32[8,32,128]{2,1,0:T(8,128)S(1)} %get-tuple-element.32), channel_id=1, source_target_pairs={{128,256},{129,257},{130,258},{131,259},{132,260},{133,261},{134,2... | collective-permute-start | bytes 393224 | tf_op jit(solution)/shard_map/ppermute | solution.py:350
  56.5 0.7 collective-permute-start.9
  57.2 13.8 %collective-permute-done.8.block.b2 = f32[8,32,128]{2,1,0:T(8,128)S(1)} collective-permute-done((f32[8,32,128]{2,1,0:T(8,128)S(1)}, f32[8,32,128]{2,1,0:T(8,128)S(1)}, u32[]{:S(2)}, u32[]{:S(2)}) %collective-permute-start.8) | collective-permute-done | bytes 131104 | tf_op jit(solution)/shard_map/ppermute | solution.py:350
  71.0 2.1 %all-gather.2 = f32[16,32,128]{2,1,0:T(8,128)S(1)} all-gather(f32[8,32,128]{2,1,0:T(8,128)S(1)} %collective-permute-done.8.block.b2), channel_id=4, replica_groups={{0,1},{2,3},{4,5},{6,7},{8,9},{10,11},{12,13},{14,15},{16,17},{18,19},{..., dimensions={0}, use_global_device_ids=true | all-gather | bytes 393216 | tf_op jit(solution)/shard_map/all_gather | solution.py:354
  73.1 1.3 %collective-permute-start.11 = (f32[8,32,128]{2,1,0:T(8,128)S(1)}, f32[8,32,128]{2,1,0:T(8,128)S(1)}, u32[]{:S(2)}, u32[]{:S(2)}) collective-permute-start(f32[8,32,128]{2,1,0:T(8,128)S(1)} %get-tuple-element.35), channel_id=1, source_target_pairs={{256,384},{257,385},{258,386},{259,387},{260,388},{261,389},{262,3... | collective-permute-start | bytes 393224 | tf_op jit(solution)/shard_map/ppermute | solution.py:350
  74.4 1.3 %collective-permute-start.12 = (f32[8,32,128]{2,1,0:T(8,128)S(1)}, f32[8,32,128]{2,1,0:T(8,128)S(1)}, u32[]{:S(2)}, u32[]{:S(2)}) collective-permute-start(f32[8,32,128]{2,1,0:T(8,128)S(1)} %get-tuple-element.35), channel_id=1, source_target_pairs={{257,386},{259,388},{261,390},{263,392},{265,394},{267,396},{269,3... | collective-permute-start | bytes 393224 | tf_op jit(solution)/shard_map/ppermute | solution.py:350
  75.7 7.5 %collective-permute-done.11.b3 = f32[8,32,128]{2,1,0:T(8,128)S(1)} collective-permute-done((f32[8,32,128]{2,1,0:T(8,128)S(1)}, f32[8,32,128]{2,1,0:T(8,128)S(1)}, u32[]{:S(2)}, u32[]{:S(2)}) %collective-permute-start.11) | collective-permute-done | bytes 131104 | tf_op jit(solution)/shard_map/ppermute | solution.py:350
  83.2 2.5 %all-gather.3 = f32[16,32,128]{2,1,0:T(8,128)S(1)} all-gather(f32[8,32,128]{2,1,0:T(8,128)S(1)} %collective-permute-done.11.b3), channel_id=5, replica_groups={{0,1},{2,3},{4,5},{6,7},{8,9},{10,11},{12,13},{14,15},{16,17},{18,19},{..., dimensions={0}, use_global_device_ids=true | all-gather | bytes 393216 | tf_op jit(solution)/shard_map/all_gather | solution.py:354
  85.7 1.5 %shard_map.64 = f32[4,8,32,128]{3,2,1,0:T(8,128)} custom-call(f32[8,32,128]{2,1,0:T(8,128)S(1)} %collective-permute-done.6.block.b1, f32[8,32,128]{2,1,0:T(8,128)S(1)} %collective-permute-done.7.outer.o1, f32[2,8,32,128]{3,2,1,0:T(8,128)S(1)} %bitcast.10, f32[8,32,128]{2,1,0:T(8,128)S(1)} %collective-permute-done.8.block.b2, ...), custom_call_target="tpu_custom_call" | custom-call | tf_op jit(solution)/shard_map/pallas_call | solution.py:392
  (18 shorter events, 1.8 us)
Async XLA Ops:
  2.6 13.1 %collective-permute-start = (f32[38,32,128]{2,1,0:T(8,128)}, f32[38,32,128]{2,1,0:T(8,128)S(1)}, u32[]{:S(2)}, u32[]{:S(2)}) collective-permute-start(f32[38,32,128]{2,1,0:T(8,128)} %get-tuple-element.23), channel_id=1, source_target_pairs={{1,2},{3,4},{5,6},{7,8},{9,10},{11,12},{13,14},{15,16},{17,18},{19... | collective-permute-start | bytes 1867784 | tf_op jit(solution)/shard_map/ppermute | solution.py:341
  7.5 8.1 %collective-permute-start.1 = (f32[38,32,128]{2,1,0:T(8,128)}, f32[38,32,128]{2,1,0:T(8,128)S(1)}, u32[]{:S(2)}, u32[]{:S(2)}) collective-permute-start(f32[38,32,128]{2,1,0:T(8,128)} %get-tuple-element.24), channel_id=1, source_target_pairs={{0,1},{1,0},{2,3},{3,2},{4,5},{5,4},{6,7},{7,6},{8,9},{9,8},{10,11... | collective-permute-start | bytes 1867784 | tf_op jit(solution)/shard_map/ppermute | solution.py:344
  9.5 2.6 %collective-permute-start.2 = (f32[7,32,128]{2,1,0:T(8,128)}, f32[7,32,128]{2,1,0:T(8,128)S(1)}, u32[]{:S(2)}, u32[]{:S(2)}) collective-permute-start(f32[7,32,128]{2,1,0:T(8,128)} %get-tuple-element.25), channel_id=1, source_target_pairs={{1,2},{3,4},{5,6},{7,8},{9,10},{11,12},{13,14},{15,16},{17,18},{19... | collective-permute-start | bytes 344072 | tf_op jit(solution)/shard_map/ppermute | solution.py:350
  10.1 1.9 %collective-permute-start.3 = (f32[7,32,128]{2,1,0:T(8,128)}, f32[7,32,128]{2,1,0:T(8,128)S(1)}, u32[]{:S(2)}, u32[]{:S(2)}) collective-permute-start(f32[7,32,128]{2,1,0:T(8,128)} %get-tuple-element.26), channel_id=1, source_target_pairs={{0,1},{1,0},{2,3},{3,2},{4,5},{5,4},{6,7},{7,6},{8,9},{9,8},{10,11... | collective-permute-start | bytes 344072 | tf_op jit(solution)/shard_map/ppermute | solution.py:350
  10.8 1.2 %copy-start = (f32[56,32,128]{2,1,0:T(8,128)S(1)}, f32[56,32,128]{2,1,0:T(8,128)}, u32[]{:S(2)}) copy-start(f32[56,32,128]{2,1,0:T(8,128)} %get-tuple-element.22.held) | copy-start | bytes 2752516
  38.8 8.3 %collective-permute-start.4 = (f32[12,32,128]{2,1,0:T(8,128)S(1)}, f32[12,32,128]{2,1,0:T(8,128)S(1)}, u32[]{:S(2)}, u32[]{:S(2)}) collective-permute-start(f32[12,32,128]{2,1,0:T(8,128)S(1)} %get-tuple-element.28), channel_id=1, source_target_pairs={{1,2},{3,4},{5,6},{7,8},{9,10},{11,12},{13,14},{15,16},{17,18},{19... | collective-permute-start | bytes 589832 | tf_op jit(solution)/shard_map/ppermute | solution.py:341
  43.8 3.3 %collective-permute-start.5 = (f32[12,32,128]{2,1,0:T(8,128)S(1)}, f32[12,32,128]{2,1,0:T(8,128)S(1)}, u32[]{:S(2)}, u32[]{:S(2)}) collective-permute-start(f32[12,32,128]{2,1,0:T(8,128)S(1)} %get-tuple-element.29), channel_id=1, source_target_pairs={{0,1},{1,0},{2,3},{3,2},{4,5},{5,4},{6,7},{7,6},{8,9},{9,8},{10,11... | collective-permute-start | bytes 589832 | tf_op jit(solution)/shard_map/ppermute | solution.py:344
  48.0 5.1 %collective-permute-start.6 = (f32[8,32,128]{2,1,0:T(8,128)S(1)}, f32[8,32,128]{2,1,0:T(8,128)S(1)}, u32[]{:S(2)}, u32[]{:S(2)}) collective-permute-start(f32[8,32,128]{2,1,0:T(8,128)S(1)} %get-tuple-element.30.total), channel_id=1, source_target_pairs={{0,128},{1,129},{2,130},{3,131},{4,132},{5,133},{6,134},{7,135},{8... | collective-permute-start | bytes 393224 | tf_op jit(solution)/shard_map/ppermute | solution.py:350
  48.7 6.5 %collective-permute-start.7 = (f32[8,32,128]{2,1,0:T(8,128)S(1)}, f32[8,32,128]{2,1,0:T(8,128)S(1)}, u32[]{:S(2)}, u32[]{:S(2)}) collective-permute-start(f32[8,32,128]{2,1,0:T(8,128)S(1)} %get-tuple-element.30.total), channel_id=1, source_target_pairs={{1,130},{3,132},{5,134},{7,136},{9,138},{11,140},{13,142},{15,144}... | collective-permute-start | bytes 393224 | tf_op jit(solution)/shard_map/ppermute | solution.py:350
  49.4 23.7 %collective-permute-start.10 = (f32[14,32,128]{2,1,0:T(8,128)S(1)}, f32[14,32,128]{2,1,0:T(8,128)S(1)}, u32[]{:S(2)}, u32[]{:S(2)}) collective-permute-start(f32[14,32,128]{2,1,0:T(8,128)S(1)} %shard_map.62), channel_id=1, source_target_pairs={{0,32},{1,33},{2,34},{3,35},{4,36},{5,37},{6,38},{7,39},{8,40},{9,... | collective-permute-start | bytes 688136 | tf_op jit(solution)/shard_map/ppermute | solution.py:350
  55.2 15.8 %collective-permute-start.8 = (f32[8,32,128]{2,1,0:T(8,128)S(1)}, f32[8,32,128]{2,1,0:T(8,128)S(1)}, u32[]{:S(2)}, u32[]{:S(2)}) collective-permute-start(f32[8,32,128]{2,1,0:T(8,128)S(1)} %get-tuple-element.32), channel_id=1, source_target_pairs={{128,256},{129,257},{130,258},{131,259},{132,260},{133,261},{134,2... | collective-permute-start | bytes 393224 | tf_op jit(solution)/shard_map/ppermute | solution.py:350
  56.5 16.6 %collective-permute-start.9 = (f32[8,32,128]{2,1,0:T(8,128)S(1)}, f32[8,32,128]{2,1,0:T(8,128)S(1)}, u32[]{:S(2)}, u32[]{:S(2)}) collective-permute-start(f32[8,32,128]{2,1,0:T(8,128)S(1)} %get-tuple-element.32), channel_id=1, source_target_pairs={{129,258},{131,260},{133,262},{135,264},{137,266},{139,268},{141,2... | collective-permute-start | bytes 393224 | tf_op jit(solution)/shard_map/ppermute | solution.py:350
  73.1 10.1 %collective-permute-start.11 = (f32[8,32,128]{2,1,0:T(8,128)S(1)}, f32[8,32,128]{2,1,0:T(8,128)S(1)}, u32[]{:S(2)}, u32[]{:S(2)}) collective-permute-start(f32[8,32,128]{2,1,0:T(8,128)S(1)} %get-tuple-element.35), channel_id=1, source_target_pairs={{256,384},{257,385},{258,386},{259,387},{260,388},{261,389},{262,3... | collective-permute-start | bytes 393224 | tf_op jit(solution)/shard_map/ppermute | solution.py:350
  74.4 11.3 %collective-permute-start.12 = (f32[8,32,128]{2,1,0:T(8,128)S(1)}, f32[8,32,128]{2,1,0:T(8,128)S(1)}, u32[]{:S(2)}, u32[]{:S(2)}) collective-permute-start(f32[8,32,128]{2,1,0:T(8,128)S(1)} %get-tuple-element.35), channel_id=1, source_target_pairs={{257,386},{259,388},{261,390},{263,392},{265,394},{267,396},{269,3... | collective-permute-start | bytes 393224 | tf_op jit(solution)/shard_map/ppermute | solution.py:350

commit v6 on v5

--- a/solution.py
+++ b/solution.py
@@ -131,13 +131,25 @@
         if not 0 <= z < L:
             vz = -vz
         write_coefs(coef, z + FINE_HALO, get(2, z), vz, get(4, z), get(5, z), STEP)
+    opens = lax.axis_index("tm") == 0
     for z in range(-7, L + 7):
         y[z + 7] = get(6, z)
     for z in range(-4, L + 4):
         c[z + 4] = get(0, z)
     for step in range(4):
         halo = 6 - step
-        sweep(y, 7, coef, FINE_HALO, -halo, L + halo, lambda z, cur, new: new + get(1, z))
+        if step == 0:
+
+            @pl.when(opens)
+            def _():
+                sweep(y, 7, coef, FINE_HALO, -6, L + 6, lambda z, cur, new: new + get(1, z))
+
+            @pl.when(jnp.logical_not(opens))
+            def _():
+                for z in range(-6, L + 6):
+                    y[z + 7] = get(1, z)
+        else:
+            sweep(y, 7, coef, FINE_HALO, -halo, L + halo, lambda z, cur, new: new + get(1, z))
         halo = 3 - step
         sweep(c, 4, coef, FINE_HALO, -halo, L + halo)
     for z in range(-2, L + 2):

time: 87.7 us -> 87.5 us (level)
  no operation moved by 1% of the time
where the time goes in v6:
time: 87.5 us; the launch traced here: 87.1 us
  blocking collectives  28.2 us (32%)
  waiting for transfers between devices  26 us (30%)
  starting transfers between devices  24.7 us (28%)
  Pallas kernels  6.87 us (8%)
  local copies, waits for them, and re-layouts  1.17 us (1%)
    all_gather x1, blocking collectives, body(): lax.all_gather(d, 'tm', axis_index_groups=[[4 * a + b for b in range(4)]...  21.6 us
    ppermute x9, waiting for transfers between devices, move(): return lax.ppermute(x, ('tm', 'space'), pairs)  21.3 us
    ppermute x9, starting transfers between devices, move(): return lax.ppermute(x, ('tm', 'space'), pairs)  10.9 us
    ppermute x2, starting transfers between devices, from_outer(): return lax.ppermute(x, 'space', facing)  9.9 us
    all_gather x3, blocking collectives, hop(): lax.all_gather(block, 'space', axis_index_groups=[[i, i + 1] for i in ran...  6.63 us
    ppermute x2, waiting for transfers between devices, from_outer(): return lax.ppermute(x, 'space', facing)  4.65 us
    ppermute x2, starting transfers between devices, from_inner(): return lax.ppermute(x, 'space', paired)  3.84 us
    pallas_call x1, Pallas kernels, body(): pl.pallas_call(pack_kernel, out_shape=[jax.ShapeDtypeStruct((n, NY, NX),...  2.54 us
  transfers between devices with their start and end apart: 13, of which 4 were waited for; matrix products, arithmetic and copies ran while one was open for 0% of the time, Pallas kernels for 0%

profile of v6, /device:TPU:95, one launch (start us, length us, event | category | flops | bytes accessed | tf_op | source)
XLA Modules:
  0.0 87.1 jit_solution(2683240565059147794)
XLA Ops:
  0.0 2.5 %shard_map.55 = (f32[56,32,128]{2,1,0:T(8,128)}, f32[38,32,128]{2,1,0:T(8,128)}, f32[38,32,128]{2,1,0:T(8,128)}, f32[7,32,128]{2,1,0:T(8,128)}, f32[7,32,128]{2,1,0:T(8,128)}) custom-call(f32[1,8,32,128]{3,2,1,0:T(8,128)} %guesses.1, f32[1,8,32,128]{3,2,1,0:T(8,128)} %forcing.1, f32[8,32,128]{2,1,0:T(8,128)} %kappa.1, f32[3,8,32,128]{3,2,1,0:T(8,128)} %velocity.1, ...), custom_call_target="tpu_custom_call" | custom-call | tf_op jit(solution)/shard_map/pallas_call | solution.py:370
  2.6 5.0 %collective-permute-start = (f32[38,32,128]{2,1,0:T(8,128)}, f32[38,32,128]{2,1,0:T(8,128)S(1)}, u32[]{:S(2)}, u32[]{:S(2)}) collective-permute-start(f32[38,32,128]{2,1,0:T(8,128)} %get-tuple-element.23), channel_id=1, source_target_pairs={{1,2},{3,4},{5,6},{7,8},{9,10},{11,12},{13,14},{15,16},{17,18},{19... | collective-permute-start | bytes 1867784 | tf_op jit(solution)/shard_map/ppermute | solution.py:353
  7.5 1.9 %collective-permute-start.1 = (f32[38,32,128]{2,1,0:T(8,128)}, f32[38,32,128]{2,1,0:T(8,128)S(1)}, u32[]{:S(2)}, u32[]{:S(2)}) collective-permute-start(f32[38,32,128]{2,1,0:T(8,128)} %get-tuple-element.24), channel_id=1, source_target_pairs={{0,1},{1,0},{2,3},{3,2},{4,5},{5,4},{6,7},{7,6},{8,9},{9,8},{10,11... | collective-permute-start | bytes 1867784 | tf_op jit(solution)/shard_map/ppermute | solution.py:356
  10.8 1.2 %copy-done = f32[56,32,128]{2,1,0:T(8,128)S(1)} copy-done((f32[56,32,128]{2,1,0:T(8,128)S(1)}, f32[56,32,128]{2,1,0:T(8,128)}, u32[]{:S(2)}) %copy-start) | copy-done | bytes 917528
  12.1 3.6 %collective-permute-done.outer = f32[38,32,128]{2,1,0:T(8,128)S(1)} collective-permute-done((f32[38,32,128]{2,1,0:T(8,128)}, f32[38,32,128]{2,1,0:T(8,128)S(1)}, u32[]{:S(2)}, u32[]{:S(2)}) %collective-permute-start) | collective-permute-done | bytes 622624 | tf_op jit(solution)/shard_map/ppermute | solution.py:353
  15.7 1.4 %shard_map.57 = (f32[8,32,128]{2,1,0:T(8,128)S(1)}, f32[14,32,128]{2,1,0:T(8,128)S(1)}, f32[7,20,32,128]{3,2,1,0:T(8,128)S(1)}) custom-call(f32[56,32,128]{2,1,0:T(8,128)S(1)} %shard_map.56.own, f32[38,32,128]{2,1,0:T(8,128)S(1)} %collective-permute-done.outer, f32[38,32,128]{2,1,0:T(8,128)S(1)} %collective-permute-done.1.inner, ...), custom_call_target="tpu_custom_call" | custom-call | tf_op jit(solution)/shard_map/pallas_call | solution.py:385
  17.1 21.6 %all-gather = f32[32,32,128]{2,1,0:T(8,128)S(1)} all-gather(f32[8,32,128]{2,1,0:T(8,128)S(1)} %get-tuple-element.27.d), channel_id=2, replica_groups={{0,32,64,96},{128,160,192,224},{256,288,320,352},{384,416,448,480},{1,3..., dimensions={0}, use_global_device_ids=true | all-gather | bytes 655360 | tf_op jit(solution)/shard_map/all_gather | solution.py:389
  38.7 4.9 %collective-permute-start.4 = (f32[12,32,128]{2,1,0:T(8,128)S(1)}, f32[12,32,128]{2,1,0:T(8,128)S(1)}, u32[]{:S(2)}, u32[]{:S(2)}) collective-permute-start(f32[12,32,128]{2,1,0:T(8,128)S(1)} %get-tuple-element.28), channel_id=1, source_target_pairs={{1,2},{3,4},{5,6},{7,8},{9,10},{11,12},{13,14},{15,16},{17,18},{19... | collective-permute-start | bytes 589832 | tf_op jit(solution)/shard_map/ppermute | solution.py:353
  43.6 1.9 %collective-permute-start.5 = (f32[12,32,128]{2,1,0:T(8,128)S(1)}, f32[12,32,128]{2,1,0:T(8,128)S(1)}, u32[]{:S(2)}, u32[]{:S(2)}) collective-permute-start(f32[12,32,128]{2,1,0:T(8,128)S(1)} %get-tuple-element.29), channel_id=1, source_target_pairs={{0,1},{1,0},{2,3},{3,2},{4,5},{5,4},{6,7},{7,6},{8,9},{9,8},{10,11... | collective-permute-start | bytes 589832 | tf_op jit(solution)/shard_map/ppermute | solution.py:356
  45.9 1.1 %collective-permute-done.4.outer = f32[12,32,128]{2,1,0:T(8,128)S(1)} collective-permute-done((f32[12,32,128]{2,1,0:T(8,128)S(1)}, f32[12,32,128]{2,1,0:T(8,128)S(1)}, u32[]{:S(2)}, u32[]{:S(2)}) %collective-permute-start.4) | collective-permute-done | bytes 196640 | tf_op jit(solution)/shard_map/ppermute | solution.py:353
  47.0 0.9 %shard_map.60 = (f32[8,32,128]{2,1,0:T(8,128)S(1)}, f32[8,32,128]{2,1,0:T(8,128)S(1)}, f32[14,32,128]{2,1,0:T(8,128)S(1)}) custom-call(f32[4,8,32,128]{3,2,1,0:T(8,128)S(1)} %bitcast.5, f32[12,32,128]{2,1,0:T(8,128)S(1)} %collective-permute-done.4.outer, f32[12,32,128]{2,1,0:T(8,128)S(1)} %collective-permute-done.5.inner, f32[7,22,32,128]{3,2,1,0:T(8,128)S(1)} %shard_map.59.coef), custom_call_target="tpu_custom_call" | custom-call | tf_op jit(solution)/shard_map/pallas_call | solution.py:392
  47.9 0.7 collective-permute-start.6
  48.5 0.7 collective-permute-start.7
  49.2 3.7 %collective-permute-start.10 = (f32[14,32,128]{2,1,0:T(8,128)S(1)}, f32[14,32,128]{2,1,0:T(8,128)S(1)}, u32[]{:S(2)}, u32[]{:S(2)}) collective-permute-start(f32[14,32,128]{2,1,0:T(8,128)S(1)} %shard_map.62), channel_id=1, source_target_pairs={{0,32},{1,33},{2,34},{3,35},{4,36},{5,37},{6,38},{7,39},{8,40},{9,... | collective-permute-start | bytes 688136 | tf_op jit(solution)/shard_map/ppermute | solution.py:362
  53.0 2.1 %all-gather.1 = f32[16,32,128]{2,1,0:T(8,128)S(1)} all-gather(f32[8,32,128]{2,1,0:T(8,128)S(1)} %collective-permute-done.6.block.b1), channel_id=3, replica_groups={{0,1},{2,3},{4,5},{6,7},{8,9},{10,11},{12,13},{14,15},{16,17},{18,19},{..., dimensions={0}, use_global_device_ids=true | all-gather | bytes 393216 | tf_op jit(solution)/shard_map/all_gather | solution.py:366
  55.1 1.3 %collective-permute-start.8 = (f32[8,32,128]{2,1,0:T(8,128)S(1)}, f32[8,32,128]{2,1,0:T(8,128)S(1)}, u32[]{:S(2)}, u32[]{:S(2)}) collective-permute-start(f32[8,32,128]{2,1,0:T(8,128)S(1)} %get-tuple-element.32), channel_id=1, source_target_pairs={{128,256},{129,257},{130,258},{131,259},{132,260},{133,261},{134,2... | collective-permute-start | bytes 393224 | tf_op jit(solution)/shard_map/ppermute | solution.py:362
  56.4 0.7 collective-permute-start.9
  57.0 13.8 %collective-permute-done.8.block.b2 = f32[8,32,128]{2,1,0:T(8,128)S(1)} collective-permute-done((f32[8,32,128]{2,1,0:T(8,128)S(1)}, f32[8,32,128]{2,1,0:T(8,128)S(1)}, u32[]{:S(2)}, u32[]{:S(2)}) %collective-permute-start.8) | collective-permute-done | bytes 131104 | tf_op jit(solution)/shard_map/ppermute | solution.py:362
  70.9 2.1 %all-gather.2 = f32[16,32,128]{2,1,0:T(8,128)S(1)} all-gather(f32[8,32,128]{2,1,0:T(8,128)S(1)} %collective-permute-done.8.block.b2), channel_id=4, replica_groups={{0,1},{2,3},{4,5},{6,7},{8,9},{10,11},{12,13},{14,15},{16,17},{18,19},{..., dimensions={0}, use_global_device_ids=true | all-gather | bytes 393216 | tf_op jit(solution)/shard_map/all_gather | solution.py:366
  73.0 1.3 %collective-permute-start.11 = (f32[8,32,128]{2,1,0:T(8,128)S(1)}, f32[8,32,128]{2,1,0:T(8,128)S(1)}, u32[]{:S(2)}, u32[]{:S(2)}) collective-permute-start(f32[8,32,128]{2,1,0:T(8,128)S(1)} %get-tuple-element.35), channel_id=1, source_target_pairs={{256,384},{257,385},{258,386},{259,387},{260,388},{261,389},{262,3... | collective-permute-start | bytes 393224 | tf_op jit(solution)/shard_map/ppermute | solution.py:362
  74.3 1.3 %collective-permute-start.12 = (f32[8,32,128]{2,1,0:T(8,128)S(1)}, f32[8,32,128]{2,1,0:T(8,128)S(1)}, u32[]{:S(2)}, u32[]{:S(2)}) collective-permute-start(f32[8,32,128]{2,1,0:T(8,128)S(1)} %get-tuple-element.35), channel_id=1, source_target_pairs={{257,386},{259,388},{261,390},{263,392},{265,394},{267,396},{269,3... | collective-permute-start | bytes 393224 | tf_op jit(solution)/shard_map/ppermute | solution.py:362
  75.6 7.5 %collective-permute-done.11.b3 = f32[8,32,128]{2,1,0:T(8,128)S(1)} collective-permute-done((f32[8,32,128]{2,1,0:T(8,128)S(1)}, f32[8,32,128]{2,1,0:T(8,128)S(1)}, u32[]{:S(2)}, u32[]{:S(2)}) %collective-permute-start.11) | collective-permute-done | bytes 131104 | tf_op jit(solution)/shard_map/ppermute | solution.py:362
  83.1 2.5 %all-gather.3 = f32[16,32,128]{2,1,0:T(8,128)S(1)} all-gather(f32[8,32,128]{2,1,0:T(8,128)S(1)} %collective-permute-done.11.b3), channel_id=5, replica_groups={{0,1},{2,3},{4,5},{6,7},{8,9},{10,11},{12,13},{14,15},{16,17},{18,19},{..., dimensions={0}, use_global_device_ids=true | all-gather | bytes 393216 | tf_op jit(solution)/shard_map/all_gather | solution.py:366
  85.6 1.5 %shard_map.64 = f32[4,8,32,128]{3,2,1,0:T(8,128)} custom-call(f32[8,32,128]{2,1,0:T(8,128)S(1)} %collective-permute-done.6.block.b1, f32[8,32,128]{2,1,0:T(8,128)S(1)} %collective-permute-done.7.outer.o1, f32[2,8,32,128]{3,2,1,0:T(8,128)S(1)} %bitcast.10, f32[8,32,128]{2,1,0:T(8,128)S(1)} %collective-permute-done.8.block.b2, ...), custom_call_target="tpu_custom_call" | custom-call | tf_op jit(solution)/shard_map/pallas_call | solution.py:404
  (18 shorter events, 1.8 us)
Async XLA Ops:
  2.6 13.1 %collective-permute-start = (f32[38,32,128]{2,1,0:T(8,128)}, f32[38,32,128]{2,1,0:T(8,128)S(1)}, u32[]{:S(2)}, u32[]{:S(2)}) collective-permute-start(f32[38,32,128]{2,1,0:T(8,128)} %get-tuple-element.23), channel_id=1, source_target_pairs={{1,2},{3,4},{5,6},{7,8},{9,10},{11,12},{13,14},{15,16},{17,18},{19... | collective-permute-start | bytes 1867784 | tf_op jit(solution)/shard_map/ppermute | solution.py:353
  7.5 8.1 %collective-permute-start.1 = (f32[38,32,128]{2,1,0:T(8,128)}, f32[38,32,128]{2,1,0:T(8,128)S(1)}, u32[]{:S(2)}, u32[]{:S(2)}) collective-permute-start(f32[38,32,128]{2,1,0:T(8,128)} %get-tuple-element.24), channel_id=1, source_target_pairs={{0,1},{1,0},{2,3},{3,2},{4,5},{5,4},{6,7},{7,6},{8,9},{9,8},{10,11... | collective-permute-start | bytes 1867784 | tf_op jit(solution)/shard_map/ppermute | solution.py:356
  9.5 2.6 %collective-permute-start.2 = (f32[7,32,128]{2,1,0:T(8,128)}, f32[7,32,128]{2,1,0:T(8,128)S(1)}, u32[]{:S(2)}, u32[]{:S(2)}) collective-permute-start(f32[7,32,128]{2,1,0:T(8,128)} %get-tuple-element.25), channel_id=1, source_target_pairs={{1,2},{3,4},{5,6},{7,8},{9,10},{11,12},{13,14},{15,16},{17,18},{19... | collective-permute-start | bytes 344072 | tf_op jit(solution)/shard_map/ppermute | solution.py:362
  10.1 1.9 %collective-permute-start.3 = (f32[7,32,128]{2,1,0:T(8,128)}, f32[7,32,128]{2,1,0:T(8,128)S(1)}, u32[]{:S(2)}, u32[]{:S(2)}) collective-permute-start(f32[7,32,128]{2,1,0:T(8,128)} %get-tuple-element.26), channel_id=1, source_target_pairs={{0,1},{1,0},{2,3},{3,2},{4,5},{5,4},{6,7},{7,6},{8,9},{9,8},{10,11... | collective-permute-start | bytes 344072 | tf_op jit(solution)/shard_map/ppermute | solution.py:362
  10.8 1.2 %copy-start = (f32[56,32,128]{2,1,0:T(8,128)S(1)}, f32[56,32,128]{2,1,0:T(8,128)}, u32[]{:S(2)}) copy-start(f32[56,32,128]{2,1,0:T(8,128)} %get-tuple-element.22.held) | copy-start | bytes 2752516
  38.7 8.3 %collective-permute-start.4 = (f32[12,32,128]{2,1,0:T(8,128)S(1)}, f32[12,32,128]{2,1,0:T(8,128)S(1)}, u32[]{:S(2)}, u32[]{:S(2)}) collective-permute-start(f32[12,32,128]{2,1,0:T(8,128)S(1)} %get-tuple-element.28), channel_id=1, source_target_pairs={{1,2},{3,4},{5,6},{7,8},{9,10},{11,12},{13,14},{15,16},{17,18},{19... | collective-permute-start | bytes 589832 | tf_op jit(solution)/shard_map/ppermute | solution.py:353
  43.6 3.3 %collective-permute-start.5 = (f32[12,32,128]{2,1,0:T(8,128)S(1)}, f32[12,32,128]{2,1,0:T(8,128)S(1)}, u32[]{:S(2)}, u32[]{:S(2)}) collective-permute-start(f32[12,32,128]{2,1,0:T(8,128)S(1)} %get-tuple-element.29), channel_id=1, source_target_pairs={{0,1},{1,0},{2,3},{3,2},{4,5},{5,4},{6,7},{7,6},{8,9},{9,8},{10,11... | collective-permute-start | bytes 589832 | tf_op jit(solution)/shard_map/ppermute | solution.py:356
  47.9 5.1 %collective-permute-start.6 = (f32[8,32,128]{2,1,0:T(8,128)S(1)}, f32[8,32,128]{2,1,0:T(8,128)S(1)}, u32[]{:S(2)}, u32[]{:S(2)}) collective-permute-start(f32[8,32,128]{2,1,0:T(8,128)S(1)} %get-tuple-element.30.total), channel_id=1, source_target_pairs={{0,128},{1,129},{2,130},{3,131},{4,132},{5,133},{6,134},{7,135},{8... | collective-permute-start | bytes 393224 | tf_op jit(solution)/shard_map/ppermute | solution.py:362
  48.5 6.5 %collective-permute-start.7 = (f32[8,32,128]{2,1,0:T(8,128)S(1)}, f32[8,32,128]{2,1,0:T(8,128)S(1)}, u32[]{:S(2)}, u32[]{:S(2)}) collective-permute-start(f32[8,32,128]{2,1,0:T(8,128)S(1)} %get-tuple-element.30.total), channel_id=1, source_target_pairs={{1,130},{3,132},{5,134},{7,136},{9,138},{11,140},{13,142},{15,144}... | collective-permute-start | bytes 393224 | tf_op jit(solution)/shard_map/ppermute | solution.py:362
  49.2 23.7 %collective-permute-start.10 = (f32[14,32,128]{2,1,0:T(8,128)S(1)}, f32[14,32,128]{2,1,0:T(8,128)S(1)}, u32[]{:S(2)}, u32[]{:S(2)}) collective-permute-start(f32[14,32,128]{2,1,0:T(8,128)S(1)} %shard_map.62), channel_id=1, source_target_pairs={{0,32},{1,33},{2,34},{3,35},{4,36},{5,37},{6,38},{7,39},{8,40},{9,... | collective-permute-start | bytes 688136 | tf_op jit(solution)/shard_map/ppermute | solution.py:362
  55.1 15.8 %collective-permute-start.8 = (f32[8,32,128]{2,1,0:T(8,128)S(1)}, f32[8,32,128]{2,1,0:T(8,128)S(1)}, u32[]{:S(2)}, u32[]{:S(2)}) collective-permute-start(f32[8,32,128]{2,1,0:T(8,128)S(1)} %get-tuple-element.32), channel_id=1, source_target_pairs={{128,256},{129,257},{130,258},{131,259},{132,260},{133,261},{134,2... | collective-permute-start | bytes 393224 | tf_op jit(solution)/shard_map/ppermute | solution.py:362
  56.4 16.6 %collective-permute-start.9 = (f32[8,32,128]{2,1,0:T(8,128)S(1)}, f32[8,32,128]{2,1,0:T(8,128)S(1)}, u32[]{:S(2)}, u32[]{:S(2)}) collective-permute-start(f32[8,32,128]{2,1,0:T(8,128)S(1)} %get-tuple-element.32), channel_id=1, source_target_pairs={{129,258},{131,260},{133,262},{135,264},{137,266},{139,268},{141,2... | collective-permute-start | bytes 393224 | tf_op jit(solution)/shard_map/ppermute | solution.py:362
  73.0 10.1 %collective-permute-start.11 = (f32[8,32,128]{2,1,0:T(8,128)S(1)}, f32[8,32,128]{2,1,0:T(8,128)S(1)}, u32[]{:S(2)}, u32[]{:S(2)}) collective-permute-start(f32[8,32,128]{2,1,0:T(8,128)S(1)} %get-tuple-element.35), channel_id=1, source_target_pairs={{256,384},{257,385},{258,386},{259,387},{260,388},{261,389},{262,3... | collective-permute-start | bytes 393224 | tf_op jit(solution)/shard_map/ppermute | solution.py:362
  74.3 11.3 %collective-permute-start.12 = (f32[8,32,128]{2,1,0:T(8,128)S(1)}, f32[8,32,128]{2,1,0:T(8,128)S(1)}, u32[]{:S(2)}, u32[]{:S(2)}) collective-permute-start(f32[8,32,128]{2,1,0:T(8,128)S(1)} %get-tuple-element.35), channel_id=1, source_target_pairs={{257,386},{259,388},{261,390},{263,392},{265,394},{267,396},{269,3... | collective-permute-start | bytes 393224 | tf_op jit(solution)/shard_map/ppermute | solution.py:362
